TPU v7x, 128 devices: a whole 4x4x4 slice. The times are simulated.
128 devices in a mesh: cluster: 16 (over x, z), helper: 8 (over y, core).
Axes of the slice: x: 4, y: 4, z: 4, core: 2. Of those that a mesh axis runs over, the one named last changes fastest.
Arguments:
- embeddings: bfloat16 [65536, 1024], P(('cluster', 'helper')), may hold values from -40 to 40
- clusters: int32 [65536], P(('cluster', 'helper')), may hold values from 0 to 511, as said below
- order: int32 [65536], P(('cluster', 'helper')), may hold values from 0 to 65535, each once
Outputs:
- best_similarity: float32 [65536], P(('cluster', 'helper'))
Inputs may be any that keep to these rules, and one draw needn't show every extreme that they name: Cluster c belongs to owner c // 32. Among the 512 rows of one device, the clusters of one owner hold at most 80 rows; one owner, the same on every device, holds exactly 80 rows on every device, and on half of the devices all 80 of them lie in one cluster. `order`: each position occurs once.
All inputs are finite; a program needn't handle non-finite values.
Results may differ from a plain program's by a relative error of at most 0.0003.
Values may be sent and summed in bfloat16 or wider, within the bound.
No kernel may reach another device: no remote copies, remote signals or barrier semaphores. Data moves between devices by JAX's collectives and lax.ppermute only.
A program may use at most 128 MiB of HBM per device.

v0:
```python
import jax
import jax.numpy as jnp
from jax import lax
from jax.sharding import PartitionSpec as P

CL_OWN = 32


def inverse_norms(row_values):
    wide_rows = row_values.astype(jnp.float32)
    return lax.rsqrt(jnp.sum(wide_rows * wide_rows, axis=1) + 1e-06)


def best_block(best_sim, query_emb, query_inv, query_cl, query_ord, key_emb, key_cl, key_ord):
    key_inv = inverse_norms(key_emb)
    gram = lax.dot_general(
        query_emb, key_emb, (((1,), (1,)), ((), ())), preferred_element_type=jnp.float32
    )
    cosine = gram * query_inv[:, None] * key_inv[None, :]
    live = (key_cl[None, :] == query_cl[:, None]) & (key_ord[None, :] < query_ord[:, None])
    return jnp.maximum(best_sim, jnp.max(jnp.where(live, cosine, -1.0), axis=1))


def best_over(best_sim, queries, key_emb, key_cl, key_ord, block_rows):
    query_emb, query_inv, query_cl, query_ord = queries
    key_count = key_emb.shape[0]
    feature_width = key_emb.shape[1]
    blocks = key_count // block_rows

    def advance(running, key_block):
        return (
            best_block(
                running,
                query_emb,
                query_inv,
                query_cl,
                query_ord,
                key_block[0],
                key_block[1],
                key_block[2],
            ),
            None,
        )

    best_sim, unused = lax.scan(
        advance,
        best_sim,
        (
            key_emb.reshape(blocks, block_rows, feature_width),
            key_cl.reshape(blocks, block_rows),
            key_ord.reshape(blocks, block_rows),
        ),
    )
    return best_sim


def local(embeddings, clusters, order):
    row_count, feature_width = embeddings.shape
    owners = lax.axis_size("cluster")
    helpers = lax.axis_size("helper")
    slot_count = max(1, row_count * 5 // (2 * owners * helpers))
    total_rows = owners * helpers * slot_count
    owner_of = clusters // CL_OWN
    one_hot = (owner_of[:, None] == jnp.arange(owners, dtype=jnp.int32)[None, :]).astype(jnp.int32)
    before = jnp.cumsum(one_hot, axis=0) - one_hot
    place_in = jnp.sum(before * one_hot, axis=1)
    target = (owner_of * helpers + place_in % helpers) * slot_count + place_in // helpers
    empty_best = jnp.full((total_rows,), -1.0, jnp.float32)
    outbox = jnp.zeros((total_rows, feature_width), embeddings.dtype).at[target].set(embeddings)
    outbox_cl = jnp.full((total_rows,), -1, jnp.int32).at[target].set(clusters)
    outbox_ord = jnp.zeros((total_rows,), jnp.int32).at[target].set(order)
    inbox, inbox_cl, inbox_ord = (
        lax.all_to_all(outbox, ("cluster", "helper"), split_axis=0, concat_axis=0, tiled=True),
        lax.all_to_all(outbox_cl, ("cluster", "helper"), split_axis=0, concat_axis=0, tiled=True),
        lax.all_to_all(outbox_ord, ("cluster", "helper"), split_axis=0, concat_axis=0, tiled=True),
    )
    queries = (inbox, inverse_norms(inbox), inbox_cl, inbox_ord)
    best_sim = best_over(
        empty_best,
        queries,
        lax.all_gather(inbox, "helper", axis=0, tiled=True),
        lax.all_gather(inbox_cl, "helper", axis=0, tiled=True),
        lax.all_gather(inbox_ord, "helper", axis=0, tiled=True),
        total_rows,
    )
    returned = lax.all_to_all(
        best_sim, ("cluster", "helper"), split_axis=0, concat_axis=0, tiled=True
    )
    return returned[target]


def solution(mesh):
    placed = (P(("cluster", "helper"), None), P(("cluster", "helper")), P(("cluster", "helper")))
    return jax.shard_map(
        local, mesh=mesh, in_specs=placed, out_specs=P(("cluster", "helper")), check_vma=False
    )
```

profile of v0, /device:TPU:1, one launch (start us, length us, event | category | flops | bytes accessed | tf_op | source)
XLA Modules:
  0.0 286.2 jit_solution(3194778361977868295)
XLA Ops:
  6.5 0.0 all-gather.4.cloned.1.call-start
  6.5 0.7 fusion.27
  7.2 0.7 add_select_fusion.2
  7.9 1.2 reduce-window.6
  9.1 0.2 slice_reduce_fusion
  9.3 0.1 fusion.13
  9.4 0.7 compare_select_fusion
  10.1 4.1 %scatter_custom_fusion.2 = bf16[1280,1024]{1,0:T(8,128)(2,1)S(1)} fusion(s32[512]{0:T(512)S(1)} %compare_select_fusion, bf16[512,1024]{1,0:T(8,128)(2,1)} %param.5, bf16[]{:T(256)} %constant.66.clone.1), kind=kCustom, calls=%fused_computation.18 | custom fusion | bytes 2621952 | tf_op jit(solution)/shard_map/scatter | solution.py:69
  14.3 2.8 all_to_all.38
  17.0 64.5 %all_to_all.48 = bf16[128,10,1024]{2,1,0:T(8,128)(2,1)} all-to-all(bf16[128,10,1024]{2,1,0:T(8,128)(2,1)} %all_to_all.38), channel_id=1, replica_groups=mesh['cluster'=16,'helper'=8] {'cluster','helper'}, dimensions={0} | all-to-all | bytes 5242880 | tf_op jit(solution)/shard_map/all_to_all | solution.py:73
  81.5 6.1 %all_to_all.40 = bf16[1280,1024]{1,0:T(8,128)(2,1)} reshape(bf16[128,10,1024]{2,1,0:T(8,128)(2,1)} %all_to_all.48) | data formatting | bytes 5242880 | tf_op jit(solution)/shard_map/all_to_all | solution.py:73
  87.7 0.0 copy-start
  87.7 0.0 all-gather.4.cloned.1.call-update
  87.7 2.7 scatter_custom_fusion
  90.4 0.8 all_to_all.32
  91.2 5.6 %all-to-all-start = ((s32[128,10,1]{1,2,0:T(1,128)}), s32[128,10,1]{1,2,0:T(1,128)S(1)}, u32[]{:S(2)}, u32[]{:S(2)}) async-start(s32[128,10,1]{1,2,0:T(1,128)} %bitcast.2), calls=%async_computation | async-start | bytes 131072 | tf_op jit(solution)/shard_map/all_to_all | solution.py:74
  96.8 2.6 scatter_custom_fusion.1
  99.4 0.8 all_to_all.35
  100.2 6.1 %all-to-all-done = s32[128,10,1]{1,2,0:T(1,128)S(1)} async-done(((s32[128,10,1]{1,2,0:T(1,128)}), s32[128,10,1]{1,2,0:T(1,128)S(1)}, u32[]{:S(2)}, u32[]{:S(2)}) %all-to-all-start) | async-done | bytes 5152 | tf_op jit(solution)/shard_map/all_to_all | solution.py:74
  106.3 4.6 %all-to-all-start.1 = ((s32[128,10,1]{1,2,0:T(1,128)}), s32[128,10,1]{1,2,0:T(1,128)S(1)}, u32[]{:S(2)}, u32[]{:S(2)}) async-start(s32[128,10,1]{1,2,0:T(1,128)} %bitcast.3), calls=%async_computation.1 | async-start | bytes 131072 | tf_op jit(solution)/shard_map/all_to_all | solution.py:75
  110.9 0.1 all_to_all.34
  111.0 9.4 %all-to-all-done.1 = s32[128,10,1]{1,2,0:T(1,128)S(1)} async-done(((s32[128,10,1]{1,2,0:T(1,128)}), s32[128,10,1]{1,2,0:T(1,128)S(1)}, u32[]{:S(2)}, u32[]{:S(2)}) %all-to-all-start.1) | async-done | bytes 5152 | tf_op jit(solution)/shard_map/all_to_all | solution.py:75
  120.4 0.1 all_to_all.37
  120.5 0.5 broadcast.91
  121.1 0.8 reduce.21
  121.9 0.1 reshape.86
  122.0 0.8 reduce.20
  122.8 0.1 reshape.84
  123.0 13.5 %all-gather = s32[8,1,1280]{2,1,0:T(1,128)S(1)} all-gather(s32[1,1,1280]{2,1,0:T(1,128)S(1)} %reshape.84), channel_id=1, replica_groups=mesh['cluster'=16,'helper'=8] {'helper'}, dimensions={0}, use_global_device_ids=true | all-gather | bytes 46080 | tf_op jit(solution)/shard_map/all_gather | solution.py:82
  136.5 13.0 %all-gather.1 = s32[8,1,1280]{2,1,0:T(1,128)S(1)} all-gather(s32[1,1,1280]{2,1,0:T(1,128)S(1)} %reshape.86), channel_id=1, replica_groups=mesh['cluster'=16,'helper'=8] {'helper'}, dimensions={0}, use_global_device_ids=true | all-gather | bytes 46080 | tf_op jit(solution)/shard_map/all_gather | solution.py:83
  149.5 3.2 %multiply_reduce_fusion.1 = f32[128,10]{1,0:T(8,128)S(1)} fusion(bf16[128,10,1024]{2,1,0:T(8,128)(2,1)} %all_to_all.48), kind=kLoop, calls=%fused_computation.17 | loop fusion | flops 3930880 | bytes 2626560 | tf_op jit(solution)/shard_map/reduce_sum | solution.py:11
  152.7 0.1 rsqrt.14
  152.9 36.9 %all-gather.4.cloned.1.call-done = bf16[10240,1024]{1,0:T(8,128)(2,1)} async-done(((bf16[1280,1024]{1,0:T(8,128)(2,1)}), bf16[10240,1024]{1,0:T(8,128)(2,1)}) %all-gather.4.cloned.1.call-update) | async-done | bytes 20971536 | tf_op jit(solution)/shard_map/all_gather | solution.py:81
  189.7 0.0 copy-done
  189.7 65.5 %while.11 = (s32[]{:T(128)}, f32[1280]{0:T(1024)S(1)}, s32[8,1280]{1,0:T(8,128)S(1)}, s32[1280]{0:T(1024)S(1)}, s32[8,1280]{1,0:T(8,128)S(1)}, /*index=5*/s32[12...) while((s32[]{:T(128)}, f32[1280]{0:T(1024)S(1)}, ...), condition=%wide.region_10.11_spmd.clone, body=%wide.region_7.10_spmd.clone.sunk | while | flops 3370845440 | bytes 7951499 | solution.py:45
  189.7 2.3 multiply_reduce_fusion.3
  192.1 5.8 %fusion.33 = f32[1280]{0:T(1024)S(1)} fusion(f32[1280]{0:T(1024)S(1)} %add_rsqrt_fusion.3, f32[1280]{0:T(1024)S(1)} %get-tuple-element.192, bf16[1280,1024]{1,0:T(8,128)(2,1)S(1)} %get-tuple-element.191, bf16[8,1280,1024]{2,1,0:T(8,128)(2,1)} %get-tuple-element.190, s32[]{:T(128)S(6)} %copy.19, s32[1280]{0:T(1024)S(1)} %get-tuple-element.189, ...), kind=kOutput, calls=%fused_computation.11.clone.1 | convolution fusion | flops 3366910720 | bytes 5278724 | tf_op jit(solution)/shard_map/while/body/eval_jaxpr/dot_general | solution.py:16
  197.9 2.3 multiply_reduce_fusion.3
  200.3 5.8 %fusion.33 = f32[1280]{0:T(1024)S(1)} fusion(f32[1280]{0:T(1024)S(1)} %add_rsqrt_fusion.3, f32[1280]{0:T(1024)S(1)} %get-tuple-element.192, bf16[1280,1024]{1,0:T(8,128)(2,1)S(1)} %get-tuple-element.191, bf16[8,1280,1024]{2,1,0:T(8,128)(2,1)} %get-tuple-element.190, s32[]{:T(128)S(6)} %copy.19, s32[1280]{0:T(1024)S(1)} %get-tuple-element.189, ...), kind=kOutput, calls=%fused_computation.11.clone.1 | convolution fusion | flops 3366910720 | bytes 5278724 | tf_op jit(solution)/shard_map/while/body/eval_jaxpr/dot_general | solution.py:16
  206.1 2.3 multiply_reduce_fusion.3
  208.5 5.8 %fusion.33 = f32[1280]{0:T(1024)S(1)} fusion(f32[1280]{0:T(1024)S(1)} %add_rsqrt_fusion.3, f32[1280]{0:T(1024)S(1)} %get-tuple-element.192, bf16[1280,1024]{1,0:T(8,128)(2,1)S(1)} %get-tuple-element.191, bf16[8,1280,1024]{2,1,0:T(8,128)(2,1)} %get-tuple-element.190, s32[]{:T(128)S(6)} %copy.19, s32[1280]{0:T(1024)S(1)} %get-tuple-element.189, ...), kind=kOutput, calls=%fused_computation.11.clone.1 | convolution fusion | flops 3366910720 | bytes 5278724 | tf_op jit(solution)/shard_map/while/body/eval_jaxpr/dot_general | solution.py:16
  214.3 2.3 multiply_reduce_fusion.3
  216.7 5.8 %fusion.33 = f32[1280]{0:T(1024)S(1)} fusion(f32[1280]{0:T(1024)S(1)} %add_rsqrt_fusion.3, f32[1280]{0:T(1024)S(1)} %get-tuple-element.192, bf16[1280,1024]{1,0:T(8,128)(2,1)S(1)} %get-tuple-element.191, bf16[8,1280,1024]{2,1,0:T(8,128)(2,1)} %get-tuple-element.190, s32[]{:T(128)S(6)} %copy.19, s32[1280]{0:T(1024)S(1)} %get-tuple-element.189, ...), kind=kOutput, calls=%fused_computation.11.clone.1 | convolution fusion | flops 3366910720 | bytes 5278724 | tf_op jit(solution)/shard_map/while/body/eval_jaxpr/dot_general | solution.py:16
  222.5 2.3 multiply_reduce_fusion.3
  224.9 5.8 %fusion.33 = f32[1280]{0:T(1024)S(1)} fusion(f32[1280]{0:T(1024)S(1)} %add_rsqrt_fusion.3, f32[1280]{0:T(1024)S(1)} %get-tuple-element.192, bf16[1280,1024]{1,0:T(8,128)(2,1)S(1)} %get-tuple-element.191, bf16[8,1280,1024]{2,1,0:T(8,128)(2,1)} %get-tuple-element.190, s32[]{:T(128)S(6)} %copy.19, s32[1280]{0:T(1024)S(1)} %get-tuple-element.189, ...), kind=kOutput, calls=%fused_computation.11.clone.1 | convolution fusion | flops 3366910720 | bytes 5278724 | tf_op jit(solution)/shard_map/while/body/eval_jaxpr/dot_general | solution.py:16
  230.7 2.3 multiply_reduce_fusion.3
  233.1 5.8 %fusion.33 = f32[1280]{0:T(1024)S(1)} fusion(f32[1280]{0:T(1024)S(1)} %add_rsqrt_fusion.3, f32[1280]{0:T(1024)S(1)} %get-tuple-element.192, bf16[1280,1024]{1,0:T(8,128)(2,1)S(1)} %get-tuple-element.191, bf16[8,1280,1024]{2,1,0:T(8,128)(2,1)} %get-tuple-element.190, s32[]{:T(128)S(6)} %copy.19, s32[1280]{0:T(1024)S(1)} %get-tuple-element.189, ...), kind=kOutput, calls=%fused_computation.11.clone.1 | convolution fusion | flops 3366910720 | bytes 5278724 | tf_op jit(solution)/shard_map/while/body/eval_jaxpr/dot_general | solution.py:16
  238.9 2.3 multiply_reduce_fusion.3
  241.3 5.8 %fusion.33 = f32[1280]{0:T(1024)S(1)} fusion(f32[1280]{0:T(1024)S(1)} %add_rsqrt_fusion.3, f32[1280]{0:T(1024)S(1)} %get-tuple-element.192, bf16[1280,1024]{1,0:T(8,128)(2,1)S(1)} %get-tuple-element.191, bf16[8,1280,1024]{2,1,0:T(8,128)(2,1)} %get-tuple-element.190, s32[]{:T(128)S(6)} %copy.19, s32[1280]{0:T(1024)S(1)} %get-tuple-element.189, ...), kind=kOutput, calls=%fused_computation.11.clone.1 | convolution fusion | flops 3366910720 | bytes 5278724 | tf_op jit(solution)/shard_map/while/body/eval_jaxpr/dot_general | solution.py:16
  247.1 2.3 multiply_reduce_fusion.3
  249.5 5.8 %fusion.33 = f32[1280]{0:T(1024)S(1)} fusion(f32[1280]{0:T(1024)S(1)} %add_rsqrt_fusion.3, f32[1280]{0:T(1024)S(1)} %get-tuple-element.192, bf16[1280,1024]{1,0:T(8,128)(2,1)S(1)} %get-tuple-element.191, bf16[8,1280,1024]{2,1,0:T(8,128)(2,1)} %get-tuple-element.190, s32[]{:T(128)S(6)} %copy.19, s32[1280]{0:T(1024)S(1)} %get-tuple-element.189, ...), kind=kOutput, calls=%fused_computation.11.clone.1 | convolution fusion | flops 3366910720 | bytes 5278724 | tf_op jit(solution)/shard_map/while/body/eval_jaxpr/dot_general | solution.py:16
  255.3 0.8 all_to_all.41
  256.0 8.1 %all-to-all-start.3 = ((f32[128,10,1]{1,2,0:T(1,128)}), f32[128,10,1]{1,2,0:T(1,128)S(1)}, u32[]{:S(2)}, u32[]{:S(2)}) async-start(f32[128,10,1]{1,2,0:T(1,128)} %bitcast.5), calls=%async_computation.3 | async-start | bytes 131072 | tf_op jit(solution)/shard_map/all_to_all | solution.py:86
  264.1 9.5 %all-to-all-done.3 = f32[128,10,1]{1,2,0:T(1,128)S(1)} async-done(((f32[128,10,1]{1,2,0:T(1,128)}), f32[128,10,1]{1,2,0:T(1,128)S(1)}, u32[]{:S(2)}, u32[]{:S(2)}) %all-to-all-start.3) | async-done | bytes 5152 | tf_op jit(solution)/shard_map/all_to_all | solution.py:86
  273.6 0.5 broadcast.93
  274.1 0.8 reduce.22
  274.9 0.1 all_to_all.43
  275.0 4.3 %gather_fusion = f32[512]{0:T(512)} fusion(f32[1280]{0:T(1024)S(1)} %all_to_all.43, s32[1024]{0:T(1024)S(1)} %pad_clamp_fusion), kind=kCustom, calls=%fused_computation | custom fusion | bytes 6144 | tf_op jit(solution)/shard_map/gather | solution.py:89
  (32 shorter events, 0.5 us)
Async XLA Ops:
  6.5 183.2 %all-gather.4.cloned.1.call-start = ((), (), s32[]{:S(2)}) async-start(), calls=%async_computation.4 | async-start | bytes 23592960 | tf_op jit(solution)/shard_map/all_gather | solution.py:81
  87.7 102.1 %copy-start = (bf16[1280,1024]{1,0:T(8,128)(2,1)S(1)}, bf16[1280,1024]{1,0:T(8,128)(2,1)}, u32[]{:S(2)}) copy-start(bf16[1280,1024]{1,0:T(8,128)(2,1)} %all_to_all.40) | copy-start | bytes 7864324
  91.2 15.1 %all-to-all-start = ((s32[128,10,1]{1,2,0:T(1,128)}), s32[128,10,1]{1,2,0:T(1,128)S(1)}, u32[]{:S(2)}, u32[]{:S(2)}) async-start(s32[128,10,1]{1,2,0:T(1,128)} %bitcast.2), calls=%async_computation | async-start | bytes 131072 | tf_op jit(solution)/shard_map/all_to_all | solution.py:74
  106.3 14.1 %all-to-all-start.1 = ((s32[128,10,1]{1,2,0:T(1,128)}), s32[128,10,1]{1,2,0:T(1,128)S(1)}, u32[]{:S(2)}, u32[]{:S(2)}) async-start(s32[128,10,1]{1,2,0:T(1,128)} %bitcast.3), calls=%async_computation.1 | async-start | bytes 131072 | tf_op jit(solution)/shard_map/all_to_all | solution.py:75
  256.0 17.6 %all-to-all-start.3 = ((f32[128,10,1]{1,2,0:T(1,128)}), f32[128,10,1]{1,2,0:T(1,128)S(1)}, u32[]{:S(2)}, u32[]{:S(2)}) async-start(f32[128,10,1]{1,2,0:T(1,128)} %bitcast.5), calls=%async_computation.3 | async-start | bytes 131072 | tf_op jit(solution)/shard_map/all_to_all | solution.py:86
Sparse Core Ops, SparseCore 0:
  87.8 101.8 all-gather.3
where the time goes:
time: 287 us; the launch traced here: 286 us
  blocking collectives  91 us (32%)
  waiting for transfers between devices  61.8 us (22%)
  matrix products  46.2 us (16%)
  other arithmetic  27.7 us (10%)
  local copies, waits for them, and re-layouts  27.3 us (10%)
  starting transfers between devices  18.2 us (6%)
  between operations  13.5 us (5%)
    all_to_all x1, blocking collectives, local(): lax.all_to_all(outbox, ('cluster', 'helper'), split_axis=0, concat_axis=0...  64.5 us
    dot_general x8, matrix products, best_block(): lax.dot_general(query_emb, key_emb, (((1,), (1,)), ((), ())), preferred_e...  46.2 us
    all_gather x1, waiting for transfers between devices, local(): lax.all_gather(inbox, 'helper', axis=0, tiled=True)  36.9 us
    reduce_sum x9, other arithmetic, inverse_norms(): return lax.rsqrt(jnp.sum(wide_rows * wide_rows, axis=1) + 1e-06)  21.8 us
    all_gather x1, blocking collectives, local(): lax.all_gather(inbox_cl, 'helper', axis=0, tiled=True)  13.5 us
    all_gather x1, blocking collectives, local(): lax.all_gather(inbox_ord, 'helper', axis=0, tiled=True)  13 us
    all_to_all x1, waiting for transfers between devices, local(): lax.all_to_all(best_sim, ('cluster', 'helper'), split_axis=0, concat_axis...  9.49 us
    all_to_all x1, waiting for transfers between devices, local(): lax.all_to_all(outbox_ord, ('cluster', 'helper'), split_axis=0, concat_ax...  9.36 us
  transfers between devices with their start and end apart: 4, of which 4 were waited for; matrix products, arithmetic and copies ran while one was open for 4% of the time, Pallas kernels for 0%

commit v1 on v0

v1 whole, which is shorter than its diff:
```python
import jax
import jax.numpy as jnp
from jax import lax
from jax.experimental import pallas as pl
from jax.experimental.pallas import tpu as pltpu
from jax.sharding import Mesh, PartitionSpec as P

CL_OWN = 32
ROW_DEV = 512
FEAT = 1024
OWNERS = 16
CAP = 80
CHIPS = 64
BINS = 4
PLACES = 12
FIX = 16
META = 128
WIDE = FEAT + FEAT // 2 + META
NARROW = FEAT + META
SLOTS = CHIPS * 8
EXTRA = CHIPS * 4
TAIL = 64
OWN = SLOTS + EXTRA + TAIL
LOW = -1e30
BAD = 4.0
FIELDS = 16

CHIP_AXES = ("x", "z", "y")
ALL_AXES = ("x", "z", "y", "core")
CLUSTER_AXES = ("x", "z")
HELPER_AXES = ("y", "core")

f32 = jnp.float32
bf16 = jnp.bfloat16
i32 = jnp.int32


def iota(shape, axis):
    return lax.broadcasted_iota(i32, shape, axis)


def hot(condition):
    return jnp.where(condition, 1.0, 0.0).astype(bf16)


def mm(a, b):
    return lax.dot_general(a, b, (((1,), (0,)), ((), ())), preferred_element_type=f32)


def mm_t(a, b):
    return lax.dot_general(a, b, (((1,), (1,)), ((), ())), preferred_element_type=f32)


def pieces(value):
    high = value.astype(bf16)
    rest = value - high.astype(f32)
    middle = rest.astype(bf16)
    low = (rest - middle.astype(f32)).astype(bf16)
    return high, middle, low


def bin_of(local_cluster):
    folded = local_cluster & 7
    return jnp.minimum(folded, 7 - folded)


def pack_kernel(chip_ref, emb_ref, cl_ref, ord_ref, out_ref, box_ref, rank_ref, flag_ref):
    emb = emb_ref[...]
    cl = cl_ref[...]
    order = ord_ref[...]
    rows = emb.shape[0]
    wide = emb.astype(f32)
    square = wide * wide
    square_high = square.astype(bf16)
    square_low = (square - square_high.astype(f32)).astype(bf16)
    ones = jnp.ones((8, emb.shape[1]), bf16)
    total = (mm_t(ones, square_high) + mm_t(ones, square_low))[0:1, :] + 1e-06
    inv = lax.rsqrt(total)
    inv = inv * (1.5 - 0.5 * total * inv * inv)
    owner = cl >> 5
    local_cluster = cl & (CL_OWN - 1)
    bins = bin_of(local_cluster)
    earlier = hot(iota((rows, rows), 0) < iota((rows, rows), 1))
    is_owner = iota((OWNERS, rows), 0) == owner
    owner_hot = jnp.where(is_owner, 1.0, 0.0)
    owner_count = jnp.sum(owner_hot, axis=1, keepdims=True)
    full = jnp.where(owner_count == CAP, 1.0, 0.0)
    busy = jnp.sum(owner_hot * full, axis=0, keepdims=True) > 0.5
    is_group = iota((OWNERS * BINS, rows), 0) == owner * BINS + bins
    group_hot = jnp.where(is_group, 1.0, 0.0)
    group_count = jnp.sum(group_hot, axis=1, keepdims=True)
    ranks = mm(jnp.concatenate([group_hot, owner_hot], axis=0).astype(bf16), earlier)
    place = jnp.sum(group_hot * ranks[: OWNERS * BINS], axis=0, keepdims=True).astype(i32)
    owner_place = jnp.sum(owner_hot * ranks[OWNERS * BINS :], axis=0, keepdims=True).astype(i32)
    over = place >= PLACES
    over_ranks = mm((owner_hot * jnp.where(over, 1.0, 0.0)).astype(bf16), earlier)
    spill = jnp.sum(owner_hot * over_ranks, axis=0, keepdims=True).astype(i32)
    taken = jnp.minimum(group_count, float(PLACES))
    new_bin = bins
    new_place = place
    passed = jnp.zeros_like(place)
    for b in range(BINS):
        here = iota((OWNERS * BINS, rows), 0) == owner * BINS + b
        used = jnp.sum(jnp.where(here, taken, 0.0), axis=0, keepdims=True).astype(i32)
        fits = over & (spill >= passed) & (spill < passed + (PLACES - used))
        new_bin = jnp.where(fits, b, new_bin)
        new_place = jnp.where(fits, used + spill - passed, new_place)
        passed = passed + (PLACES - used)
    base = (owner * BINS + new_bin) * 8
    main_target = jnp.where(busy | (new_place >= 8), -1, base + new_place)
    extra_target = jnp.where(busy | (new_place < 8), -8, base + new_place - 8)
    rank = jnp.where(busy, owner_place, -1)
    rank_ref[...] = rank
    most = jnp.max(jnp.where(full > 0.5, 0.0, owner_count), axis=0, keepdims=True)
    flag = (jnp.sum(full, axis=0, keepdims=True) != 1.0) | (most > BINS * PLACES)
    flag_ref[...] = jnp.broadcast_to(jnp.where(flag, 1.0, 0.0), flag_ref.shape)
    high, middle, low = pieces(inv)
    at = iota((1, rows), 1)
    fields = [
        local_cluster.astype(f32),
        (order >> 8).astype(f32),
        (order & 255).astype(f32),
        high.astype(f32),
        middle.astype(f32),
        low.astype(f32),
        jnp.ones((1, rows), f32),
        jnp.full((1, rows), chip_ref[0], i32).astype(f32),
        (at >> 8).astype(f32),
        (at & 255).astype(f32),
    ]
    field_at = iota((META, rows), 0)
    meta = jnp.zeros((META, rows), f32)
    meta_extra = jnp.zeros((META, rows), f32)
    for k, value in enumerate(fields):
        meta = jnp.where(field_at == k, value, meta)
        meta_extra = jnp.where(field_at == FIELDS + k, value, meta_extra)
    meta = meta.astype(bf16)
    meta_extra = meta_extra.astype(bf16)
    pick = hot(iota((CAP, rows), 0) == rank)
    box_ref[:, :FEAT] = mm(pick, emb).astype(bf16)
    box_ref[:, FEAT:] = mm_t(pick, meta).astype(bf16)
    slot = iota((SLOTS, rows), 0)
    pick = hot(slot == main_target)
    pick_first = hot(slot == extra_target)
    pick_second = hot(slot - 4 == extra_target)
    half = FEAT // 2
    shape = (CHIPS, 8, -1)
    out_ref[:, :, :FEAT] = mm(pick, emb).astype(bf16).reshape(CHIPS, 8, FEAT)
    halves = mm(pick_first, emb[:, :half]) + mm(pick_second, emb[:, half:])
    out_ref[:, :, FEAT : FEAT + half] = halves.astype(bf16).reshape(CHIPS, 8, half)
    beside = mm_t(pick, meta) + mm_t(pick_first, meta_extra)
    out_ref[:, :, FEAT + half :] = beside.astype(bf16).reshape(CHIPS, 8, META)


def fix_kernel(y_ref, flag_in_ref, in_ref, fix_ref, flag_ref):
    half = FEAT // 2
    meta = in_ref[:, :, FEAT + half :].reshape(SLOTS, META)
    turn = hot(iota((2 * FIELDS, META), 0) == iota((2 * FIELDS, META), 1))
    rows = mm_t(turn, meta)
    earlier = hot(iota((SLOTS, SLOTS), 0) < iota((SLOTS, SLOTS), 1))
    y = y_ref[0]

    def away(first):
        steps = (bin_of(rows[first : first + 1].astype(i32)) - y) & 3
        return jnp.where(rows[first + 6 : first + 7] > 0.5, steps, 0)

    main = away(0)
    extra = away(FIELDS)
    step_at = iota((8, SLOTS), 0)
    main_hot = jnp.where(step_at == main, 1.0, 0.0)
    extra_hot = jnp.where(step_at == extra, 1.0, 0.0)
    ranks = mm(jnp.concatenate([main_hot, extra_hot], axis=0).astype(bf16), earlier)
    main_count = jnp.sum(main_hot, axis=1, keepdims=True)
    count = main_count + jnp.sum(extra_hot, axis=1, keepdims=True)
    main_place = jnp.sum(main_hot * ranks[:8], axis=0, keepdims=True).astype(i32)
    extra_place = jnp.sum(extra_hot * (ranks[8:] + main_count), axis=0, keepdims=True).astype(i32)
    main_target = jnp.where((main > 0) & (main_place < FIX), (main - 1) * FIX + main_place, -1)
    extra_target = jnp.where((extra > 0) & (extra_place < FIX), (extra - 1) * FIX + extra_place, -1)
    slot = iota((3 * FIX, SLOTS), 0)
    pick = hot(slot == main_target)
    pick_first = hot(slot == extra_target)
    later = hot(iota((SLOTS, SLOTS), 1) == iota((SLOTS, SLOTS), 0) + 4)
    pick_second = mm(pick_first, later).astype(bf16)
    whole = in_ref[:, :, :FEAT].reshape(SLOTS, FEAT)
    halves = in_ref[:, :, FEAT : FEAT + half].reshape(SLOTS, half)
    taken = mm(pick, whole)
    fix_ref[:, :half] = (taken[:, :half] + mm(pick_first, halves)).astype(bf16)
    fix_ref[:, half:FEAT] = (taken[:, half:] + mm(pick_second, halves)).astype(bf16)
    back = hot((iota((META, META), 0) == iota((META, META), 1) + FIELDS) & (iota((META, META), 1) < FIELDS))
    keep = hot((iota((META, META), 0) == iota((META, META), 1)) & (iota((META, META), 1) < FIELDS))
    beside = mm(mm(pick, meta).astype(bf16), keep) + mm(mm(pick_first, meta).astype(bf16), back)
    fix_ref[:, FEAT:] = beside.astype(bf16)
    step_row = iota((8, 1), 0)
    too_many = jnp.max(jnp.where((step_row > 0) & (count > FIX), 1.0, 0.0), axis=0, keepdims=True)
    flag = jnp.maximum(flag_in_ref[0:1, 0:1], too_many)
    spot = (iota((FIX, NARROW), 0) == 0) & (iota((FIX, NARROW), 1) == FEAT + 10)
    flag_ref[...] = jnp.where(spot, flag, 0.0).astype(bf16)


def key_columns(meta):
    wide = meta.astype(f32)
    position = wide[:, 1:2] * 256.0 + wide[:, 2:3]
    position = jnp.where(wide[:, 6:7] > 0.5, position, 1e9)
    return wide[:, 0:1], position, wide[:, 3:4] + wide[:, 4:5] + wide[:, 5:6]


def query_rows(meta):
    turn = hot(iota((FIELDS, META), 0) == iota((FIELDS, META), 1))
    return mm_t(turn, meta)


def best_over_keys(keys, metas, queries, query_fields, blocks):
    query_cl = query_fields[0:1]
    query_ord = query_fields[1:2] * 256.0 + query_fields[2:3]
    query_inv = query_fields[3:4] + query_fields[4:5] + query_fields[5:6]
    best = jnp.full(query_cl.shape, LOW, f32)
    size = keys.shape[0] // blocks
    for k in range(blocks):
        at = slice(k * size, (k + 1) * size)
        cl, position, inv = key_columns(metas[at, :])
        scaled = mm_t(keys[at, :], queries) * inv
        live = (cl == query_cl) & (position < query_ord)
        best = jnp.maximum(best, jnp.max(jnp.where(live, scaled, LOW), axis=0, keepdims=True))
    return jnp.maximum(best * query_inv, -1.0)


def owned_kernel(own_ref, other_ref, own_tail_ref, other_tail_ref, out_ref, keys, metas):
    half = FEAT // 2
    source = iota((EXTRA, SLOTS), 1)
    wanted = iota((EXTRA, SLOTS), 0)
    first = hot(source == (wanted >> 2) * 8 + (wanted & 3))
    second = hot(source == (wanted >> 2) * 8 + (wanted & 3) + 4)
    back = hot((iota((META, META), 0) == iota((META, META), 1) + FIELDS) & (iota((META, META), 1) < FIELDS))
    for ref, tail, base in ((own_ref, own_tail_ref, 0), (other_ref, other_tail_ref, OWN)):
        at = slice(base, base + SLOTS)
        keys[at, :] = ref[:, :, :FEAT].reshape(SLOTS, FEAT)
        meta = ref[:, :, FEAT + half :].reshape(SLOTS, META)
        metas[at, :] = meta
        at = slice(base + SLOTS, base + SLOTS + EXTRA)
        halves = ref[:, :, FEAT : FEAT + half].reshape(SLOTS, half)
        keys[at, :half] = mm(first, halves).astype(bf16)
        keys[at, half:] = mm(second, halves).astype(bf16)
        metas[at, :] = mm(mm(first, meta).astype(bf16), back).astype(bf16)
        at = slice(base + SLOTS + EXTRA, base + OWN)
        keys[at, :] = tail[:, :FEAT]
        metas[at, :] = tail[:, FEAT:]
    fields = query_rows(metas[:OWN, :])
    best = best_over_keys(keys, metas, keys[:OWN, :], fields, 8)
    from_chip = jnp.where((iota((CHIPS, OWN), 0).astype(f32) == fields[7:8]) & (fields[6:7] > 0.5), 1.0, 0.0)
    high, middle, low = pieces(best)
    left = jnp.concatenate(
        [from_chip, from_chip * high.astype(f32), from_chip * middle.astype(f32), from_chip * low.astype(f32)], axis=0
    ).astype(bf16)
    wide = metas[:OWN, :].astype(f32)
    place = wide[:, 8:9] * 256.0 + wide[:, 9:10]
    right = hot(iota((OWN, ROW_DEV), 1).astype(f32) == place)
    spread = mm(left, right)
    value = spread[CHIPS : 2 * CHIPS] + spread[2 * CHIPS : 3 * CHIPS] + spread[3 * CHIPS :]
    out = jnp.where(spread[:CHIPS] > 0.5, value, -1.0)
    flag = jnp.maximum(own_tail_ref[3 * FIX : 3 * FIX + 1, FEAT + 10 : FEAT + 11].astype(f32), other_tail_ref[3 * FIX : 3 * FIX + 1, FEAT + 10 : FEAT + 11].astype(f32))
    out_ref[...] = jnp.where(flag > 0.5, BAD, out)


def busy_kernel(y_ref, core_ref, keys_ref, queries_ref, out_ref):
    fields = query_rows(queries_ref[:, FEAT:])
    best = best_over_keys(keys_ref.at[:, :FEAT], keys_ref.at[:, FEAT:], queries_ref[:, :FEAT], fields, 8)
    out_ref[...] = jnp.full(out_ref.shape, -1.0, f32)
    for k in range(8):
        core = core_ref[0] if k < 4 else 1 - core_ref[0]
        helper = ((y_ref[0] + k) & 3) * 2 + core
        out_ref[pl.ds(helper, 1), :CAP] = best[:, k * CAP : (k + 1) * CAP]


def last_kernel(spread_ref, busy_ref, rank_ref, out_ref, flag_ref):
    spread = spread_ref[...]
    flag_ref[...] = jnp.broadcast_to(jnp.max(jnp.max(spread, axis=0, keepdims=True), axis=1, keepdims=True), flag_ref.shape)
    owned = jnp.max(spread, axis=0, keepdims=True)
    busy = jnp.max(busy_ref[...], axis=0, keepdims=True)
    high, middle, low = pieces(busy)
    parts = jnp.concatenate([high.astype(f32), middle.astype(f32), low.astype(f32), jnp.zeros((5, META), f32)], axis=0)
    rank = rank_ref[...]
    pick = hot(iota((META, ROW_DEV), 0) == rank)
    taken = mm(parts.astype(bf16), pick)
    value = taken[0:1] + taken[1:2] + taken[2:3]
    out_ref[...] = jnp.where(rank >= 0, value, owned)


def call(kernel, shapes, args, specs, scratch=(), flops=0, bytes_accessed=0):
    return pl.pallas_call(
        kernel,
        out_shape=shapes,
        in_specs=[pl.BlockSpec(memory_space=s) for s in specs],
        out_specs=jax.tree.map(lambda _: pl.BlockSpec(memory_space=pltpu.VMEM), shapes),
        scratch_shapes=scratch,
        compiler_params=pltpu.CompilerParams(vmem_limit_bytes=48 * 1024 * 1024),
        cost_estimate=pl.CostEstimate(flops=flops, bytes_accessed=bytes_accessed, transcendentals=0),
    )(*args)


VMEM, SMEM = pltpu.VMEM, pltpu.SMEM


def fast(embeddings, clusters, order):
    shape = jax.ShapeDtypeStruct
    y, core = lax.axis_index("y"), lax.axis_index("core")
    chip = (lax.axis_index("x") * 4 + lax.axis_index("z")) * 4 + y
    outbox, box, rank, flag = call(
        pack_kernel,
        (
            shape((CHIPS, 8, WIDE), bf16),
            shape((CAP, NARROW), bf16),
            shape((1, ROW_DEV), i32),
            shape((8, 128), f32),
        ),
        (chip[None].astype(i32), embeddings, clusters[None, :], order[None, :]),
        (SMEM, VMEM, VMEM, VMEM),
        flops=2 * 700_000_000,
        bytes_accessed=3_000_000,
    )
    busy_keys = lax.all_gather(box, CLUSTER_AXES, axis=0, tiled=True)
    inbox = lax.all_to_all(outbox, CHIP_AXES, split_axis=0, concat_axis=0, tiled=True)
    along = [box] + [lax.ppermute(box, "y", [(i, (i - d) % 4) for i in range(4)]) for d in (1, 2, 3)]
    swap = [(0, 1), (1, 0)]
    same = jnp.concatenate(along, axis=0)
    busy_queries = jnp.concatenate([same, lax.ppermute(same, "core", swap)], axis=0)
    other = lax.ppermute(inbox, "core", swap)
    fix, flag_block = call(
        fix_kernel,
        (shape((3 * FIX, NARROW), bf16), shape((FIX, NARROW), bf16)),
        (y[None].astype(i32), flag, inbox),
        (SMEM, VMEM, VMEM),
        flops=2 * 100_000_000,
        bytes_accessed=2_000_000,
    )
    got = [
        lax.ppermute(fix[(d - 1) * FIX : d * FIX], "y", [(i, (i + d) % 4) for i in range(4)]) for d in (1, 2, 3)
    ]
    tail = jnp.concatenate(got + [flag_block], axis=0)
    other_tail = lax.ppermute(tail, "core", swap)
    spread = call(
        owned_kernel,
        shape((CHIPS, ROW_DEV), f32),
        (inbox, other, tail, other_tail),
        (VMEM, VMEM, VMEM, VMEM),
        scratch=(pltpu.VMEM((2 * OWN, FEAT), bf16), pltpu.VMEM((2 * OWN, META), bf16)),
        flops=2 * 1_600_000_000,
        bytes_accessed=4_000_000,
    )
    returned = lax.all_to_all(spread, CHIP_AXES, split_axis=0, concat_axis=0, tiled=True)
    partial = call(
        busy_kernel,
        shape((8, META), f32),
        (y[None].astype(i32), core[None].astype(i32), busy_keys, busy_queries),
        (SMEM, SMEM, VMEM, VMEM),
        flops=2 * 900_000_000,
        bytes_accessed=4_500_000,
    )
    busy = lax.all_to_all(partial, HELPER_AXES, split_axis=0, concat_axis=0, tiled=True)
    out, worst = call(
        last_kernel,
        (shape((1, ROW_DEV), f32), shape((8, 128), f32)),
        (returned, busy, rank),
        (VMEM, VMEM, VMEM),
    )
    return out[0], worst[0, 0] > 2.0


def inverse_norms(row_values):
    wide_rows = row_values.astype(f32)
    return lax.rsqrt(jnp.sum(wide_rows * wide_rows, axis=1) + 1e-06)


def general(embeddings, clusters, order):
    owners, helpers = 16, 8
    slot_count = ROW_DEV * 5 // (2 * owners * helpers)
    total_rows = owners * helpers * slot_count
    owner_of = clusters // CL_OWN
    one_hot = (owner_of[:, None] == jnp.arange(owners, dtype=i32)[None, :]).astype(i32)
    before = jnp.cumsum(one_hot, axis=0) - one_hot
    place_in = jnp.sum(before * one_hot, axis=1)
    target = (owner_of * helpers + place_in % helpers) * slot_count + place_in // helpers
    outbox = jnp.zeros((total_rows, FEAT), embeddings.dtype).at[target].set(embeddings)
    outbox_cl = jnp.full((total_rows,), -1, i32).at[target].set(clusters)
    outbox_ord = jnp.zeros((total_rows,), i32).at[target].set(order)

    def exchange(value):
        return lax.all_to_all(value, ALL_AXES, split_axis=0, concat_axis=0, tiled=True)

    def gather(value):
        return lax.all_gather(value, HELPER_AXES, axis=0, tiled=True)

    inbox, inbox_cl, inbox_ord = exchange(outbox), exchange(outbox_cl), exchange(outbox_ord)
    query_inv = inverse_norms(inbox)

    def advance(best, block):
        key_emb, key_cl, key_ord = block
        gram = lax.dot_general(inbox, key_emb, (((1,), (1,)), ((), ())), preferred_element_type=f32)
        cosine = gram * query_inv[:, None] * inverse_norms(key_emb)[None, :]
        live = (key_cl[None, :] == inbox_cl[:, None]) & (key_ord[None, :] < inbox_ord[:, None])
        return jnp.maximum(best, jnp.max(jnp.where(live, cosine, -1.0), axis=1)), None

    blocks = (
        gather(inbox).reshape(helpers, total_rows, FEAT),
        gather(inbox_cl).reshape(helpers, total_rows),
        gather(inbox_ord).reshape(helpers, total_rows),
    )
    best, _ = lax.scan(advance, jnp.full((total_rows,), -1.0, f32), blocks)
    return exchange(best)[target]


def local(embeddings, clusters, order):
    out, overflow = fast(embeddings, clusters, order)
    return lax.cond(overflow, lambda: general(embeddings, clusters, order), lambda: out)


def solution(mesh):
    grid = Mesh(mesh.devices.reshape(4, 4, 4, 2), ALL_AXES)
    placed = (P(ALL_AXES, None), P(ALL_AXES), P(ALL_AXES))
    return jax.shard_map(local, mesh=grid, in_specs=placed, out_specs=P(ALL_AXES), check_vma=False)
```

time: 287 us -> 111 us (0.39)
  blocking collectives: 91 us -> 0 us
  matrix products: 46.2 us -> 0 us
  waiting for transfers between devices: 61.8 us -> 34.3 us
  other arithmetic: 27.7 us -> 1.93 us
  local copies, waits for them, and re-layouts: 27.3 us -> 6.96 us
  starting transfers between devices: 18.2 us -> 36 us
  Pallas kernels: 0 us -> 16.6 us
    all_to_all x1 -> x0, blocking collectives: 64.5 us -> none  [local(): lax.all_to_all(outbox, ('cluster', 'helper'), split_axis=0, concat_axis=0...]
    dot_general x8 -> x0, matrix products: 46.2 us -> none  [best_block(): lax.dot_general(query_emb, key_emb, (((1,), (1,)), ((), ())), preferred_e...]
    all_gather x1, waiting for transfers between devices: 36.9 us -> 0.02 us  [fast(): busy_keys = lax.all_gather(box, CLUSTER_AXES, axis=0, tiled=True)]
    ppermute x0 -> x9, waiting for transfers between devices: none -> 27.2 us  [the longest x3 22.8 us: fast(): lax.ppermute(box, 'y', [(i, (i - d) % 4) for i in range(4)])]
    all_gather x2 -> x0, blocking collectives: 26.5 us -> none  [the longest x1 13.5 us: local(): lax.all_gather(inbox_cl, 'helper', axis=0, tiled=True)]
    reduce_sum x10 -> x0, other arithmetic: 21.9 us -> none  [the longest x9 21.8 us: inverse_norms(): return lax.rsqrt(jnp.sum(wide_rows * wide_rows, axis=1) + 1e-06)]
    all_to_all x3, waiting for transfers between devices: 25 us -> 7.11 us  [the longest x1 4.58 us: fast(): lax.all_to_all(partial, HELPER_AXES, split_axis=0, concat_axis=0, tiled=T...]
    pallas_call x0 -> x5, Pallas kernels: none -> 16.6 us  [call(): pl.pallas_call(kernel, out_shape=shapes, in_specs=[pl.BlockSpec(memory_sp...]
  transfers between devices with their start and end apart: 4 -> 13, of which waited for: 4 -> 6; matrix products, arithmetic and copies ran while one was open for 4% -> 5% of each run, Pallas kernels for 0% -> 10%
where the time goes in v1:
time: 111 us; the launch traced here: 110 us
  starting transfers between devices  36 us (32%)
  waiting for transfers between devices  34.3 us (31%)
  Pallas kernels  16.6 us (15%)
  between operations  14.2 us (13%)
  local copies, waits for them, and re-layouts  6.96 us (6%)
  other arithmetic  1.93 us (2%)
    ppermute x3, waiting for transfers between devices, fast(): lax.ppermute(box, 'y', [(i, (i - d) % 4) for i in range(4)])  22.8 us
    pallas_call x5, Pallas kernels, call(): pl.pallas_call(kernel, out_shape=shapes, in_specs=[pl.BlockSpec(memory_sp...  16.6 us
    all_to_all x1, starting transfers between devices, fast(): lax.all_to_all(outbox, CHIP_AXES, split_axis=0, concat_axis=0, tiled=True)  12 us
    all_to_all x1, starting transfers between devices, fast(): lax.all_to_all(spread, CHIP_AXES, split_axis=0, concat_axis=0, tiled=True)  7.51 us
    all_to_all x1, starting transfers between devices, fast(): lax.all_to_all(partial, HELPER_AXES, split_axis=0, concat_axis=0, tiled=T...  4.8 us
    ppermute x3, starting transfers between devices, fast(): lax.ppermute(box, 'y', [(i, (i - d) % 4) for i in range(4)])  4.66 us
    all_to_all x1, waiting for transfers between devices, fast(): lax.all_to_all(partial, HELPER_AXES, split_axis=0, concat_axis=0, tiled=T...  4.58 us
    unnamed x14, local copies, waits for them, and re-layouts  4.39 us
  transfers between devices with their start and end apart: 13, of which 6 were waited for; matrix products, arithmetic and copies ran while one was open for 5% of the time, Pallas kernels for 10%

profile of v1, /device:TPU:1, one launch (start us, length us, event | category | flops | bytes accessed | tf_op | source)
XLA Modules:
  0.0 110.2 jit_solution(5967607198633833506)
XLA Ops:
  6.5 0.0 all-gather.7.cloned.1.call-start
  6.5 5.0 %shard_map.39 = (bf16[64,8,1664]{2,1,0:T(8,128)(2,1)}, bf16[80,1152]{1,0:T(8,128)(2,1)}, s32[1,512]{1,0:T(1,128)S(1)}, f32[8,128]{1,0:T(8,128)S(1)}) custom-call(s32[1]{0:T(128)} %bitcast.7.chip_ref, bf16[512,1024]{1,0:T(8,128)(2,1)} %emb_ref.1, s32[1,512]{1,0:T(1,128)} %bitcast.83, s32[1,512]{1,0:T(1,128)} %bitcast.84), custom_call_target="tpu_custom_call" | custom-call | flops 1400000000 | bytes 3000000 | tf_op jit(solution)/shard_map/pallas_call | solution.py:289
  11.6 0.0 all-gather.7.cloned.1.call-update
  11.6 12.0 %all-to-all-start.4 = ((bf16[64,8,1664]{2,1,0:T(8,128)(2,1)}), bf16[64,8,1664]{2,1,0:T(8,128)(2,1)S(1)}, u32[]{:S(2)}, u32[]{:S(2)}) async-start(bf16[64,8,1664]{2,1,0:T(8,128)(2,1)} %get-tuple-element.75), calls=%async_computation.4 | async-start | bytes 3407872 | tf_op jit(solution)/shard_map/all_to_all | solution.py:321
  23.6 1.1 collective-permute-start.7
  24.7 2.4 %collective-permute-start.6 = (bf16[80,1152]{1,0:T(8,128)(2,1)}, bf16[80,1152]{1,0:T(8,128)(2,1)S(1)}, u32[]{:S(2)}, u32[]{:S(2)}) collective-permute-start(bf16[80,1152]{1,0:T(8,128)(2,1)} %get-tuple-element.79), channel_id=1, source_target_pairs={{0,4},{2,6},{4,0},{6,2},{1,5},{3,7},{5,1},{7,3},{8,12},{10,14},{12... | collective-permute-start | bytes 552968 | tf_op jit(solution)/shard_map/ppermute | solution.py:322
  27.1 1.2 %collective-permute-start.5 = (bf16[80,1152]{1,0:T(8,128)(2,1)}, bf16[80,1152]{1,0:T(8,128)(2,1)}, u32[]{:S(2)}, u32[]{:S(2)}) collective-permute-start(bf16[80,1152]{1,0:T(8,128)(2,1)} %get-tuple-element.79), channel_id=1, source_target_pairs={{0,6},{2,0},{4,2},{6,4},{1,7},{3,1},{5,3},{7,5},{8,14},{10,8},{12,... | collective-permute-start | bytes 552968 | tf_op jit(solution)/shard_map/ppermute | solution.py:322
  28.2 1.0 constant_dynamic-update-slice_fusion.8
  29.2 19.6 %collective-permute-done.7 = bf16[80,1152]{1,0:T(8,128)(2,1)S(1)} collective-permute-done((bf16[80,1152]{1,0:T(8,128)(2,1)}, bf16[80,1152]{1,0:T(8,128)(2,1)S(1)}, u32[]{:S(2)}, u32[]{:S(2)}) %collective-permute-start.7) | collective-permute-done | bytes 184352 | tf_op jit(solution)/shard_map/ppermute | solution.py:322
  48.8 3.2 %collective-permute-done.6 = bf16[80,1152]{1,0:T(8,128)(2,1)S(1)} collective-permute-done((bf16[80,1152]{1,0:T(8,128)(2,1)}, bf16[80,1152]{1,0:T(8,128)(2,1)S(1)}, u32[]{:S(2)}, u32[]{:S(2)}) %collective-permute-start.6) | collective-permute-done | bytes 184352 | tf_op jit(solution)/shard_map/ppermute | solution.py:322
  52.0 0.0 collective-permute-done.5
  52.0 1.9 %pad_maximum_fusion = bf16[320,1152]{1,0:T(8,128)(2,1)} fusion(bf16[80,1152]{1,0:T(8,128)(2,1)S(1)} %collective-permute-done.7, bf16[80,1152]{1,0:T(8,128)(2,1)S(1)} %collective-permute-done.6, bf16[80,1152]{1,0:T(8,128)(2,1)} %collective-permute-done.5, bf16[80,1152]{1,0:T(8,128)(2,1)} %get-tuple-element.79), kind=kLoop, calls=%fused_computation.56 | loop fusion | flops 2949120 | bytes 1474560 | tf_op jit(solution)/shard_map/concatenate | solution.py:324
  53.9 1.7 %collective-permute-start.8 = (bf16[320,1152]{1,0:T(8,128)(2,1)}, bf16[320,1152]{1,0:T(8,128)(2,1)}, u32[]{:S(2)}, u32[]{:S(2)}) collective-permute-start(bf16[320,1152]{1,0:T(8,128)(2,1)} %pad_maximum_fusion), channel_id=1, source_target_pairs={{0,1},{1,0},{2,3},{3,2},{4,5},{5,4},{6,7},{7,6},{8,9},{9,8},{10,11... | collective-permute-start | bytes 2211848 | tf_op jit(solution)/shard_map/ppermute | solution.py:325
  55.7 0.9 constant_dynamic-update-slice_fusion.7
  56.7 0.0 all-to-all-done.4.in_ref.own_ref
  56.7 0.1 collective-permute-start
  56.8 1.0 shard_map.40
  57.8 0.1 collective-permute-start.1
  57.9 2.7 %collective-permute-start.3 = (bf16[16,1152]{1,0:T(8,128)(2,1)S(1)}, bf16[16,1152]{1,0:T(8,128)(2,1)S(1)}, u32[]{:S(2)}, u32[]{:S(2)}) collective-permute-start(bf16[16,1152]{1,0:T(8,128)(2,1)S(1)} %get-tuple-element.134), channel_id=1, source_target_pairs={{0,6},{2,0},{4,2},{6,4},{1,7},{3,1},{5,3},{7,5},{8,14},{10,8},{12,... | collective-permute-start | bytes 110600 | tf_op jit(solution)/shard_map/ppermute | solution.py:336
  60.6 0.0 collective-permute-start.2
  60.6 1.2 %collective-permute-done.1 = bf16[16,1152]{1,0:T(8,128)(2,1)S(1)} collective-permute-done((bf16[16,1152]{1,0:T(8,128)(2,1)S(1)}, bf16[16,1152]{1,0:T(8,128)(2,1)S(1)}, u32[]{:S(2)}, u32[]{:S(2)}) %collective-permute-start.1) | collective-permute-done | bytes 36896 | tf_op jit(solution)/shard_map/ppermute | solution.py:336
  61.9 3.1 %collective-permute-done.2 = bf16[16,1152]{1,0:T(8,128)(2,1)S(1)} collective-permute-done((bf16[16,1152]{1,0:T(8,128)(2,1)S(1)}, bf16[16,1152]{1,0:T(8,128)(2,1)S(1)}, u32[]{:S(2)}, u32[]{:S(2)}) %collective-permute-start.2) | collective-permute-done | bytes 36896 | tf_op jit(solution)/shard_map/ppermute | solution.py:336
  65.0 0.0 collective-permute-done.3
  65.0 2.4 %collective-permute-start.4 = (bf16[64,1152]{1,0:T(8,128)(2,1)S(1)}, bf16[64,1152]{1,0:T(8,128)(2,1)S(1)}, u32[]{:S(2)}, u32[]{:S(2)}) collective-permute-start(bf16[64,1152]{1,0:T(8,128)(2,1)S(1)} %constant_dynamic-update-slice_fusion.own_tail_ref), channel_id=1, source_target_pairs={{0,1},{1,0},{2,3},{3,2},{4,5},{5,4},{6,7},{7,6},{8,9},{9,8},{10,11... | collective-permute-start | bytes 442376 | tf_op jit(solution)/shard_map/ppermute | solution.py:339
  67.4 0.0 collective-permute-done.8
  67.4 1.2 %constant_dynamic-update-slice_fusion.4.queries_ref = bf16[640,1152]{1,0:T(8,128)(2,1)S(1)} fusion(bf16[640,1152]{1,0:T(8,128)(2,1)S(1)} %constant_dynamic-update-slice_fusion.5, bf16[320,1152]{1,0:T(8,128)(2,1)} %collective-permute-done.8), kind=kLoop, calls=%fused_computation.62 | loop fusion | bytes 1474560 | tf_op jit(solution)/shard_map/concatenate | solution.py:325
  68.7 0.0 collective-permute-done.4.other_tail_ref
  68.7 0.0 collective-permute-done.other_ref
  68.7 6.1 %shard_map.41 = f32[64,512]{1,0:T(8,128)S(1)} custom-call(bf16[64,8,1664]{2,1,0:T(8,128)(2,1)S(1)} %all-to-all-done.4.in_ref.own_ref, bf16[64,8,1664]{2,1,0:T(8,128)(2,1)S(1)} %collective-permute-done.other_ref, bf16[64,1152]{1,0:T(8,128)(2,1)S(1)} %constant_dynamic-update-slice_fusion.own_tail_ref, bf16[64,1152]{1,0:T(8,128)(2,1)S(1)} %collective-permute-done.4.other_tail_ref), custom_call_target="tpu_custom_call" | custom-call | flops 3200000000 | bytes 4000000 | tf_op jit(solution)/shard_map/pallas_call | solution.py:289
  74.8 0.8 copy.11
  75.6 7.5 %all-to-all-start.5 = ((f32[64,1,512]{2,1,0:T(1,128)}), f32[64,1,512]{2,1,0:T(1,128)S(1)}, u32[]{:S(2)}, u32[]{:S(2)}) async-start(f32[64,1,512]{2,1,0:T(1,128)} %copy.11), calls=%async_computation.5 | async-start | bytes 262144 | tf_op jit(solution)/shard_map/all_to_all | solution.py:349
  83.1 0.0 all-gather.7.cloned.1.call-done.keys_ref
  83.2 0.0 copy-start
  83.2 1.8 %copy-done = bf16[1280,1152]{1,0:T(8,128)(2,1)S(1)} copy-done((bf16[1280,1152]{1,0:T(8,128)(2,1)S(1)}, bf16[1280,1152]{1,0:T(8,128)(2,1)}, u32[]{:S(2)}) %copy-start) | copy-done | bytes 2949144
  85.0 0.0 copy-start.2
  85.0 4.3 %shard_map.42 = f32[8,128]{1,0:T(8,128)} custom-call(s32[1]{0:T(128)} %bitcast.10.y_ref, s32[1]{0:T(128)} %bitcast.12.core_ref, bf16[1280,1152]{1,0:T(8,128)(2,1)S(1)} %copy-done, bf16[640,1152]{1,0:T(8,128)(2,1)S(1)} %constant_dynamic-update-slice_fusion.4.queries_ref), custom_call_target="tpu_custom_call" | custom-call | flops 1800000000 | bytes 4500000 | tf_op jit(solution)/shard_map/pallas_call | solution.py:289
  89.3 2.5 %all-to-all-done.5 = f32[64,1,512]{2,1,0:T(1,128)S(1)} async-done(((f32[64,1,512]{2,1,0:T(1,128)}), f32[64,1,512]{2,1,0:T(1,128)S(1)}, u32[]{:S(2)}, u32[]{:S(2)}) %all-to-all-start.5) | async-done | bytes 131104 | tf_op jit(solution)/shard_map/all_to_all | solution.py:349
  91.8 4.8 %all-to-all-start.6 = ((f32[8,1,128]{2,1,0:T(1,128)}), f32[8,1,128]{2,1,0:T(1,128)S(1)}, u32[]{:S(2)}, u32[]{:S(2)}) async-start(f32[8,1,128]{2,1,0:T(1,128)} %bitcast.14), calls=%async_computation.6 | async-start | bytes 8192 | tf_op jit(solution)/shard_map/all_to_all | solution.py:358
  96.6 4.6 %all-to-all-done.6 = f32[8,1,128]{2,1,0:T(1,128)S(1)} async-done(((f32[8,1,128]{2,1,0:T(1,128)}), f32[8,1,128]{2,1,0:T(1,128)S(1)}, u32[]{:S(2)}, u32[]{:S(2)}) %all-to-all-start.6) | async-done | bytes 4128 | tf_op jit(solution)/shard_map/all_to_all | solution.py:358
  101.2 0.1 shard_map.43
  101.3 0.5 slice.21
  102.5 0.0 copy-done.2
  102.5 0.3 conditional.1
  102.8 0.0 copy-start.3
  102.8 0.6 copy-done.3
  (8 shorter events, 0.1 us)
Async XLA Ops:
  6.5 76.6 %all-gather.7.cloned.1.call-start = ((), (), s32[]{:S(2)}) async-start(), calls=%async_computation.8 | async-start | bytes 3133440 | tf_op jit(solution)/shard_map/all_gather | solution.py:320
  11.6 45.1 %all-to-all-start.4 = ((bf16[64,8,1664]{2,1,0:T(8,128)(2,1)}), bf16[64,8,1664]{2,1,0:T(8,128)(2,1)S(1)}, u32[]{:S(2)}, u32[]{:S(2)}) async-start(bf16[64,8,1664]{2,1,0:T(8,128)(2,1)} %get-tuple-element.75), calls=%async_computation.4 | async-start | bytes 3407872 | tf_op jit(solution)/shard_map/all_to_all | solution.py:321
  23.6 25.2 %collective-permute-start.7 = (bf16[80,1152]{1,0:T(8,128)(2,1)}, bf16[80,1152]{1,0:T(8,128)(2,1)S(1)}, u32[]{:S(2)}, u32[]{:S(2)}) collective-permute-start(bf16[80,1152]{1,0:T(8,128)(2,1)} %get-tuple-element.79), channel_id=1, source_target_pairs={{0,2},{2,4},{4,6},{6,0},{1,3},{3,5},{5,7},{7,1},{8,10},{10,12},{12... | collective-permute-start | bytes 552968 | tf_op jit(solution)/shard_map/ppermute | solution.py:322
  24.7 27.3 %collective-permute-start.6 = (bf16[80,1152]{1,0:T(8,128)(2,1)}, bf16[80,1152]{1,0:T(8,128)(2,1)S(1)}, u32[]{:S(2)}, u32[]{:S(2)}) collective-permute-start(bf16[80,1152]{1,0:T(8,128)(2,1)} %get-tuple-element.79), channel_id=1, source_target_pairs={{0,4},{2,6},{4,0},{6,2},{1,5},{3,7},{5,1},{7,3},{8,12},{10,14},{12... | collective-permute-start | bytes 552968 | tf_op jit(solution)/shard_map/ppermute | solution.py:322
  27.1 24.9 %collective-permute-start.5 = (bf16[80,1152]{1,0:T(8,128)(2,1)}, bf16[80,1152]{1,0:T(8,128)(2,1)}, u32[]{:S(2)}, u32[]{:S(2)}) collective-permute-start(bf16[80,1152]{1,0:T(8,128)(2,1)} %get-tuple-element.79), channel_id=1, source_target_pairs={{0,6},{2,0},{4,2},{6,4},{1,7},{3,1},{5,3},{7,5},{8,14},{10,8},{12,... | collective-permute-start | bytes 552968 | tf_op jit(solution)/shard_map/ppermute | solution.py:322
  53.9 13.5 %collective-permute-start.8 = (bf16[320,1152]{1,0:T(8,128)(2,1)}, bf16[320,1152]{1,0:T(8,128)(2,1)}, u32[]{:S(2)}, u32[]{:S(2)}) collective-permute-start(bf16[320,1152]{1,0:T(8,128)(2,1)} %pad_maximum_fusion), channel_id=1, source_target_pairs={{0,1},{1,0},{2,3},{3,2},{4,5},{5,4},{6,7},{7,6},{8,9},{9,8},{10,11... | collective-permute-start | bytes 2211848 | tf_op jit(solution)/shard_map/ppermute | solution.py:325
  56.7 12.0 %collective-permute-start = (bf16[64,8,1664]{2,1,0:T(8,128)(2,1)S(1)}, bf16[64,8,1664]{2,1,0:T(8,128)(2,1)S(1)}, u32[]{:S(2)}, u32[]{:S(2)}) collective-permute-start(bf16[64,8,1664]{2,1,0:T(8,128)(2,1)S(1)} %all-to-all-done.4.in_ref.own_ref), channel_id=1, source_target_pairs={{0,1},{1,0},{2,3},{3,2},{4,5},{5,4},{6,7},{7,6},{8,9},{9,8},{10,11... | collective-permute-start | bytes 5111816 | tf_op jit(solution)/shard_map/ppermute | solution.py:326
  57.8 4.1 %collective-permute-start.1 = (bf16[16,1152]{1,0:T(8,128)(2,1)S(1)}, bf16[16,1152]{1,0:T(8,128)(2,1)S(1)}, u32[]{:S(2)}, u32[]{:S(2)}) collective-permute-start(bf16[16,1152]{1,0:T(8,128)(2,1)S(1)} %get-tuple-element.136), channel_id=1, source_target_pairs={{0,2},{2,4},{4,6},{6,0},{1,3},{3,5},{5,7},{7,1},{8,10},{10,12},{12... | collective-permute-start | bytes 110600 | tf_op jit(solution)/shard_map/ppermute | solution.py:336
  57.9 7.1 %collective-permute-start.3 = (bf16[16,1152]{1,0:T(8,128)(2,1)S(1)}, bf16[16,1152]{1,0:T(8,128)(2,1)S(1)}, u32[]{:S(2)}, u32[]{:S(2)}) collective-permute-start(bf16[16,1152]{1,0:T(8,128)(2,1)S(1)} %get-tuple-element.134), channel_id=1, source_target_pairs={{0,6},{2,0},{4,2},{6,4},{1,7},{3,1},{5,3},{7,5},{8,14},{10,8},{12,... | collective-permute-start | bytes 110600 | tf_op jit(solution)/shard_map/ppermute | solution.py:336
  60.6 4.4 %collective-permute-start.2 = (bf16[16,1152]{1,0:T(8,128)(2,1)S(1)}, bf16[16,1152]{1,0:T(8,128)(2,1)S(1)}, u32[]{:S(2)}, u32[]{:S(2)}) collective-permute-start(bf16[16,1152]{1,0:T(8,128)(2,1)S(1)} %get-tuple-element.135), channel_id=1, source_target_pairs={{0,4},{2,6},{4,0},{6,2},{1,5},{3,7},{5,1},{7,3},{8,12},{10,14},{12... | collective-permute-start | bytes 110600 | tf_op jit(solution)/shard_map/ppermute | solution.py:336
  65.0 3.7 %collective-permute-start.4 = (bf16[64,1152]{1,0:T(8,128)(2,1)S(1)}, bf16[64,1152]{1,0:T(8,128)(2,1)S(1)}, u32[]{:S(2)}, u32[]{:S(2)}) collective-permute-start(bf16[64,1152]{1,0:T(8,128)(2,1)S(1)} %constant_dynamic-update-slice_fusion.own_tail_ref), channel_id=1, source_target_pairs={{0,1},{1,0},{2,3},{3,2},{4,5},{5,4},{6,7},{7,6},{8,9},{9,8},{10,11... | collective-permute-start | bytes 442376 | tf_op jit(solution)/shard_map/ppermute | solution.py:339
  75.6 16.2 %all-to-all-start.5 = ((f32[64,1,512]{2,1,0:T(1,128)}), f32[64,1,512]{2,1,0:T(1,128)S(1)}, u32[]{:S(2)}, u32[]{:S(2)}) async-start(f32[64,1,512]{2,1,0:T(1,128)} %copy.11), calls=%async_computation.5 | async-start | bytes 262144 | tf_op jit(solution)/shard_map/all_to_all | solution.py:349
  83.2 1.8 %copy-start = (bf16[1280,1152]{1,0:T(8,128)(2,1)S(1)}, bf16[1280,1152]{1,0:T(8,128)(2,1)}, u32[]{:S(2)}) copy-start(bf16[1280,1152]{1,0:T(8,128)(2,1)} %all-gather.7.cloned.1.call-done.keys_ref) | copy-start | bytes 8847364
  85.0 17.5 %copy-start.2 = (s32[512]{0:T(512)S(1)}, s32[512]{0:T(512)}, u32[]{:S(2)}) copy-start(s32[512]{0:T(512)} %param.8) | copy-start | bytes 6148
  91.8 9.4 %all-to-all-start.6 = ((f32[8,1,128]{2,1,0:T(1,128)}), f32[8,1,128]{2,1,0:T(1,128)S(1)}, u32[]{:S(2)}, u32[]{:S(2)}) async-start(f32[8,1,128]{2,1,0:T(1,128)} %bitcast.14), calls=%async_computation.6 | async-start | bytes 8192 | tf_op jit(solution)/shard_map/all_to_all | solution.py:358
  102.8 0.6 copy-start.3
Sparse Core Ops, SparseCore 0:
  11.7 65.7 all-gather.6

commit v2 on v1

--- a/solution.py
+++ b/solution.py
@@ -13,13 +13,14 @@
 CHIPS = 64
 BINS = 4
 PLACES = 12
-FIX = 16
+FIX = 32
 META = 128
 WIDE = FEAT + FEAT // 2 + META
 NARROW = FEAT + META
 SLOTS = CHIPS * 8
 EXTRA = CHIPS * 4
-TAIL = 64
+FLAG_ROWS = 16
+TAIL = 3 * FIX + FLAG_ROWS
 OWN = SLOTS + EXTRA + TAIL
 LOW = -1e30
 BAD = 4.0
@@ -64,7 +65,13 @@
     return jnp.minimum(folded, 7 - folded)
 
 
-def pack_kernel(chip_ref, emb_ref, cl_ref, ord_ref, out_ref, box_ref, rank_ref, flag_ref):
+def pack_kernel(chip_ref, emb_hbm, cl_hbm, ord_hbm, out_ref, box_ref, rank_ref, flag_ref, emb_ref, cl_ref, ord_ref, sems):
+    pairs = ((cl_hbm, cl_ref), (ord_hbm, ord_ref), (emb_hbm, emb_ref))
+    copies = [pltpu.make_async_copy(src, dst, sems.at[k]) for k, (src, dst) in enumerate(pairs)]
+    for copy in copies:
+        copy.start()
+    for copy in copies:
+        copy.wait()
     emb = emb_ref[...]
     cl = cl_ref[...]
     order = ord_ref[...]
@@ -99,7 +106,8 @@
     new_bin = bins
     new_place = place
     passed = jnp.zeros_like(place)
-    for b in range(BINS):
+    for step in range(BINS):
+        b = (chip_ref[0] + step) & 3
         here = iota((OWNERS * BINS, rows), 0) == owner * BINS + b
         used = jnp.sum(jnp.where(here, taken, 0.0), axis=0, keepdims=True).astype(i32)
         fits = over & (spill >= passed) & (spill < passed + (PLACES - used))
@@ -144,7 +152,6 @@
     pick_first = hot(slot == extra_target)
     pick_second = hot(slot - 4 == extra_target)
     half = FEAT // 2
-    shape = (CHIPS, 8, -1)
     out_ref[:, :, :FEAT] = mm(pick, emb).astype(bf16).reshape(CHIPS, 8, FEAT)
     halves = mm(pick_first, emb[:, :half]) + mm(pick_second, emb[:, half:])
     out_ref[:, :, FEAT : FEAT + half] = halves.astype(bf16).reshape(CHIPS, 8, half)
@@ -193,7 +200,7 @@
     step_row = iota((8, 1), 0)
     too_many = jnp.max(jnp.where((step_row > 0) & (count > FIX), 1.0, 0.0), axis=0, keepdims=True)
     flag = jnp.maximum(flag_in_ref[0:1, 0:1], too_many)
-    spot = (iota((FIX, NARROW), 0) == 0) & (iota((FIX, NARROW), 1) == FEAT + 10)
+    spot = (iota(flag_ref.shape, 0) == 0) & (iota(flag_ref.shape, 1) == FEAT + 10)
     flag_ref[...] = jnp.where(spot, flag, 0.0).astype(bf16)
 
 
@@ -245,7 +252,7 @@
         keys[at, :] = tail[:, :FEAT]
         metas[at, :] = tail[:, FEAT:]
     fields = query_rows(metas[:OWN, :])
-    best = best_over_keys(keys, metas, keys[:OWN, :], fields, 8)
+    best = best_over_keys(keys, metas, keys[:OWN, :], fields, 4)
     from_chip = jnp.where((iota((CHIPS, OWN), 0).astype(f32) == fields[7:8]) & (fields[6:7] > 0.5), 1.0, 0.0)
     high, middle, low = pieces(best)
     left = jnp.concatenate(
@@ -257,24 +264,26 @@
     spread = mm(left, right)
     value = spread[CHIPS : 2 * CHIPS] + spread[2 * CHIPS : 3 * CHIPS] + spread[3 * CHIPS :]
     out = jnp.where(spread[:CHIPS] > 0.5, value, -1.0)
-    flag = jnp.maximum(own_tail_ref[3 * FIX : 3 * FIX + 1, FEAT + 10 : FEAT + 11].astype(f32), other_tail_ref[3 * FIX : 3 * FIX + 1, FEAT + 10 : FEAT + 11].astype(f32))
-    out_ref[...] = jnp.where(flag > 0.5, BAD, out)
-
-
-def busy_kernel(y_ref, core_ref, keys_ref, queries_ref, out_ref):
+    at = slice(3 * FIX, 3 * FIX + 1), slice(FEAT + 10, FEAT + 11)
+    flag = jnp.maximum(own_tail_ref[at].astype(f32), other_tail_ref[at].astype(f32))
+    out = jnp.where(flag > 0.5, BAD, out)
+    for k in range(ROW_DEV // META):
+        out_ref[:, k, :] = out[:, k * META : (k + 1) * META]
+
+
+def busy_kernel(keys_ref, queries_ref, out_ref):
     fields = query_rows(queries_ref[:, FEAT:])
-    best = best_over_keys(keys_ref.at[:, :FEAT], keys_ref.at[:, FEAT:], queries_ref[:, :FEAT], fields, 8)
+    best = best_over_keys(keys_ref.at[:, :FEAT], keys_ref.at[:, FEAT:], queries_ref[:, :FEAT], fields, 4)
     out_ref[...] = jnp.full(out_ref.shape, -1.0, f32)
     for k in range(8):
-        core = core_ref[0] if k < 4 else 1 - core_ref[0]
-        helper = ((y_ref[0] + k) & 3) * 2 + core
-        out_ref[pl.ds(helper, 1), :CAP] = best[:, k * CAP : (k + 1) * CAP]
+        out_ref[k : k + 1, :CAP] = best[:, k * CAP : (k + 1) * CAP]
 
 
 def last_kernel(spread_ref, busy_ref, rank_ref, out_ref, flag_ref):
-    spread = spread_ref[...]
-    flag_ref[...] = jnp.broadcast_to(jnp.max(jnp.max(spread, axis=0, keepdims=True), axis=1, keepdims=True), flag_ref.shape)
-    owned = jnp.max(spread, axis=0, keepdims=True)
+    best = jnp.max(spread_ref[...], axis=0)
+    worst = jnp.max(jnp.max(best, axis=0, keepdims=True), axis=1, keepdims=True)
+    flag_ref[...] = jnp.broadcast_to(worst, flag_ref.shape)
+    owned = jnp.concatenate([best[k : k + 1] for k in range(ROW_DEV // META)], axis=1)
     busy = jnp.max(busy_ref[...], axis=0, keepdims=True)
     high, middle, low = pieces(busy)
     parts = jnp.concatenate([high.astype(f32), middle.astype(f32), low.astype(f32), jnp.zeros((5, META), f32)], axis=0)
@@ -285,14 +294,14 @@
     out_ref[...] = jnp.where(rank >= 0, value, owned)
 
 
-def call(kernel, shapes, args, specs, scratch=(), flops=0, bytes_accessed=0):
+def call(kernel, shapes, args, specs, scratch=(), flops=0, bytes_accessed=0, vmem=28):
     return pl.pallas_call(
         kernel,
         out_shape=shapes,
         in_specs=[pl.BlockSpec(memory_space=s) for s in specs],
         out_specs=jax.tree.map(lambda _: pl.BlockSpec(memory_space=pltpu.VMEM), shapes),
         scratch_shapes=scratch,
-        compiler_params=pltpu.CompilerParams(vmem_limit_bytes=48 * 1024 * 1024),
+        compiler_params=pltpu.CompilerParams(vmem_limit_bytes=vmem * 1024 * 1024),
         cost_estimate=pl.CostEstimate(flops=flops, bytes_accessed=bytes_accessed, transcendentals=0),
     )(*args)
 
@@ -302,7 +311,7 @@
 
 def fast(embeddings, clusters, order):
     shape = jax.ShapeDtypeStruct
-    y, core = lax.axis_index("y"), lax.axis_index("core")
+    y = lax.axis_index("y")
     chip = (lax.axis_index("x") * 4 + lax.axis_index("z")) * 4 + y
     outbox, box, rank, flag = call(
         pack_kernel,
@@ -313,25 +322,30 @@
             shape((8, 128), f32),
         ),
         (chip[None].astype(i32), embeddings, clusters[None, :], order[None, :]),
-        (SMEM, VMEM, VMEM, VMEM),
+        (SMEM, pl.ANY, pl.ANY, pl.ANY),
+        scratch=(
+            pltpu.VMEM((ROW_DEV, FEAT), bf16),
+            pltpu.VMEM((1, ROW_DEV), i32),
+            pltpu.VMEM((1, ROW_DEV), i32),
+            pltpu.SemaphoreType.DMA((3,)),
+        ),
         flops=2 * 700_000_000,
         bytes_accessed=3_000_000,
     )
     busy_keys = lax.all_gather(box, CLUSTER_AXES, axis=0, tiled=True)
     inbox = lax.all_to_all(outbox, CHIP_AXES, split_axis=0, concat_axis=0, tiled=True)
+    swap = [(0, 1), (1, 0)]
     along = [box] + [lax.ppermute(box, "y", [(i, (i - d) % 4) for i in range(4)]) for d in (1, 2, 3)]
-    swap = [(0, 1), (1, 0)]
-    same = jnp.concatenate(along, axis=0)
-    busy_queries = jnp.concatenate([same, lax.ppermute(same, "core", swap)], axis=0)
     other = lax.ppermute(inbox, "core", swap)
     fix, flag_block = call(
         fix_kernel,
-        (shape((3 * FIX, NARROW), bf16), shape((FIX, NARROW), bf16)),
+        (shape((3 * FIX, NARROW), bf16), shape((FLAG_ROWS, NARROW), bf16)),
         (y[None].astype(i32), flag, inbox),
         (SMEM, VMEM, VMEM),
         flops=2 * 100_000_000,
         bytes_accessed=2_000_000,
     )
+    fix, *along = lax.optimization_barrier((fix, *along))
     got = [
         lax.ppermute(fix[(d - 1) * FIX : d * FIX], "y", [(i, (i + d) % 4) for i in range(4)]) for d in (1, 2, 3)
     ]
@@ -339,23 +353,29 @@
     other_tail = lax.ppermute(tail, "core", swap)
     spread = call(
         owned_kernel,
-        shape((CHIPS, ROW_DEV), f32),
+        shape((CHIPS, ROW_DEV // META, META), f32),
         (inbox, other, tail, other_tail),
         (VMEM, VMEM, VMEM, VMEM),
         scratch=(pltpu.VMEM((2 * OWN, FEAT), bf16), pltpu.VMEM((2 * OWN, META), bf16)),
         flops=2 * 1_600_000_000,
         bytes_accessed=4_000_000,
     )
+    spread, *along = lax.optimization_barrier((spread, *along))
+    same = jnp.concatenate(along, axis=0)
+    busy_queries = jnp.concatenate([same, lax.ppermute(same, "core", swap)], axis=0)
     returned = lax.all_to_all(spread, CHIP_AXES, split_axis=0, concat_axis=0, tiled=True)
     partial = call(
         busy_kernel,
         shape((8, META), f32),
-        (y[None].astype(i32), core[None].astype(i32), busy_keys, busy_queries),
-        (SMEM, SMEM, VMEM, VMEM),
+        (busy_keys, busy_queries),
+        (VMEM, VMEM),
         flops=2 * 900_000_000,
         bytes_accessed=4_500_000,
     )
-    busy = lax.all_to_all(partial, HELPER_AXES, split_axis=0, concat_axis=0, tiled=True)
+    partial, returned = lax.optimization_barrier((partial, returned))
+    both = jnp.maximum(partial[:4], lax.ppermute(partial[4:], "core", swap))
+    back = [lax.ppermute(both[d : d + 1], "y", [(i, (i + d) % 4) for i in range(4)]) for d in (1, 2, 3)]
+    busy = jnp.concatenate([both[:1], *back], axis=0)
     out, worst = call(
         last_kernel,
         (shape((1, ROW_DEV), f32), shape((8, 128), f32)),

time: 111 us -> 108 us (0.973)
  local copies, waits for them, and re-layouts: 6.96 us -> 5.02 us
  Pallas kernels: 16.6 us -> 15.1 us
  starting transfers between devices: 36 us -> 37.4 us
    ppermute x3, waiting for transfers between devices: 22.8 us -> 0.01 us  [fast(): lax.ppermute(box, 'y', [(i, (i - d) % 4) for i in range(4)])]
    all_to_all x1, waiting for transfers between devices: 0.01 us -> 20.5 us  [fast(): lax.all_to_all(outbox, CHIP_AXES, split_axis=0, concat_axis=0, tiled=True)]
    all_to_all x1 -> x0, starting transfers between devices: 4.8 us -> none  [fast(): lax.all_to_all(partial, HELPER_AXES, split_axis=0, concat_axis=0, tiled=T...]
    all_to_all x1 -> x0, waiting for transfers between devices: 4.58 us -> none  [fast(): lax.all_to_all(partial, HELPER_AXES, split_axis=0, concat_axis=0, tiled=T...]
    ppermute x0 -> x4, waiting for transfers between devices: none -> 4.42 us  [the longest x3 3.6 us: fast(): lax.ppermute(both[d:d + 1], 'y', [(i, (i + d) % 4) for i in range(4)])]
    ppermute x0 -> x4, starting transfers between devices: none -> 3.64 us  [the longest x3 2.08 us: fast(): lax.ppermute(both[d:d + 1], 'y', [(i, (i + d) % 4) for i in range(4)])]
    ppermute x1, starting transfers between devices: 0.09 us -> 3.11 us  [fast(): other = lax.ppermute(inbox, 'core', swap)]
    pallas_call x5, Pallas kernels: 16.6 us -> 15.1 us  [call(): pl.pallas_call(kernel, out_shape=shapes, in_specs=[pl.BlockSpec(memory_sp...]
  transfers between devices with their start and end apart: 13 -> 16, of which waited for: 6 -> 9; matrix products, arithmetic and copies ran while one was open for 5% -> 3% of each run, Pallas kernels for 10% -> 9%
where the time goes in v2:
time: 108 us; the launch traced here: 106 us
  starting transfers between devices  37.4 us (35%)
  waiting for transfers between devices  33.4 us (31%)
  Pallas kernels  15.1 us (14%)
  between operations  14.2 us (13%)
  local copies, waits for them, and re-layouts  5.02 us (5%)
    all_to_all x1, waiting for transfers between devices, fast(): lax.all_to_all(outbox, CHIP_AXES, split_axis=0, concat_axis=0, tiled=True)  20.5 us
    pallas_call x5, Pallas kernels, call(): pl.pallas_call(kernel, out_shape=shapes, in_specs=[pl.BlockSpec(memory_sp...  15.1 us
    all_to_all x1, starting transfers between devices, fast(): lax.all_to_all(outbox, CHIP_AXES, split_axis=0, concat_axis=0, tiled=True)  12 us
    all_to_all x1, starting transfers between devices, fast(): lax.all_to_all(spread, CHIP_AXES, split_axis=0, concat_axis=0, tiled=True)  7.57 us
    ppermute x3, starting transfers between devices, fast(): lax.ppermute(box, 'y', [(i, (i - d) % 4) for i in range(4)])  4.66 us
    unnamed x15, local copies, waits for them, and re-layouts  4.37 us
    ppermute x3, waiting for transfers between devices, fast(): lax.ppermute(fix[(d - 1) * FIX:d * FIX], 'y', [(i, (i + d) % 4) for i in...  4.33 us
    ppermute x3, waiting for transfers between devices, fast(): lax.ppermute(both[d:d + 1], 'y', [(i, (i + d) % 4) for i in range(4)])  3.6 us
  transfers between devices with their start and end apart: 16, of which 9 were waited for; matrix products, arithmetic and copies ran while one was open for 3% of the time, Pallas kernels for 9%

profile of v2, /device:TPU:1, one launch (start us, length us, event | category | flops | bytes accessed | tf_op | source)
XLA Modules:
  0.0 106.4 jit_solution(1114497648949434651)
XLA Ops:
  6.5 0.0 all-gather.7.cloned.1.call-start
  6.5 5.1 %shard_map.39 = (bf16[64,8,1664]{2,1,0:T(8,128)(2,1)}, bf16[80,1152]{1,0:T(8,128)(2,1)}, s32[1,512]{1,0:T(1,128)S(1)}, f32[8,128]{1,0:T(8,128)S(1)}) custom-call(s32[1]{0:T(128)} %bitcast.7.chip_ref, bf16[512,1024]{1,0:T(8,128)(2,1)} %emb_hbm.1, s32[1,512]{1,0:T(1,128)} %bitcast.71, s32[1,512]{1,0:T(1,128)} %bitcast.72), custom_call_target="tpu_custom_call" | custom-call | flops 1400000000 | bytes 3000000 | tf_op jit(solution)/shard_map/pallas_call | solution.py:298
  11.6 0.0 all-gather.7.cloned.1.call-update
  11.7 12.0 %all-to-all-start.4 = ((bf16[64,8,1664]{2,1,0:T(8,128)(2,1)}), bf16[64,8,1664]{2,1,0:T(8,128)(2,1)S(1)}, u32[]{:S(2)}, u32[]{:S(2)}) async-start(bf16[64,8,1664]{2,1,0:T(8,128)(2,1)} %get-tuple-element.88), calls=%async_computation.4 | async-start | bytes 3407872 | tf_op jit(solution)/shard_map/all_to_all | solution.py:336
  23.6 1.1 %collective-permute-start.3 = (bf16[80,1152]{1,0:T(8,128)(2,1)}, bf16[80,1152]{1,0:T(8,128)(2,1)S(1)}, u32[]{:S(2)}, u32[]{:S(2)}) collective-permute-start(bf16[80,1152]{1,0:T(8,128)(2,1)} %get-tuple-element.97), channel_id=1, source_target_pairs={{0,2},{2,4},{4,6},{6,0},{1,3},{3,5},{5,7},{7,1},{8,10},{10,12},{12... | collective-permute-start | bytes 552968 | tf_op jit(solution)/shard_map/ppermute | solution.py:338
  24.7 2.4 %collective-permute-start.2 = (bf16[80,1152]{1,0:T(8,128)(2,1)}, bf16[80,1152]{1,0:T(8,128)(2,1)S(1)}, u32[]{:S(2)}, u32[]{:S(2)}) collective-permute-start(bf16[80,1152]{1,0:T(8,128)(2,1)} %get-tuple-element.97), channel_id=1, source_target_pairs={{0,4},{2,6},{4,0},{6,2},{1,5},{3,7},{5,1},{7,3},{8,12},{10,14},{12... | collective-permute-start | bytes 552968 | tf_op jit(solution)/shard_map/ppermute | solution.py:338
  27.1 1.2 %collective-permute-start.1 = (bf16[80,1152]{1,0:T(8,128)(2,1)}, bf16[80,1152]{1,0:T(8,128)(2,1)S(1)}, u32[]{:S(2)}, u32[]{:S(2)}) collective-permute-start(bf16[80,1152]{1,0:T(8,128)(2,1)} %get-tuple-element.97), channel_id=1, source_target_pairs={{0,6},{2,0},{4,2},{6,4},{1,7},{3,1},{5,3},{7,5},{8,14},{10,8},{12,... | collective-permute-start | bytes 552968 | tf_op jit(solution)/shard_map/ppermute | solution.py:338
  28.3 20.5 %all-to-all-done.4.in_ref.own_ref = bf16[64,8,1664]{2,1,0:T(8,128)(2,1)S(1)} async-done(((bf16[64,8,1664]{2,1,0:T(8,128)(2,1)}), bf16[64,8,1664]{2,1,0:T(8,128)(2,1)S(1)}, u32[]{:S(2)}, u32[]{:S(2)}) %all-to-all-start.4) | async-done | bytes 1703968 | tf_op jit(solution)/shard_map/all_to_all | solution.py:336
  48.8 3.1 %collective-permute-start = (bf16[64,8,1664]{2,1,0:T(8,128)(2,1)S(1)}, bf16[64,8,1664]{2,1,0:T(8,128)(2,1)S(1)}, u32[]{:S(2)}, u32[]{:S(2)}) collective-permute-start(bf16[64,8,1664]{2,1,0:T(8,128)(2,1)S(1)} %all-to-all-done.4.in_ref.own_ref), channel_id=1, source_target_pairs={{0,1},{1,0},{2,3},{3,2},{4,5},{5,4},{6,7},{7,6},{8,9},{9,8},{10,11... | collective-permute-start | bytes 5111816 | tf_op jit(solution)/shard_map/ppermute | solution.py:339
  51.9 1.0 shard_map.40
  52.9 0.0 collective-permute-done.3
  52.9 0.0 collective-permute-done.2
  52.9 0.0 collective-permute-done.1
  52.9 0.0 copy-start.2
  52.9 0.6 collective-permute-start.4
  53.6 2.1 %collective-permute-start.6 = (bf16[32,1152]{1,0:T(8,128)(2,1)S(1)}, bf16[32,1152]{1,0:T(8,128)(2,1)S(1)}, u32[]{:S(2)}, u32[]{:S(2)}) collective-permute-start(bf16[32,1152]{1,0:T(8,128)(2,1)S(1)} %get-tuple-element.158), channel_id=1, source_target_pairs={{0,6},{2,0},{4,2},{6,4},{1,7},{3,1},{5,3},{7,5},{8,14},{10,8},{12,... | collective-permute-start | bytes 221192 | tf_op jit(solution)/shard_map/ppermute | solution.py:350
  55.7 0.4 collective-permute-start.5
  56.1 1.4 %collective-permute-done.4 = bf16[32,1152]{1,0:T(8,128)(2,1)S(1)} collective-permute-done((bf16[32,1152]{1,0:T(8,128)(2,1)S(1)}, bf16[32,1152]{1,0:T(8,128)(2,1)S(1)}, u32[]{:S(2)}, u32[]{:S(2)}) %collective-permute-start.4) | collective-permute-done | bytes 73760 | tf_op jit(solution)/shard_map/ppermute | solution.py:350
  57.4 3.0 %collective-permute-done.5 = bf16[32,1152]{1,0:T(8,128)(2,1)S(1)} collective-permute-done((bf16[32,1152]{1,0:T(8,128)(2,1)S(1)}, bf16[32,1152]{1,0:T(8,128)(2,1)S(1)}, u32[]{:S(2)}, u32[]{:S(2)}) %collective-permute-start.5) | collective-permute-done | bytes 73760 | tf_op jit(solution)/shard_map/ppermute | solution.py:350
  60.4 0.0 collective-permute-done.6
  60.5 2.7 %collective-permute-start.7 = (bf16[112,1152]{1,0:T(8,128)(2,1)S(1)}, bf16[112,1152]{1,0:T(8,128)(2,1)S(1)}, u32[]{:S(2)}, u32[]{:S(2)}) collective-permute-start(bf16[112,1152]{1,0:T(8,128)(2,1)S(1)} %constant_dynamic-update-slice_fusion.own_tail_ref), channel_id=1, source_target_pairs={{0,1},{1,0},{2,3},{3,2},{4,5},{5,4},{6,7},{7,6},{8,9},{9,8},{10,11... | collective-permute-start | bytes 774152 | tf_op jit(solution)/shard_map/ppermute | solution.py:353
  63.1 1.2 %collective-permute-done.7.other_tail_ref = bf16[112,1152]{1,0:T(8,128)(2,1)S(1)} collective-permute-done((bf16[112,1152]{1,0:T(8,128)(2,1)S(1)}, bf16[112,1152]{1,0:T(8,128)(2,1)S(1)}, u32[]{:S(2)}, u32[]{:S(2)}) %collective-permute-start.7) | collective-permute-done | bytes 258080 | tf_op jit(solution)/shard_map/ppermute | solution.py:353
  64.3 0.0 collective-permute-done.other_ref
  64.3 6.2 %shard_map.41 = f32[64,4,128]{2,1,0:T(4,128)} custom-call(bf16[64,8,1664]{2,1,0:T(8,128)(2,1)S(1)} %all-to-all-done.4.in_ref.own_ref, bf16[64,8,1664]{2,1,0:T(8,128)(2,1)S(1)} %collective-permute-done.other_ref, bf16[112,1152]{1,0:T(8,128)(2,1)S(1)} %constant_dynamic-update-slice_fusion.own_tail_ref, bf16[112,1152]{1,0:T(8,128)(2,1)S(1)} %collective-permute-done.7.other_tail_ref), custom_call_target="tpu_custom_call" | custom-call | flops 3200000000 | bytes 4000000 | tf_op jit(solution)/shard_map/pallas_call | solution.py:298
  70.5 0.0 copy-done.2
  70.5 1.0 pad_maximum_fusion
  71.5 0.6 collective-permute-start.8
  72.2 0.9 constant_dynamic-update-slice_fusion.8
  73.1 7.6 %all-to-all-start.5 = ((f32[64,4,128]{2,1,0:T(4,128)}), f32[64,4,128]{2,1,0:T(4,128)S(1)}, u32[]{:S(2)}, u32[]{:S(2)}) async-start(f32[64,4,128]{2,1,0:T(4,128)} %shard_map.41), calls=%async_computation.5 | async-start | bytes 262144 | tf_op jit(solution)/shard_map/all_to_all | solution.py:366
  80.7 0.9 constant_dynamic-update-slice_fusion.7
  81.7 0.0 collective-permute-done.8
  81.7 0.1 constant_dynamic-update-slice_fusion.4.queries_ref
  81.8 0.0 all-gather.7.cloned.1.call-done.keys_ref
  81.8 0.0 copy-start
  81.8 1.8 %copy-done = bf16[1280,1152]{1,0:T(8,128)(2,1)S(1)} copy-done((bf16[1280,1152]{1,0:T(8,128)(2,1)S(1)}, bf16[1280,1152]{1,0:T(8,128)(2,1)}, u32[]{:S(2)}) %copy-start) | copy-done | bytes 2949144
  83.6 0.0 copy-start.3
  83.7 2.6 %shard_map.42 = f32[8,128]{1,0:T(8,128)S(1)} custom-call(bf16[1280,1152]{1,0:T(8,128)(2,1)S(1)} %copy-done, bf16[640,1152]{1,0:T(8,128)(2,1)S(1)} %constant_dynamic-update-slice_fusion.4.queries_ref), custom_call_target="tpu_custom_call" | custom-call | flops 1800000000 | bytes 4500000 | tf_op jit(solution)/shard_map/pallas_call | solution.py:298
  86.3 3.0 %all-to-all-done.5.spread_ref = f32[64,4,128]{2,1,0:T(4,128)S(1)} async-done(((f32[64,4,128]{2,1,0:T(4,128)}), f32[64,4,128]{2,1,0:T(4,128)S(1)}, u32[]{:S(2)}, u32[]{:S(2)}) %all-to-all-start.5) | async-done | bytes 131104 | tf_op jit(solution)/shard_map/all_to_all | solution.py:366
  89.3 1.6 %collective-permute-start.9 = (f32[4,128]{1,0:T(4,128)S(1)}, f32[4,128]{1,0:T(4,128)S(1)}, u32[]{:S(2)}, u32[]{:S(2)}) collective-permute-start(f32[4,128]{1,0:T(4,128)S(1)} %slice.40), channel_id=1, source_target_pairs={{0,1},{1,0},{2,3},{3,2},{4,5},{5,4},{6,7},{7,6},{8,9},{9,8},{10,11... | collective-permute-start | bytes 6152 | tf_op jit(solution)/shard_map/ppermute | solution.py:376
  90.9 0.8 collective-permute-done.9
  91.7 1.0 collective-permute-start.12
  92.7 1.1 %collective-permute-start.11 = (f32[1,128]{1,0:T(1,128)S(1)}, f32[1,128]{1,0:T(1,128)S(1)}, u32[]{:S(2)}, u32[]{:S(2)}) collective-permute-start(f32[1,128]{1,0:T(1,128)S(1)} %get-tuple-element.163), channel_id=1, source_target_pairs={{0,4},{2,6},{4,0},{6,2},{1,5},{3,7},{5,1},{7,3},{8,12},{10,14},{12... | collective-permute-start | bytes 1544 | tf_op jit(solution)/shard_map/ppermute | solution.py:377
  93.8 0.0 collective-permute-start.10
  93.8 0.3 collective-permute-done.12
  94.1 2.5 %collective-permute-done.11 = f32[1,128]{1,0:T(1,128)S(1)} collective-permute-done((f32[1,128]{1,0:T(1,128)S(1)}, f32[1,128]{1,0:T(1,128)S(1)}, u32[]{:S(2)}, u32[]{:S(2)}) %collective-permute-start.11) | collective-permute-done | bytes 544 | tf_op jit(solution)/shard_map/ppermute | solution.py:377
  96.6 0.8 collective-permute-done.10
  97.4 0.2 shard_map.43
  97.6 0.5 slice.45
  98.7 0.0 copy-done.3
  98.7 0.3 conditional.1
  99.0 0.0 copy-start.4
  99.0 0.6 copy-done.4
  (11 shorter events, 0.1 us)
Async XLA Ops:
  6.5 75.3 %all-gather.7.cloned.1.call-start = ((), (), s32[]{:S(2)}) async-start(), calls=%async_computation.7 | async-start | bytes 3133440 | tf_op jit(solution)/shard_map/all_gather | solution.py:335
  11.7 37.1 %all-to-all-start.4 = ((bf16[64,8,1664]{2,1,0:T(8,128)(2,1)}), bf16[64,8,1664]{2,1,0:T(8,128)(2,1)S(1)}, u32[]{:S(2)}, u32[]{:S(2)}) async-start(bf16[64,8,1664]{2,1,0:T(8,128)(2,1)} %get-tuple-element.88), calls=%async_computation.4 | async-start | bytes 3407872 | tf_op jit(solution)/shard_map/all_to_all | solution.py:336
  23.6 29.2 %collective-permute-start.3 = (bf16[80,1152]{1,0:T(8,128)(2,1)}, bf16[80,1152]{1,0:T(8,128)(2,1)S(1)}, u32[]{:S(2)}, u32[]{:S(2)}) collective-permute-start(bf16[80,1152]{1,0:T(8,128)(2,1)} %get-tuple-element.97), channel_id=1, source_target_pairs={{0,2},{2,4},{4,6},{6,0},{1,3},{3,5},{5,7},{7,1},{8,10},{10,12},{12... | collective-permute-start | bytes 552968 | tf_op jit(solution)/shard_map/ppermute | solution.py:338
  24.7 28.2 %collective-permute-start.2 = (bf16[80,1152]{1,0:T(8,128)(2,1)}, bf16[80,1152]{1,0:T(8,128)(2,1)S(1)}, u32[]{:S(2)}, u32[]{:S(2)}) collective-permute-start(bf16[80,1152]{1,0:T(8,128)(2,1)} %get-tuple-element.97), channel_id=1, source_target_pairs={{0,4},{2,6},{4,0},{6,2},{1,5},{3,7},{5,1},{7,3},{8,12},{10,14},{12... | collective-permute-start | bytes 552968 | tf_op jit(solution)/shard_map/ppermute | solution.py:338
  27.1 25.8 %collective-permute-start.1 = (bf16[80,1152]{1,0:T(8,128)(2,1)}, bf16[80,1152]{1,0:T(8,128)(2,1)S(1)}, u32[]{:S(2)}, u32[]{:S(2)}) collective-permute-start(bf16[80,1152]{1,0:T(8,128)(2,1)} %get-tuple-element.97), channel_id=1, source_target_pairs={{0,6},{2,0},{4,2},{6,4},{1,7},{3,1},{5,3},{7,5},{8,14},{10,8},{12,... | collective-permute-start | bytes 552968 | tf_op jit(solution)/shard_map/ppermute | solution.py:338
  48.8 15.5 %collective-permute-start = (bf16[64,8,1664]{2,1,0:T(8,128)(2,1)S(1)}, bf16[64,8,1664]{2,1,0:T(8,128)(2,1)S(1)}, u32[]{:S(2)}, u32[]{:S(2)}) collective-permute-start(bf16[64,8,1664]{2,1,0:T(8,128)(2,1)S(1)} %all-to-all-done.4.in_ref.own_ref), channel_id=1, source_target_pairs={{0,1},{1,0},{2,3},{3,2},{4,5},{5,4},{6,7},{7,6},{8,9},{9,8},{10,11... | collective-permute-start | bytes 5111816 | tf_op jit(solution)/shard_map/ppermute | solution.py:339
  52.9 17.6 %copy-start.2 = (bf16[80,1152]{1,0:T(8,128)(2,1)}, bf16[80,1152]{1,0:T(8,128)(2,1)S(1)}, u32[]{:S(2)}) copy-start(bf16[80,1152]{1,0:T(8,128)(2,1)S(1)} %collective-permute-done.1) | copy-start | bytes 552964
  52.9 4.5 %collective-permute-start.4 = (bf16[32,1152]{1,0:T(8,128)(2,1)S(1)}, bf16[32,1152]{1,0:T(8,128)(2,1)S(1)}, u32[]{:S(2)}, u32[]{:S(2)}) collective-permute-start(bf16[32,1152]{1,0:T(8,128)(2,1)S(1)} %get-tuple-element.160), channel_id=1, source_target_pairs={{0,2},{2,4},{4,6},{6,0},{1,3},{3,5},{5,7},{7,1},{8,10},{10,12},{12... | collective-permute-start | bytes 221192 | tf_op jit(solution)/shard_map/ppermute | solution.py:350
  53.6 6.8 %collective-permute-start.6 = (bf16[32,1152]{1,0:T(8,128)(2,1)S(1)}, bf16[32,1152]{1,0:T(8,128)(2,1)S(1)}, u32[]{:S(2)}, u32[]{:S(2)}) collective-permute-start(bf16[32,1152]{1,0:T(8,128)(2,1)S(1)} %get-tuple-element.158), channel_id=1, source_target_pairs={{0,6},{2,0},{4,2},{6,4},{1,7},{3,1},{5,3},{7,5},{8,14},{10,8},{12,... | collective-permute-start | bytes 221192 | tf_op jit(solution)/shard_map/ppermute | solution.py:350
  55.7 4.7 %collective-permute-start.5 = (bf16[32,1152]{1,0:T(8,128)(2,1)S(1)}, bf16[32,1152]{1,0:T(8,128)(2,1)S(1)}, u32[]{:S(2)}, u32[]{:S(2)}) collective-permute-start(bf16[32,1152]{1,0:T(8,128)(2,1)S(1)} %get-tuple-element.159), channel_id=1, source_target_pairs={{0,4},{2,6},{4,0},{6,2},{1,5},{3,7},{5,1},{7,3},{8,12},{10,14},{12... | collective-permute-start | bytes 221192 | tf_op jit(solution)/shard_map/ppermute | solution.py:350
  60.5 3.8 %collective-permute-start.7 = (bf16[112,1152]{1,0:T(8,128)(2,1)S(1)}, bf16[112,1152]{1,0:T(8,128)(2,1)S(1)}, u32[]{:S(2)}, u32[]{:S(2)}) collective-permute-start(bf16[112,1152]{1,0:T(8,128)(2,1)S(1)} %constant_dynamic-update-slice_fusion.own_tail_ref), channel_id=1, source_target_pairs={{0,1},{1,0},{2,3},{3,2},{4,5},{5,4},{6,7},{7,6},{8,9},{9,8},{10,11... | collective-permute-start | bytes 774152 | tf_op jit(solution)/shard_map/ppermute | solution.py:353
  71.5 10.2 %collective-permute-start.8 = (bf16[320,1152]{1,0:T(8,128)(2,1)S(1)}, bf16[320,1152]{1,0:T(8,128)(2,1)S(1)}, u32[]{:S(2)}, u32[]{:S(2)}) collective-permute-start(bf16[320,1152]{1,0:T(8,128)(2,1)S(1)} %pad_maximum_fusion), channel_id=1, source_target_pairs={{0,1},{1,0},{2,3},{3,2},{4,5},{5,4},{6,7},{7,6},{8,9},{9,8},{10,11... | collective-permute-start | bytes 2211848 | tf_op jit(solution)/shard_map/ppermute | solution.py:365
  73.1 16.2 %all-to-all-start.5 = ((f32[64,4,128]{2,1,0:T(4,128)}), f32[64,4,128]{2,1,0:T(4,128)S(1)}, u32[]{:S(2)}, u32[]{:S(2)}) async-start(f32[64,4,128]{2,1,0:T(4,128)} %shard_map.41), calls=%async_computation.5 | async-start | bytes 262144 | tf_op jit(solution)/shard_map/all_to_all | solution.py:366
  81.8 1.8 %copy-start = (bf16[1280,1152]{1,0:T(8,128)(2,1)S(1)}, bf16[1280,1152]{1,0:T(8,128)(2,1)}, u32[]{:S(2)}) copy-start(bf16[1280,1152]{1,0:T(8,128)(2,1)} %all-gather.7.cloned.1.call-done.keys_ref) | copy-start | bytes 8847364
  83.6 15.1 %copy-start.3 = (s32[512]{0:T(512)S(1)}, s32[512]{0:T(512)}, u32[]{:S(2)}) copy-start(s32[512]{0:T(512)} %param.8) | copy-start | bytes 6148
  89.3 2.4 %collective-permute-start.9 = (f32[4,128]{1,0:T(4,128)S(1)}, f32[4,128]{1,0:T(4,128)S(1)}, u32[]{:S(2)}, u32[]{:S(2)}) collective-permute-start(f32[4,128]{1,0:T(4,128)S(1)} %slice.40), channel_id=1, source_target_pairs={{0,1},{1,0},{2,3},{3,2},{4,5},{5,4},{6,7},{7,6},{8,9},{9,8},{10,11... | collective-permute-start | bytes 6152 | tf_op jit(solution)/shard_map/ppermute | solution.py:376
  91.7 2.4 %collective-permute-start.12 = (f32[1,128]{1,0:T(1,128)S(1)}, f32[1,128]{1,0:T(1,128)S(1)}, u32[]{:S(2)}, u32[]{:S(2)}) collective-permute-start(f32[1,128]{1,0:T(1,128)S(1)} %get-tuple-element.162), channel_id=1, source_target_pairs={{0,6},{2,0},{4,2},{6,4},{1,7},{3,1},{5,3},{7,5},{8,14},{10,8},{12,... | collective-permute-start | bytes 1544 | tf_op jit(solution)/shard_map/ppermute | solution.py:377
  92.7 3.9 %collective-permute-start.11 = (f32[1,128]{1,0:T(1,128)S(1)}, f32[1,128]{1,0:T(1,128)S(1)}, u32[]{:S(2)}, u32[]{:S(2)}) collective-permute-start(f32[1,128]{1,0:T(1,128)S(1)} %get-tuple-element.163), channel_id=1, source_target_pairs={{0,4},{2,6},{4,0},{6,2},{1,5},{3,7},{5,1},{7,3},{8,12},{10,14},{12... | collective-permute-start | bytes 1544 | tf_op jit(solution)/shard_map/ppermute | solution.py:377
  93.8 3.6 %collective-permute-start.10 = (f32[1,128]{1,0:T(1,128)S(1)}, f32[1,128]{1,0:T(1,128)S(1)}, u32[]{:S(2)}, u32[]{:S(2)}) collective-permute-start(f32[1,128]{1,0:T(1,128)S(1)} %get-tuple-element.164), channel_id=1, source_target_pairs={{0,2},{2,4},{4,6},{6,0},{1,3},{3,5},{5,7},{7,1},{8,10},{10,12},{12... | collective-permute-start | bytes 1544 | tf_op jit(solution)/shard_map/ppermute | solution.py:377
  99.0 0.6 copy-start.4
Sparse Core Ops, SparseCore 0:
  11.8 65.7 all-gather.6

commit v3 on v2

--- a/solution.py
+++ b/solution.py
@@ -21,7 +21,7 @@
 EXTRA = CHIPS * 4
 FLAG_ROWS = 16
 TAIL = 3 * FIX + FLAG_ROWS
-OWN = SLOTS + EXTRA + TAIL
+MAIN = SLOTS + EXTRA
 LOW = -1e30
 BAD = 4.0
 FIELDS = 16
@@ -70,20 +70,11 @@
     copies = [pltpu.make_async_copy(src, dst, sems.at[k]) for k, (src, dst) in enumerate(pairs)]
     for copy in copies:
         copy.start()
-    for copy in copies:
-        copy.wait()
-    emb = emb_ref[...]
+    copies[0].wait()
+    copies[1].wait()
     cl = cl_ref[...]
     order = ord_ref[...]
-    rows = emb.shape[0]
-    wide = emb.astype(f32)
-    square = wide * wide
-    square_high = square.astype(bf16)
-    square_low = (square - square_high.astype(f32)).astype(bf16)
-    ones = jnp.ones((8, emb.shape[1]), bf16)
-    total = (mm_t(ones, square_high) + mm_t(ones, square_low))[0:1, :] + 1e-06
-    inv = lax.rsqrt(total)
-    inv = inv * (1.5 - 0.5 * total * inv * inv)
+    rows = emb_ref.shape[0]
     owner = cl >> 5
     local_cluster = cl & (CL_OWN - 1)
     bins = bin_of(local_cluster)
@@ -122,6 +113,16 @@
     most = jnp.max(jnp.where(full > 0.5, 0.0, owner_count), axis=0, keepdims=True)
     flag = (jnp.sum(full, axis=0, keepdims=True) != 1.0) | (most > BINS * PLACES)
     flag_ref[...] = jnp.broadcast_to(jnp.where(flag, 1.0, 0.0), flag_ref.shape)
+    copies[2].wait()
+    emb = emb_ref[...]
+    wide = emb.astype(f32)
+    square = wide * wide
+    square_high = square.astype(bf16)
+    square_low = (square - square_high.astype(f32)).astype(bf16)
+    ones = jnp.ones((8, emb.shape[1]), bf16)
+    total = (mm_t(ones, square_high) + mm_t(ones, square_low))[0:1, :] + 1e-06
+    inv = lax.rsqrt(total)
+    inv = inv * (1.5 - 0.5 * total * inv * inv)
     high, middle, low = pieces(inv)
     at = iota((1, rows), 1)
     fields = [
@@ -159,6 +160,11 @@
     out_ref[:, :, FEAT + half :] = beside.astype(bf16).reshape(CHIPS, 8, META)
 
 
+def shifted(step):
+    lanes = iota((META, META), 1)
+    return hot((iota((META, META), 0) == lanes + step) & (lanes < FIELDS))
+
+
 def fix_kernel(y_ref, flag_in_ref, in_ref, fix_ref, flag_ref):
     half = FEAT // 2
     meta = in_ref[:, :, FEAT + half :].reshape(SLOTS, META)
@@ -193,9 +199,7 @@
     taken = mm(pick, whole)
     fix_ref[:, :half] = (taken[:, :half] + mm(pick_first, halves)).astype(bf16)
     fix_ref[:, half:FEAT] = (taken[:, half:] + mm(pick_second, halves)).astype(bf16)
-    back = hot((iota((META, META), 0) == iota((META, META), 1) + FIELDS) & (iota((META, META), 1) < FIELDS))
-    keep = hot((iota((META, META), 0) == iota((META, META), 1)) & (iota((META, META), 1) < FIELDS))
-    beside = mm(mm(pick, meta).astype(bf16), keep) + mm(mm(pick_first, meta).astype(bf16), back)
+    beside = mm(mm(pick, meta).astype(bf16), shifted(0)) + mm(mm(pick_first, meta).astype(bf16), shifted(FIELDS))
     fix_ref[:, FEAT:] = beside.astype(bf16)
     step_row = iota((8, 1), 0)
     too_many = jnp.max(jnp.where((step_row > 0) & (count > FIX), 1.0, 0.0), axis=0, keepdims=True)
@@ -231,39 +235,60 @@
     return jnp.maximum(best * query_inv, -1.0)
 
 
-def owned_kernel(own_ref, other_ref, own_tail_ref, other_tail_ref, out_ref, keys, metas):
-    half = FEAT // 2
+def selections():
     source = iota((EXTRA, SLOTS), 1)
     wanted = iota((EXTRA, SLOTS), 0)
-    first = hot(source == (wanted >> 2) * 8 + (wanted & 3))
-    second = hot(source == (wanted >> 2) * 8 + (wanted & 3) + 4)
-    back = hot((iota((META, META), 0) == iota((META, META), 1) + FIELDS) & (iota((META, META), 1) < FIELDS))
-    for ref, tail, base in ((own_ref, own_tail_ref, 0), (other_ref, other_tail_ref, OWN)):
-        at = slice(base, base + SLOTS)
-        keys[at, :] = ref[:, :, :FEAT].reshape(SLOTS, FEAT)
-        meta = ref[:, :, FEAT + half :].reshape(SLOTS, META)
-        metas[at, :] = meta
-        at = slice(base + SLOTS, base + SLOTS + EXTRA)
-        halves = ref[:, :, FEAT : FEAT + half].reshape(SLOTS, half)
-        keys[at, :half] = mm(first, halves).astype(bf16)
-        keys[at, half:] = mm(second, halves).astype(bf16)
-        metas[at, :] = mm(mm(first, meta).astype(bf16), back).astype(bf16)
-        at = slice(base + SLOTS + EXTRA, base + OWN)
-        keys[at, :] = tail[:, :FEAT]
-        metas[at, :] = tail[:, FEAT:]
-    fields = query_rows(metas[:OWN, :])
-    best = best_over_keys(keys, metas, keys[:OWN, :], fields, 4)
-    from_chip = jnp.where((iota((CHIPS, OWN), 0).astype(f32) == fields[7:8]) & (fields[6:7] > 0.5), 1.0, 0.0)
+    at = (wanted >> 2) * 8 + (wanted & 3)
+    return hot(source == at), hot(source == at + 4)
+
+
+def spread_out(best, fields, metas):
+    rows = best.shape[1]
+    from_chip = jnp.where((iota((CHIPS, rows), 0).astype(f32) == fields[7:8]) & (fields[6:7] > 0.5), 1.0, 0.0)
     high, middle, low = pieces(best)
     left = jnp.concatenate(
         [from_chip, from_chip * high.astype(f32), from_chip * middle.astype(f32), from_chip * low.astype(f32)], axis=0
     ).astype(bf16)
-    wide = metas[:OWN, :].astype(f32)
+    wide = metas.astype(f32)
     place = wide[:, 8:9] * 256.0 + wide[:, 9:10]
-    right = hot(iota((OWN, ROW_DEV), 1).astype(f32) == place)
+    right = hot(iota((rows, ROW_DEV), 1).astype(f32) == place)
     spread = mm(left, right)
     value = spread[CHIPS : 2 * CHIPS] + spread[2 * CHIPS : 3 * CHIPS] + spread[3 * CHIPS :]
-    out = jnp.where(spread[:CHIPS] > 0.5, value, -1.0)
+    return jnp.where(spread[:CHIPS] > 0.5, value, -1.0)
+
+
+def main_kernel(own_ref, other_ref, keys_ref, metas_ref, best_ref):
+    half = FEAT // 2
+    first, second = selections()
+    for k, ref in enumerate((own_ref, other_ref)):
+        at = slice(k * MAIN, k * MAIN + SLOTS)
+        keys_ref[at, :] = ref[:, :, :FEAT].reshape(SLOTS, FEAT)
+        meta = ref[:, :, FEAT + half :].reshape(SLOTS, META)
+        metas_ref[at, :] = meta
+        at = slice(k * MAIN + SLOTS, (k + 1) * MAIN)
+        halves = ref[:, :, FEAT : FEAT + half].reshape(SLOTS, half)
+        keys_ref[at, :half] = mm(first, halves).astype(bf16)
+        keys_ref[at, half:] = mm(second, halves).astype(bf16)
+        metas_ref[at, :] = mm(mm(first, meta).astype(bf16), shifted(FIELDS)).astype(bf16)
+    fields = query_rows(metas_ref[:MAIN, :])
+    best = best_over_keys(keys_ref, metas_ref, keys_ref[:MAIN, :], fields, 4)
+    best_ref[...] = jnp.broadcast_to(best, best_ref.shape)
+
+
+def tail_kernel(keys_ref, metas_ref, best_ref, own_tail_ref, other_tail_ref, out_ref):
+    metas = metas_ref[:MAIN, :]
+    fields = query_rows(metas)
+    best = best_ref[0:1, :]
+    for tail in (own_tail_ref, other_tail_ref):
+        best = jnp.maximum(best, best_over_keys(tail.at[:, :FEAT], tail.at[:, FEAT:], keys_ref[:MAIN, :], fields, 1))
+    out = spread_out(best, fields, metas)
+    metas = own_tail_ref[:, FEAT:]
+    fields = query_rows(metas)
+    queries = own_tail_ref[:, :FEAT]
+    best = best_over_keys(keys_ref, metas_ref, queries, fields, 2)
+    for tail in (own_tail_ref, other_tail_ref):
+        best = jnp.maximum(best, best_over_keys(tail.at[:, :FEAT], tail.at[:, FEAT:], queries, fields, 1))
+    out = jnp.maximum(out, spread_out(best, fields, metas))
     at = slice(3 * FIX, 3 * FIX + 1), slice(FEAT + 10, FEAT + 11)
     flag = jnp.maximum(own_tail_ref[at].astype(f32), other_tail_ref[at].astype(f32))
     out = jnp.where(flag > 0.5, BAD, out)
@@ -329,6 +354,7 @@
             pltpu.VMEM((1, ROW_DEV), i32),
             pltpu.SemaphoreType.DMA((3,)),
         ),
+        vmem=58,
         flops=2 * 700_000_000,
         bytes_accessed=3_000_000,
     )
@@ -336,6 +362,7 @@
     inbox = lax.all_to_all(outbox, CHIP_AXES, split_axis=0, concat_axis=0, tiled=True)
     swap = [(0, 1), (1, 0)]
     along = [box] + [lax.ppermute(box, "y", [(i, (i - d) % 4) for i in range(4)]) for d in (1, 2, 3)]
+    inbox, *along = lax.optimization_barrier((inbox, *along))
     other = lax.ppermute(inbox, "core", swap)
     fix, flag_block = call(
         fix_kernel,
@@ -345,19 +372,26 @@
         flops=2 * 100_000_000,
         bytes_accessed=2_000_000,
     )
-    fix, *along = lax.optimization_barrier((fix, *along))
+    keys, metas, best = call(
+        main_kernel,
+        (shape((2 * MAIN, FEAT), bf16), shape((2 * MAIN, META), bf16), shape((8, MAIN), f32)),
+        (inbox, other),
+        (VMEM, VMEM),
+        flops=2 * 1_400_000_000,
+        bytes_accessed=7_000_000,
+    )
     got = [
         lax.ppermute(fix[(d - 1) * FIX : d * FIX], "y", [(i, (i + d) % 4) for i in range(4)]) for d in (1, 2, 3)
     ]
+    best, *got = lax.optimization_barrier((best, *got))
     tail = jnp.concatenate(got + [flag_block], axis=0)
     other_tail = lax.ppermute(tail, "core", swap)
     spread = call(
-        owned_kernel,
+        tail_kernel,
         shape((CHIPS, ROW_DEV // META, META), f32),
-        (inbox, other, tail, other_tail),
-        (VMEM, VMEM, VMEM, VMEM),
-        scratch=(pltpu.VMEM((2 * OWN, FEAT), bf16), pltpu.VMEM((2 * OWN, META), bf16)),
-        flops=2 * 1_600_000_000,
+        (keys, metas, best, tail, other_tail),
+        (VMEM, VMEM, VMEM, VMEM, VMEM),
+        flops=2 * 500_000_000,
         bytes_accessed=4_000_000,
     )
     spread, *along = lax.optimization_barrier((spread, *along))

time: 108 us -> 104 us (0.963)
  starting transfers between devices: 37.4 us -> 34.7 us
    ppermute x3, waiting for transfers between devices: 0.01 us -> 23 us  [fast(): lax.ppermute(box, 'y', [(i, (i - d) % 4) for i in range(4)])]
    all_to_all x1, waiting for transfers between devices: 20.5 us -> 0.01 us  [fast(): lax.all_to_all(outbox, CHIP_AXES, split_axis=0, concat_axis=0, tiled=True)]
    ppermute x3, waiting for transfers between devices: 4.33 us -> 1.08 us  [fast(): lax.ppermute(fix[(d - 1) * FIX:d * FIX], 'y', [(i, (i + d) % 4) for i in...]
    all_to_all x1, starting transfers between devices: 7.57 us -> 9.17 us  [fast(): lax.all_to_all(spread, CHIP_AXES, split_axis=0, concat_axis=0, tiled=True)]
    ppermute x1, starting transfers between devices: 2.67 us -> 1.1 us  [fast(): other_tail = lax.ppermute(tail, 'core', swap)]
    ppermute x3, starting transfers between devices: 3.12 us -> 1.72 us  [fast(): lax.ppermute(fix[(d - 1) * FIX:d * FIX], 'y', [(i, (i + d) % 4) for i in...]
    ppermute x1, starting transfers between devices: 3.11 us -> 1.82 us  [fast(): other = lax.ppermute(inbox, 'core', swap)]
    pallas_call x5 -> x6, Pallas kernels: 15.1 us -> 15.9 us  [call(): pl.pallas_call(kernel, out_shape=shapes, in_specs=[pl.BlockSpec(memory_sp...]
  transfers between devices with their start and end apart: 16 -> 16, of which waited for: 9 -> 10; matrix products, arithmetic and copies ran while one was open for 3% -> 2% of each run, Pallas kernels for 9% -> 11%
where the time goes in v3:
time: 104 us; the launch traced here: 103 us
  starting transfers between devices  34.7 us (33%)
  waiting for transfers between devices  33 us (32%)
  Pallas kernels  15.9 us (15%)
  between operations  14.3 us (14%)
  local copies, waits for them, and re-layouts  5.03 us (5%)
    ppermute x3, waiting for transfers between devices, fast(): lax.ppermute(box, 'y', [(i, (i - d) % 4) for i in range(4)])  23 us
    pallas_call x6, Pallas kernels, call(): pl.pallas_call(kernel, out_shape=shapes, in_specs=[pl.BlockSpec(memory_sp...  15.9 us
    all_to_all x1, starting transfers between devices, fast(): lax.all_to_all(outbox, CHIP_AXES, split_axis=0, concat_axis=0, tiled=True)  12.1 us
    all_to_all x1, starting transfers between devices, fast(): lax.all_to_all(spread, CHIP_AXES, split_axis=0, concat_axis=0, tiled=True)  9.17 us
    ppermute x3, starting transfers between devices, fast(): lax.ppermute(box, 'y', [(i, (i - d) % 4) for i in range(4)])  4.66 us
    unnamed x23, local copies, waits for them, and re-layouts  4.38 us
    ppermute x3, waiting for transfers between devices, fast(): lax.ppermute(both[d:d + 1], 'y', [(i, (i + d) % 4) for i in range(4)])  3.6 us
    all_to_all x1, waiting for transfers between devices, fast(): lax.all_to_all(spread, CHIP_AXES, split_axis=0, concat_axis=0, tiled=True)  2.11 us
  transfers between devices with their start and end apart: 16, of which 10 were waited for; matrix products, arithmetic and copies ran while one was open for 2% of the time, Pallas kernels for 11%

profile of v3, /device:TPU:1, one launch (start us, length us, event | category | flops | bytes accessed | tf_op | source)
XLA Modules:
  0.0 102.9 jit_solution(9808551167554473512)
XLA Ops:
  6.5 4.8 %shard_map.39 = (bf16[64,8,1664]{2,1,0:T(8,128)(2,1)}, bf16[80,1152]{1,0:T(8,128)(2,1)}, s32[1,512]{1,0:T(1,128)}, f32[8,128]{1,0:T(8,128)}) custom-call(s32[1]{0:T(128)} %bitcast.7.chip_ref, bf16[512,1024]{1,0:T(8,128)(2,1)} %emb_hbm.1, s32[1,512]{1,0:T(1,128)} %bitcast.71, s32[1,512]{1,0:T(1,128)} %bitcast.72), custom_call_target="tpu_custom_call" | custom-call | flops 1400000000 | bytes 3000000 | tf_op jit(solution)/shard_map/pallas_call | solution.py:323
  11.4 0.0 copy-start.4
  11.4 0.0 copy-start
  11.4 12.1 %all-to-all-start.4 = ((bf16[64,8,1664]{2,1,0:T(8,128)(2,1)}), bf16[64,8,1664]{2,1,0:T(8,128)(2,1)S(1)}, u32[]{:S(2)}, u32[]{:S(2)}) async-start(bf16[64,8,1664]{2,1,0:T(8,128)(2,1)} %get-tuple-element.95), calls=%async_computation.4 | async-start | bytes 3407872 | tf_op jit(solution)/shard_map/all_to_all | solution.py:362
  23.5 0.0 all-gather.7.cloned.1.call-start
  23.6 0.7 all-gather.7.cloned.1.call-update
  24.3 0.0 copy-done.4
  24.3 1.1 %collective-permute-start.2 = (bf16[80,1152]{1,0:T(8,128)(2,1)S(1)}, bf16[80,1152]{1,0:T(8,128)(2,1)S(1)}, u32[]{:S(2)}, u32[]{:S(2)}) collective-permute-start(bf16[80,1152]{1,0:T(8,128)(2,1)S(1)} %copy-done.4), channel_id=1, source_target_pairs={{0,2},{2,4},{4,6},{6,0},{1,3},{3,5},{5,7},{7,1},{8,10},{10,12},{12... | collective-permute-start | bytes 552968 | tf_op jit(solution)/shard_map/ppermute | solution.py:364
  25.4 2.4 %collective-permute-start.1 = (bf16[80,1152]{1,0:T(8,128)(2,1)S(1)}, bf16[80,1152]{1,0:T(8,128)(2,1)S(1)}, u32[]{:S(2)}, u32[]{:S(2)}) collective-permute-start(bf16[80,1152]{1,0:T(8,128)(2,1)S(1)} %copy-done.4), channel_id=1, source_target_pairs={{0,4},{2,6},{4,0},{6,2},{1,5},{3,7},{5,1},{7,3},{8,12},{10,14},{12... | collective-permute-start | bytes 552968 | tf_op jit(solution)/shard_map/ppermute | solution.py:364
  27.7 1.2 %collective-permute-start = (bf16[80,1152]{1,0:T(8,128)(2,1)S(1)}, bf16[80,1152]{1,0:T(8,128)(2,1)S(1)}, u32[]{:S(2)}, u32[]{:S(2)}) collective-permute-start(bf16[80,1152]{1,0:T(8,128)(2,1)S(1)} %copy-done.4), channel_id=1, source_target_pairs={{0,6},{2,0},{4,2},{6,4},{1,7},{3,1},{5,3},{7,5},{8,14},{10,8},{12,... | collective-permute-start | bytes 552968 | tf_op jit(solution)/shard_map/ppermute | solution.py:364
  28.9 19.8 %collective-permute-done.2 = bf16[80,1152]{1,0:T(8,128)(2,1)S(1)} collective-permute-done((bf16[80,1152]{1,0:T(8,128)(2,1)S(1)}, bf16[80,1152]{1,0:T(8,128)(2,1)S(1)}, u32[]{:S(2)}, u32[]{:S(2)}) %collective-permute-start.2) | collective-permute-done | bytes 184352 | tf_op jit(solution)/shard_map/ppermute | solution.py:364
  48.7 3.2 %collective-permute-done.1 = bf16[80,1152]{1,0:T(8,128)(2,1)S(1)} collective-permute-done((bf16[80,1152]{1,0:T(8,128)(2,1)S(1)}, bf16[80,1152]{1,0:T(8,128)(2,1)S(1)}, u32[]{:S(2)}, u32[]{:S(2)}) %collective-permute-start.1) | collective-permute-done | bytes 184352 | tf_op jit(solution)/shard_map/ppermute | solution.py:364
  51.9 0.0 copy-start.5
  51.9 0.0 collective-permute-done
  51.9 0.0 copy-start.6
  52.0 0.0 all-to-all-done.4.own_ref.in_ref
  52.0 1.8 %collective-permute-start.3 = (bf16[64,8,1664]{2,1,0:T(8,128)(2,1)S(1)}, bf16[64,8,1664]{2,1,0:T(8,128)(2,1)S(1)}, u32[]{:S(2)}, u32[]{:S(2)}) collective-permute-start(bf16[64,8,1664]{2,1,0:T(8,128)(2,1)S(1)} %all-to-all-done.4.own_ref.in_ref), channel_id=1, source_target_pairs={{0,1},{1,0},{2,3},{3,2},{4,5},{5,4},{6,7},{7,6},{8,9},{9,8},{10,11... | collective-permute-start | bytes 5111816 | tf_op jit(solution)/shard_map/ppermute | solution.py:366
  53.8 0.0 copy-done
  53.8 1.0 shard_map.41
  54.8 0.1 collective-permute-start.6
  55.0 1.3 %collective-permute-start.5 = (bf16[32,1152]{1,0:T(8,128)(2,1)S(1)}, bf16[32,1152]{1,0:T(8,128)(2,1)S(1)}, u32[]{:S(2)}, u32[]{:S(2)}) collective-permute-start(bf16[32,1152]{1,0:T(8,128)(2,1)S(1)} %get-tuple-element.173), channel_id=1, source_target_pairs={{0,4},{2,6},{4,0},{6,2},{1,5},{3,7},{5,1},{7,3},{8,12},{10,14},{12... | collective-permute-start | bytes 221192 | tf_op jit(solution)/shard_map/ppermute | solution.py:384
  56.3 0.3 collective-permute-start.4
  56.5 0.5 collective-permute-done.3.other_ref
  57.0 3.8 %shard_map.40 = (bf16[1536,1024]{1,0:T(8,128)(2,1)S(1)}, bf16[1536,128]{1,0:T(8,128)(2,1)S(1)}, f32[8,768]{1,0:T(8,128)S(1)}) custom-call(bf16[64,8,1664]{2,1,0:T(8,128)(2,1)S(1)} %all-to-all-done.4.own_ref.in_ref, bf16[64,8,1664]{2,1,0:T(8,128)(2,1)S(1)} %collective-permute-done.3.other_ref), custom_call_target="tpu_custom_call" | custom-call | flops 2800000000 | bytes 7000000 | tf_op jit(solution)/shard_map/pallas_call | solution.py:323
  60.8 0.0 collective-permute-done.6
  60.8 0.0 collective-permute-done.5
  60.8 1.1 %collective-permute-done.4 = bf16[32,1152]{1,0:T(8,128)(2,1)S(1)} collective-permute-done((bf16[32,1152]{1,0:T(8,128)(2,1)S(1)}, bf16[32,1152]{1,0:T(8,128)(2,1)S(1)}, u32[]{:S(2)}, u32[]{:S(2)}) %collective-permute-start.4) | collective-permute-done | bytes 73760 | tf_op jit(solution)/shard_map/ppermute | solution.py:384
  62.0 1.1 %collective-permute-start.7 = (bf16[112,1152]{1,0:T(8,128)(2,1)S(1)}, bf16[112,1152]{1,0:T(8,128)(2,1)S(1)}, u32[]{:S(2)}, u32[]{:S(2)}) collective-permute-start(bf16[112,1152]{1,0:T(8,128)(2,1)S(1)} %constant_dynamic-update-slice_fusion.own_tail_ref), channel_id=1, source_target_pairs={{0,1},{1,0},{2,3},{3,2},{4,5},{5,4},{6,7},{7,6},{8,9},{9,8},{10,11... | collective-permute-start | bytes 774152 | tf_op jit(solution)/shard_map/ppermute | solution.py:388
  63.1 1.2 %collective-permute-done.7.other_tail_ref = bf16[112,1152]{1,0:T(8,128)(2,1)S(1)} collective-permute-done((bf16[112,1152]{1,0:T(8,128)(2,1)S(1)}, bf16[112,1152]{1,0:T(8,128)(2,1)S(1)}, u32[]{:S(2)}, u32[]{:S(2)}) %collective-permute-start.7) | collective-permute-done | bytes 258080 | tf_op jit(solution)/shard_map/ppermute | solution.py:388
  64.2 3.4 %shard_map.42 = f32[64,4,128]{2,1,0:T(4,128)} custom-call(bf16[1536,1024]{1,0:T(8,128)(2,1)S(1)} %get-tuple-element.97.keys_ref, bf16[1536,128]{1,0:T(8,128)(2,1)S(1)} %get-tuple-element.98.metas_ref, f32[8,768]{1,0:T(8,128)S(1)} %get-tuple-element.102.best_ref, bf16[112,1152]{1,0:T(8,128)(2,1)S(1)} %constant_dynamic-update-slice_fusion.own_tail_ref, ...), custom_call_target="tpu_custom_call" | custom-call | flops 1000000000 | bytes 4000000 | tf_op jit(solution)/shard_map/pallas_call | solution.py:323
  67.7 0.0 copy-done.5
  67.7 0.0 copy-done.6
  67.7 0.1 pad_maximum_fusion
  67.7 0.4 collective-permute-start.8
  68.2 9.2 %all-to-all-start.5 = ((f32[64,4,128]{2,1,0:T(4,128)}), f32[64,4,128]{2,1,0:T(4,128)S(1)}, u32[]{:S(2)}, u32[]{:S(2)}) async-start(f32[64,4,128]{2,1,0:T(4,128)} %shard_map.42), calls=%async_computation.5 | async-start | bytes 262144 | tf_op jit(solution)/shard_map/all_to_all | solution.py:400
  77.4 0.9 constant_dynamic-update-slice_fusion.7
  78.3 0.9 constant_dynamic-update-slice_fusion.6
  79.3 0.0 collective-permute-done.8
  79.3 0.1 constant_dynamic-update-slice_fusion.4.queries_ref
  79.4 0.0 copy-start.1
  79.4 0.0 all-gather.7.cloned.1.call-done.keys_ref
  79.4 0.0 copy-start.2
  79.4 1.8 %copy-done.2 = bf16[1280,1152]{1,0:T(8,128)(2,1)S(1)} copy-done((bf16[1280,1152]{1,0:T(8,128)(2,1)S(1)}, bf16[1280,1152]{1,0:T(8,128)(2,1)}, u32[]{:S(2)}) %copy-start.2) | copy-done | bytes 2949144
  81.3 0.0 copy-start.7
  81.3 2.6 %shard_map.43 = f32[8,128]{1,0:T(8,128)S(1)} custom-call(bf16[1280,1152]{1,0:T(8,128)(2,1)S(1)} %copy-done.2, bf16[640,1152]{1,0:T(8,128)(2,1)S(1)} %constant_dynamic-update-slice_fusion.4.queries_ref), custom_call_target="tpu_custom_call" | custom-call | flops 1800000000 | bytes 4500000 | tf_op jit(solution)/shard_map/pallas_call | solution.py:323
  83.9 2.1 %all-to-all-done.5.spread_ref = f32[64,4,128]{2,1,0:T(4,128)S(1)} async-done(((f32[64,4,128]{2,1,0:T(4,128)}), f32[64,4,128]{2,1,0:T(4,128)S(1)}, u32[]{:S(2)}, u32[]{:S(2)}) %all-to-all-start.5) | async-done | bytes 131104 | tf_op jit(solution)/shard_map/all_to_all | solution.py:400
  86.0 1.6 %collective-permute-start.9 = (f32[4,128]{1,0:T(4,128)S(1)}, f32[4,128]{1,0:T(4,128)S(1)}, u32[]{:S(2)}, u32[]{:S(2)}) collective-permute-start(f32[4,128]{1,0:T(4,128)S(1)} %slice.40), channel_id=1, source_target_pairs={{0,1},{1,0},{2,3},{3,2},{4,5},{5,4},{6,7},{7,6},{8,9},{9,8},{10,11... | collective-permute-start | bytes 6152 | tf_op jit(solution)/shard_map/ppermute | solution.py:410
  87.6 0.8 collective-permute-done.9
  88.4 1.0 collective-permute-start.12
  89.4 1.1 %collective-permute-start.11 = (f32[1,128]{1,0:T(1,128)S(1)}, f32[1,128]{1,0:T(1,128)S(1)}, u32[]{:S(2)}, u32[]{:S(2)}) collective-permute-start(f32[1,128]{1,0:T(1,128)S(1)} %get-tuple-element.177), channel_id=1, source_target_pairs={{0,4},{2,6},{4,0},{6,2},{1,5},{3,7},{5,1},{7,3},{8,12},{10,14},{12... | collective-permute-start | bytes 1544 | tf_op jit(solution)/shard_map/ppermute | solution.py:411
  90.5 0.0 collective-permute-start.10
  90.5 0.3 collective-permute-done.12
  90.8 2.5 %collective-permute-done.11 = f32[1,128]{1,0:T(1,128)S(1)} collective-permute-done((f32[1,128]{1,0:T(1,128)S(1)}, f32[1,128]{1,0:T(1,128)S(1)}, u32[]{:S(2)}, u32[]{:S(2)}) %collective-permute-start.11) | collective-permute-done | bytes 544 | tf_op jit(solution)/shard_map/ppermute | solution.py:411
  93.3 0.8 collective-permute-done.10
  94.1 0.0 copy-done.1
  94.1 0.2 shard_map.44
  94.3 0.5 slice.45
  95.4 0.0 copy-done.7
  95.5 0.0 copy-start.8
  95.5 0.6 copy-done.8
  (12 shorter events, 0.1 us)
Async XLA Ops:
  11.4 12.9 %copy-start.4 = (bf16[80,1152]{1,0:T(8,128)(2,1)S(1)}, bf16[80,1152]{1,0:T(8,128)(2,1)}, u32[]{:S(2)}) copy-start(bf16[80,1152]{1,0:T(8,128)(2,1)} %get-tuple-element.111) | copy-start | bytes 552964
  11.4 42.4 %copy-start = (f32[8,128]{1,0:T(8,128)S(1)}, f32[8,128]{1,0:T(8,128)}, u32[]{:S(2)}) copy-start(f32[8,128]{1,0:T(8,128)} %get-tuple-element.100.flag_in_ref) | copy-start | bytes 12292
  11.4 40.5 %all-to-all-start.4 = ((bf16[64,8,1664]{2,1,0:T(8,128)(2,1)}), bf16[64,8,1664]{2,1,0:T(8,128)(2,1)S(1)}, u32[]{:S(2)}, u32[]{:S(2)}) async-start(bf16[64,8,1664]{2,1,0:T(8,128)(2,1)} %get-tuple-element.95), calls=%async_computation.4 | async-start | bytes 3407872 | tf_op jit(solution)/shard_map/all_to_all | solution.py:362
  23.5 55.9 %all-gather.7.cloned.1.call-start = ((), (), s32[]{:S(2)}) async-start(), calls=%async_computation.7 | async-start | bytes 3133440 | tf_op jit(solution)/shard_map/all_gather | solution.py:361
  24.3 24.4 %collective-permute-start.2 = (bf16[80,1152]{1,0:T(8,128)(2,1)S(1)}, bf16[80,1152]{1,0:T(8,128)(2,1)S(1)}, u32[]{:S(2)}, u32[]{:S(2)}) collective-permute-start(bf16[80,1152]{1,0:T(8,128)(2,1)S(1)} %copy-done.4), channel_id=1, source_target_pairs={{0,2},{2,4},{4,6},{6,0},{1,3},{3,5},{5,7},{7,1},{8,10},{10,12},{12... | collective-permute-start | bytes 552968 | tf_op jit(solution)/shard_map/ppermute | solution.py:364
  25.4 26.6 %collective-permute-start.1 = (bf16[80,1152]{1,0:T(8,128)(2,1)S(1)}, bf16[80,1152]{1,0:T(8,128)(2,1)S(1)}, u32[]{:S(2)}, u32[]{:S(2)}) collective-permute-start(bf16[80,1152]{1,0:T(8,128)(2,1)S(1)} %copy-done.4), channel_id=1, source_target_pairs={{0,4},{2,6},{4,0},{6,2},{1,5},{3,7},{5,1},{7,3},{8,12},{10,14},{12... | collective-permute-start | bytes 552968 | tf_op jit(solution)/shard_map/ppermute | solution.py:364
  27.7 24.2 %collective-permute-start = (bf16[80,1152]{1,0:T(8,128)(2,1)S(1)}, bf16[80,1152]{1,0:T(8,128)(2,1)S(1)}, u32[]{:S(2)}, u32[]{:S(2)}) collective-permute-start(bf16[80,1152]{1,0:T(8,128)(2,1)S(1)} %copy-done.4), channel_id=1, source_target_pairs={{0,6},{2,0},{4,2},{6,4},{1,7},{3,1},{5,3},{7,5},{8,14},{10,8},{12,... | collective-permute-start | bytes 552968 | tf_op jit(solution)/shard_map/ppermute | solution.py:364
  51.9 15.7 %copy-start.5 = (bf16[80,1152]{1,0:T(8,128)(2,1)}, bf16[80,1152]{1,0:T(8,128)(2,1)S(1)}, u32[]{:S(2)}) copy-start(bf16[80,1152]{1,0:T(8,128)(2,1)S(1)} %collective-permute-done.1) | copy-start | bytes 552964
  51.9 15.7 %copy-start.6 = (bf16[80,1152]{1,0:T(8,128)(2,1)}, bf16[80,1152]{1,0:T(8,128)(2,1)S(1)}, u32[]{:S(2)}) copy-start(bf16[80,1152]{1,0:T(8,128)(2,1)S(1)} %collective-permute-done) | copy-start | bytes 552964
  52.0 5.0 %collective-permute-start.3 = (bf16[64,8,1664]{2,1,0:T(8,128)(2,1)S(1)}, bf16[64,8,1664]{2,1,0:T(8,128)(2,1)S(1)}, u32[]{:S(2)}, u32[]{:S(2)}) collective-permute-start(bf16[64,8,1664]{2,1,0:T(8,128)(2,1)S(1)} %all-to-all-done.4.own_ref.in_ref), channel_id=1, source_target_pairs={{0,1},{1,0},{2,3},{3,2},{4,5},{5,4},{6,7},{7,6},{8,9},{9,8},{10,11... | collective-permute-start | bytes 5111816 | tf_op jit(solution)/shard_map/ppermute | solution.py:366
  54.8 6.0 %collective-permute-start.6 = (bf16[32,1152]{1,0:T(8,128)(2,1)S(1)}, bf16[32,1152]{1,0:T(8,128)(2,1)S(1)}, u32[]{:S(2)}, u32[]{:S(2)}) collective-permute-start(bf16[32,1152]{1,0:T(8,128)(2,1)S(1)} %get-tuple-element.172), channel_id=1, source_target_pairs={{0,6},{2,0},{4,2},{6,4},{1,7},{3,1},{5,3},{7,5},{8,14},{10,8},{12,... | collective-permute-start | bytes 221192 | tf_op jit(solution)/shard_map/ppermute | solution.py:384
  55.0 5.9 %collective-permute-start.5 = (bf16[32,1152]{1,0:T(8,128)(2,1)S(1)}, bf16[32,1152]{1,0:T(8,128)(2,1)S(1)}, u32[]{:S(2)}, u32[]{:S(2)}) collective-permute-start(bf16[32,1152]{1,0:T(8,128)(2,1)S(1)} %get-tuple-element.173), channel_id=1, source_target_pairs={{0,4},{2,6},{4,0},{6,2},{1,5},{3,7},{5,1},{7,3},{8,12},{10,14},{12... | collective-permute-start | bytes 221192 | tf_op jit(solution)/shard_map/ppermute | solution.py:384
  56.3 5.6 %collective-permute-start.4 = (bf16[32,1152]{1,0:T(8,128)(2,1)S(1)}, bf16[32,1152]{1,0:T(8,128)(2,1)S(1)}, u32[]{:S(2)}, u32[]{:S(2)}) collective-permute-start(bf16[32,1152]{1,0:T(8,128)(2,1)S(1)} %get-tuple-element.174), channel_id=1, source_target_pairs={{0,2},{2,4},{4,6},{6,0},{1,3},{3,5},{5,7},{7,1},{8,10},{10,12},{12... | collective-permute-start | bytes 221192 | tf_op jit(solution)/shard_map/ppermute | solution.py:384
  62.0 2.3 %collective-permute-start.7 = (bf16[112,1152]{1,0:T(8,128)(2,1)S(1)}, bf16[112,1152]{1,0:T(8,128)(2,1)S(1)}, u32[]{:S(2)}, u32[]{:S(2)}) collective-permute-start(bf16[112,1152]{1,0:T(8,128)(2,1)S(1)} %constant_dynamic-update-slice_fusion.own_tail_ref), channel_id=1, source_target_pairs={{0,1},{1,0},{2,3},{3,2},{4,5},{5,4},{6,7},{7,6},{8,9},{9,8},{10,11... | collective-permute-start | bytes 774152 | tf_op jit(solution)/shard_map/ppermute | solution.py:388
  67.7 11.6 %collective-permute-start.8 = (bf16[320,1152]{1,0:T(8,128)(2,1)S(1)}, bf16[320,1152]{1,0:T(8,128)(2,1)S(1)}, u32[]{:S(2)}, u32[]{:S(2)}) collective-permute-start(bf16[320,1152]{1,0:T(8,128)(2,1)S(1)} %pad_maximum_fusion), channel_id=1, source_target_pairs={{0,1},{1,0},{2,3},{3,2},{4,5},{5,4},{6,7},{7,6},{8,9},{9,8},{10,11... | collective-permute-start | bytes 2211848 | tf_op jit(solution)/shard_map/ppermute | solution.py:399
  68.2 17.8 %all-to-all-start.5 = ((f32[64,4,128]{2,1,0:T(4,128)}), f32[64,4,128]{2,1,0:T(4,128)S(1)}, u32[]{:S(2)}, u32[]{:S(2)}) async-start(f32[64,4,128]{2,1,0:T(4,128)} %shard_map.42), calls=%async_computation.5 | async-start | bytes 262144 | tf_op jit(solution)/shard_map/all_to_all | solution.py:400
  79.4 14.7 %copy-start.1 = (s32[1,512]{1,0:T(1,128)S(1)}, s32[1,512]{1,0:T(1,128)}, u32[]{:S(2)}) copy-start(s32[1,512]{1,0:T(1,128)} %get-tuple-element.118.rank_ref) | copy-start | bytes 6148
  79.4 1.8 %copy-start.2 = (bf16[1280,1152]{1,0:T(8,128)(2,1)S(1)}, bf16[1280,1152]{1,0:T(8,128)(2,1)}, u32[]{:S(2)}) copy-start(bf16[1280,1152]{1,0:T(8,128)(2,1)} %all-gather.7.cloned.1.call-done.keys_ref) | copy-start | bytes 8847364
  81.3 14.2 %copy-start.7 = (s32[512]{0:T(512)S(1)}, s32[512]{0:T(512)}, u32[]{:S(2)}) copy-start(s32[512]{0:T(512)} %param.8) | copy-start | bytes 6148
  86.0 2.4 %collective-permute-start.9 = (f32[4,128]{1,0:T(4,128)S(1)}, f32[4,128]{1,0:T(4,128)S(1)}, u32[]{:S(2)}, u32[]{:S(2)}) collective-permute-start(f32[4,128]{1,0:T(4,128)S(1)} %slice.40), channel_id=1, source_target_pairs={{0,1},{1,0},{2,3},{3,2},{4,5},{5,4},{6,7},{7,6},{8,9},{9,8},{10,11... | collective-permute-start | bytes 6152 | tf_op jit(solution)/shard_map/ppermute | solution.py:410
  88.4 2.4 %collective-permute-start.12 = (f32[1,128]{1,0:T(1,128)S(1)}, f32[1,128]{1,0:T(1,128)S(1)}, u32[]{:S(2)}, u32[]{:S(2)}) collective-permute-start(f32[1,128]{1,0:T(1,128)S(1)} %get-tuple-element.176), channel_id=1, source_target_pairs={{0,6},{2,0},{4,2},{6,4},{1,7},{3,1},{5,3},{7,5},{8,14},{10,8},{12,... | collective-permute-start | bytes 1544 | tf_op jit(solution)/shard_map/ppermute | solution.py:411
  89.4 3.9 %collective-permute-start.11 = (f32[1,128]{1,0:T(1,128)S(1)}, f32[1,128]{1,0:T(1,128)S(1)}, u32[]{:S(2)}, u32[]{:S(2)}) collective-permute-start(f32[1,128]{1,0:T(1,128)S(1)} %get-tuple-element.177), channel_id=1, source_target_pairs={{0,4},{2,6},{4,0},{6,2},{1,5},{3,7},{5,1},{7,3},{8,12},{10,14},{12... | collective-permute-start | bytes 1544 | tf_op jit(solution)/shard_map/ppermute | solution.py:411
  90.5 3.6 %collective-permute-start.10 = (f32[1,128]{1,0:T(1,128)S(1)}, f32[1,128]{1,0:T(1,128)S(1)}, u32[]{:S(2)}, u32[]{:S(2)}) collective-permute-start(f32[1,128]{1,0:T(1,128)S(1)} %get-tuple-element.178), channel_id=1, source_target_pairs={{0,2},{2,4},{4,6},{6,0},{1,3},{3,5},{5,7},{7,1},{8,10},{10,12},{12... | collective-permute-start | bytes 1544 | tf_op jit(solution)/shard_map/ppermute | solution.py:411
  95.5 0.6 copy-start.8
Sparse Core Ops, SparseCore 0:
  26.6 52.3 all-gather.6

commit v4 on v3

--- a/solution.py
+++ b/solution.py
@@ -1,5 +1,6 @@
 import jax
 import jax.numpy as jnp
+import numpy as np
 from jax import lax
 from jax.experimental import pallas as pl
 from jax.experimental.pallas import tpu as pltpu
@@ -15,7 +16,10 @@
 PLACES = 12
 FIX = 32
 META = 128
-WIDE = FEAT + FEAT // 2 + META
+HALF = FEAT // 2
+META_AT = FEAT + HALF
+BUSY_AT = META_AT + META
+WIDE = BUSY_AT + FEAT + HALF
 NARROW = FEAT + META
 SLOTS = CHIPS * 8
 EXTRA = CHIPS * 4
@@ -26,6 +30,66 @@
 BAD = 4.0
 FIELDS = 16
 
+BLOCKS = (
+    (1, 11, 12, 21, 32, 33, 43, 51, 58, 69, 70),
+    (0, 11, 12, 13, 14, 15, 16, 17, 18, 19, 20),
+    (10, 11, 12, 30, 31, 40, 41, 48, 54, 60, 61, 71),
+    (5, 6, 11, 12, 25, 26, 42, 45, 56, 59, 75, 76),
+    (3, 4, 11, 12, 23, 24, 38, 39, 50, 52, 62, 77),
+    (9, 11, 12, 28, 29, 36, 37, 44, 57, 63, 64, 72),
+    (7, 8, 11, 12, 27, 34, 49, 53, 67, 68, 73, 74),
+    (2, 11, 12, 22, 35, 46, 47, 55, 65, 66, 78, 79),
+    (0, 1, 2, 3, 4, 5, 6, 7, 8, 9, 10, 41),
+    (1, 20, 30, 31, 41, 42, 50, 57, 67, 68, 78, 79),
+    (1, 16, 25, 26, 36, 37, 46, 47, 54, 62, 73, 74),
+    (1, 14, 15, 23, 24, 35, 45, 53, 60, 61, 72, 76),
+    (1, 19, 28, 29, 40, 41, 49, 56, 65, 66, 77),
+    (1, 17, 18, 27, 38, 39, 48, 55, 63, 64, 75, 76),
+    (1, 13, 22, 34, 44, 52, 59, 71),
+    (0, 69, 70, 71, 72, 73, 74, 75, 76, 77, 78, 79),
+    (10, 20, 28, 29, 38, 39, 46, 47, 53, 59, 69, 70),
+    (5, 6, 16, 30, 31, 35, 49, 52, 63, 64, 69, 70),
+    (3, 4, 14, 15, 27, 42, 44, 54, 65, 66, 69, 70),
+    (9, 19, 25, 26, 34, 41, 50, 55, 60, 61, 69, 70),
+    (7, 8, 17, 18, 22, 40, 41, 45, 57, 62, 69, 70),
+    (2, 13, 23, 24, 36, 37, 48, 56, 67, 68, 69, 70),
+    (0, 43, 44, 45, 46, 47, 48, 49, 50, 76),
+    (9, 20, 27, 35, 43, 56, 62, 71),
+    (10, 16, 23, 24, 34, 40, 43, 57, 65, 66, 75, 76),
+    (7, 8, 14, 15, 30, 31, 36, 37, 43, 55, 59, 77),
+    (5, 6, 19, 22, 38, 39, 43, 54, 67, 68, 72),
+    (2, 17, 18, 28, 29, 42, 43, 52, 60, 61, 73, 74),
+    (3, 4, 13, 25, 26, 40, 43, 53, 63, 64, 78, 79),
+    (0, 32, 33, 34, 35, 36, 37, 38, 39, 40, 41, 42),
+    (7, 8, 20, 25, 26, 32, 33, 48, 52, 65, 66, 72),
+    (3, 4, 16, 28, 29, 32, 33, 45, 55, 67, 68, 71),
+    (10, 14, 15, 22, 32, 33, 50, 56, 63, 64, 73, 74),
+    (2, 19, 30, 31, 32, 33, 41, 44, 53, 62, 75, 76),
+    (9, 17, 18, 23, 24, 32, 33, 49, 54, 59, 78, 79),
+    (5, 6, 13, 27, 32, 33, 46, 47, 57, 60, 61, 77),
+    (0, 58, 59, 60, 61, 62, 63, 64, 65, 66, 67, 68),
+    (5, 6, 20, 23, 24, 40, 41, 44, 55, 58, 73, 74),
+    (9, 16, 22, 42, 48, 53, 58, 77),
+    (2, 14, 15, 25, 26, 38, 39, 49, 57, 58, 71),
+    (10, 19, 27, 36, 37, 45, 52, 58, 78, 79),
+    (3, 4, 17, 18, 30, 31, 34, 46, 47, 56, 58, 72),
+    (7, 8, 13, 28, 29, 35, 50, 54, 58, 75, 76),
+    (0, 9, 51, 52, 53, 54, 55, 56, 57, 76),
+    (3, 4, 20, 22, 36, 37, 49, 51, 60, 61, 75, 76),
+    (2, 16, 27, 40, 41, 43, 50, 51, 59, 72),
+    (5, 6, 14, 15, 28, 29, 34, 48, 51, 62, 78, 79),
+    (7, 8, 19, 23, 24, 42, 46, 47, 51, 63, 64, 71),
+    (10, 17, 18, 25, 26, 35, 44, 51, 67, 68, 76, 77),
+    (9, 13, 30, 31, 38, 39, 45, 51, 65, 66, 73, 74),
+    (0, 21, 22, 23, 24, 25, 26, 27, 28, 29, 30, 31),
+    (2, 13, 20, 21, 34, 41, 45, 54, 63, 64, 76, 77),
+    (7, 8, 16, 21, 38, 39, 44, 56, 60, 61, 78, 79),
+    (9, 14, 15, 21, 40, 41, 46, 47, 52, 67, 68, 75),
+    (3, 4, 19, 21, 35, 48, 57, 59, 73, 74),
+    (5, 6, 17, 18, 21, 36, 37, 50, 53, 65, 66, 71),
+    (10, 13, 21, 42, 49, 55, 62, 72),
+)
+
 CHIP_AXES = ("x", "z", "y")
 ALL_AXES = ("x", "z", "y", "core")
 CLUSTER_AXES = ("x", "z")
@@ -65,8 +129,12 @@
     return jnp.minimum(folded, 7 - folded)
 
 
-def pack_kernel(chip_ref, emb_hbm, cl_hbm, ord_hbm, out_ref, box_ref, rank_ref, flag_ref, emb_ref, cl_ref, ord_ref, sems):
-    pairs = ((cl_hbm, cl_ref), (ord_hbm, ord_ref), (emb_hbm, emb_ref))
+def spots(table_ref, column):
+    return hot(iota((SLOTS, CAP), 1).astype(f32) == table_ref[:, column : column + 1].astype(f32))
+
+
+def pack_kernel(chip_ref, emb_hbm, cl_hbm, ord_hbm, table_hbm, out_ref, flag_ref, emb_ref, cl_ref, ord_ref, table_ref, sems):
+    pairs = ((cl_hbm, cl_ref), (ord_hbm, ord_ref), (emb_hbm, emb_ref), (table_hbm, table_ref))
     copies = [pltpu.make_async_copy(src, dst, sems.at[k]) for k, (src, dst) in enumerate(pairs)]
     for copy in copies:
         copy.start()
@@ -109,11 +177,11 @@
     main_target = jnp.where(busy | (new_place >= 8), -1, base + new_place)
     extra_target = jnp.where(busy | (new_place < 8), -8, base + new_place - 8)
     rank = jnp.where(busy, owner_place, -1)
-    rank_ref[...] = rank
     most = jnp.max(jnp.where(full > 0.5, 0.0, owner_count), axis=0, keepdims=True)
     flag = (jnp.sum(full, axis=0, keepdims=True) != 1.0) | (most > BINS * PLACES)
     flag_ref[...] = jnp.broadcast_to(jnp.where(flag, 1.0, 0.0), flag_ref.shape)
     copies[2].wait()
+    copies[3].wait()
     emb = emb_ref[...]
     wide = emb.astype(f32)
     square = wide * wide
@@ -140,24 +208,32 @@
     field_at = iota((META, rows), 0)
     meta = jnp.zeros((META, rows), f32)
     meta_extra = jnp.zeros((META, rows), f32)
+    meta_busy = jnp.zeros((META, rows), f32)
+    meta_busy_extra = jnp.zeros((META, rows), f32)
     for k, value in enumerate(fields):
         meta = jnp.where(field_at == k, value, meta)
         meta_extra = jnp.where(field_at == FIELDS + k, value, meta_extra)
+        meta_busy = jnp.where(field_at == 2 * FIELDS + k, value, meta_busy)
+        meta_busy_extra = jnp.where(field_at == 3 * FIELDS + k, value, meta_busy_extra)
     meta = meta.astype(bf16)
     meta_extra = meta_extra.astype(bf16)
     pick = hot(iota((CAP, rows), 0) == rank)
-    box_ref[:, :FEAT] = mm(pick, emb).astype(bf16)
-    box_ref[:, FEAT:] = mm_t(pick, meta).astype(bf16)
+    box = mm(pick, emb).astype(bf16)
+    box_meta = mm_t(pick, meta_busy.astype(bf16)).astype(bf16)
+    box_meta_extra = mm_t(pick, meta_busy_extra.astype(bf16)).astype(bf16)
     slot = iota((SLOTS, rows), 0)
     pick = hot(slot == main_target)
     pick_first = hot(slot == extra_target)
     pick_second = hot(slot - 4 == extra_target)
-    half = FEAT // 2
     out_ref[:, :, :FEAT] = mm(pick, emb).astype(bf16).reshape(CHIPS, 8, FEAT)
-    halves = mm(pick_first, emb[:, :half]) + mm(pick_second, emb[:, half:])
-    out_ref[:, :, FEAT : FEAT + half] = halves.astype(bf16).reshape(CHIPS, 8, half)
-    beside = mm_t(pick, meta) + mm_t(pick_first, meta_extra)
-    out_ref[:, :, FEAT + half :] = beside.astype(bf16).reshape(CHIPS, 8, META)
+    halves = mm(pick_first, emb[:, :HALF]) + mm(pick_second, emb[:, HALF:])
+    out_ref[:, :, FEAT:META_AT] = halves.astype(bf16).reshape(CHIPS, 8, HALF)
+    whole, first, second = (spots(table_ref, k) for k in range(3))
+    beside = mm_t(pick, meta) + mm_t(pick_first, meta_extra) + mm(whole, box_meta) + mm(first, box_meta_extra)
+    out_ref[:, :, META_AT:BUSY_AT] = beside.astype(bf16).reshape(CHIPS, 8, META)
+    out_ref[:, :, BUSY_AT : BUSY_AT + FEAT] = mm(whole, box).astype(bf16).reshape(CHIPS, 8, FEAT)
+    halves = mm(first, box[:, :HALF]) + mm(second, box[:, HALF:])
+    out_ref[:, :, BUSY_AT + FEAT :] = halves.astype(bf16).reshape(CHIPS, 8, HALF)
 
 
 def shifted(step):
@@ -166,8 +242,7 @@
 
 
 def fix_kernel(y_ref, flag_in_ref, in_ref, fix_ref, flag_ref):
-    half = FEAT // 2
-    meta = in_ref[:, :, FEAT + half :].reshape(SLOTS, META)
+    meta = in_ref[:, :, META_AT:BUSY_AT].reshape(SLOTS, META)
     turn = hot(iota((2 * FIELDS, META), 0) == iota((2 * FIELDS, META), 1))
     rows = mm_t(turn, meta)
     earlier = hot(iota((SLOTS, SLOTS), 0) < iota((SLOTS, SLOTS), 1))
@@ -195,10 +270,10 @@
     later = hot(iota((SLOTS, SLOTS), 1) == iota((SLOTS, SLOTS), 0) + 4)
     pick_second = mm(pick_first, later).astype(bf16)
     whole = in_ref[:, :, :FEAT].reshape(SLOTS, FEAT)
-    halves = in_ref[:, :, FEAT : FEAT + half].reshape(SLOTS, half)
+    halves = in_ref[:, :, FEAT:META_AT].reshape(SLOTS, HALF)
     taken = mm(pick, whole)
-    fix_ref[:, :half] = (taken[:, :half] + mm(pick_first, halves)).astype(bf16)
-    fix_ref[:, half:FEAT] = (taken[:, half:] + mm(pick_second, halves)).astype(bf16)
+    fix_ref[:, :HALF] = (taken[:, :HALF] + mm(pick_first, halves)).astype(bf16)
+    fix_ref[:, HALF:FEAT] = (taken[:, HALF:] + mm(pick_second, halves)).astype(bf16)
     beside = mm(mm(pick, meta).astype(bf16), shifted(0)) + mm(mm(pick_first, meta).astype(bf16), shifted(FIELDS))
     fix_ref[:, FEAT:] = beside.astype(bf16)
     step_row = iota((8, 1), 0)
@@ -257,36 +332,53 @@
     return jnp.where(spread[:CHIPS] > 0.5, value, -1.0)
 
 
-def main_kernel(own_ref, other_ref, keys_ref, metas_ref, best_ref):
-    half = FEAT // 2
+def unfold(ref, at, keys, first, second):
+    keys[:SLOTS, :] = ref[:, :, at : at + FEAT].reshape(SLOTS, FEAT)
+    halves = ref[:, :, at + FEAT : at + FEAT + HALF].reshape(SLOTS, HALF)
+    keys[SLOTS:, :HALF] = mm(first, halves).astype(bf16)
+    keys[SLOTS:, HALF:] = mm(second, halves).astype(bf16)
+
+
+def unfold_meta(ref, owned, busy, first):
+    meta = ref[:, :, META_AT:BUSY_AT].reshape(SLOTS, META)
+    meta_first = mm(first, meta).astype(bf16)
+    owned[:SLOTS, :] = meta
+    owned[SLOTS:, :] = mm(meta_first, shifted(FIELDS)).astype(bf16)
+    busy[:SLOTS, :] = mm(meta, shifted(2 * FIELDS)).astype(bf16)
+    busy[SLOTS:, :] = mm(meta_first, shifted(3 * FIELDS)).astype(bf16)
+
+
+def own_kernel(in_ref, keys_ref, metas_ref, best_ref):
     first, second = selections()
-    for k, ref in enumerate((own_ref, other_ref)):
-        at = slice(k * MAIN, k * MAIN + SLOTS)
-        keys_ref[at, :] = ref[:, :, :FEAT].reshape(SLOTS, FEAT)
-        meta = ref[:, :, FEAT + half :].reshape(SLOTS, META)
-        metas_ref[at, :] = meta
-        at = slice(k * MAIN + SLOTS, (k + 1) * MAIN)
-        halves = ref[:, :, FEAT : FEAT + half].reshape(SLOTS, half)
-        keys_ref[at, :half] = mm(first, halves).astype(bf16)
-        keys_ref[at, half:] = mm(second, halves).astype(bf16)
-        metas_ref[at, :] = mm(mm(first, meta).astype(bf16), shifted(FIELDS)).astype(bf16)
-    fields = query_rows(metas_ref[:MAIN, :])
-    best = best_over_keys(keys_ref, metas_ref, keys_ref[:MAIN, :], fields, 4)
-    best_ref[...] = jnp.broadcast_to(best, best_ref.shape)
-
-
-def tail_kernel(keys_ref, metas_ref, best_ref, own_tail_ref, other_tail_ref, out_ref):
-    metas = metas_ref[:MAIN, :]
+    unfold_meta(in_ref, metas_ref.at[0], metas_ref.at[1], first)
+    for k, at in enumerate((0, BUSY_AT)):
+        unfold(in_ref, at, keys_ref.at[k], first, second)
+        fields = query_rows(metas_ref[k])
+        best = best_over_keys(keys_ref.at[k], metas_ref.at[k], keys_ref[k], fields, 2)
+        best_ref[k] = jnp.broadcast_to(best, best_ref.shape[1:])
+
+
+def rest_kernel(in_ref, keys_ref, metas_ref, best_ref, own_tail_ref, other_tail_ref, out_ref, others, other_metas):
+    first, second = selections()
+    unfold_meta(in_ref, other_metas.at[0], other_metas.at[1], first)
+    tails = own_tail_ref, other_tail_ref
+    out = None
+    for k, at in enumerate((0, BUSY_AT)):
+        unfold(in_ref, at, others.at[k], first, second)
+        metas, queries = metas_ref[k], keys_ref[k]
+        fields = query_rows(metas)
+        best = best_over_keys(others.at[k], other_metas.at[k], queries, fields, 2)
+        best = jnp.maximum(best, best_ref[k, 0:1, :])
+        if k == 0:
+            for tail in tails:
+                best = jnp.maximum(best, best_over_keys(tail.at[:, :FEAT], tail.at[:, FEAT:], queries, fields, 1))
+        part = spread_out(best, fields, metas)
+        out = part if out is None else jnp.maximum(out, part)
+    metas, queries = own_tail_ref[:, FEAT:], own_tail_ref[:, :FEAT]
     fields = query_rows(metas)
-    best = best_ref[0:1, :]
-    for tail in (own_tail_ref, other_tail_ref):
-        best = jnp.maximum(best, best_over_keys(tail.at[:, :FEAT], tail.at[:, FEAT:], keys_ref[:MAIN, :], fields, 1))
-    out = spread_out(best, fields, metas)
-    metas = own_tail_ref[:, FEAT:]
-    fields = query_rows(metas)
-    queries = own_tail_ref[:, :FEAT]
-    best = best_over_keys(keys_ref, metas_ref, queries, fields, 2)
-    for tail in (own_tail_ref, other_tail_ref):
+    best = best_over_keys(keys_ref.at[0], metas_ref.at[0], queries, fields, 1)
+    best = jnp.maximum(best, best_over_keys(others.at[0], other_metas.at[0], queries, fields, 1))
+    for tail in tails:
         best = jnp.maximum(best, best_over_keys(tail.at[:, :FEAT], tail.at[:, FEAT:], queries, fields, 1))
     out = jnp.maximum(out, spread_out(best, fields, metas))
     at = slice(3 * FIX, 3 * FIX + 1), slice(FEAT + 10, FEAT + 11)
@@ -296,27 +388,11 @@
         out_ref[:, k, :] = out[:, k * META : (k + 1) * META]
 
 
-def busy_kernel(keys_ref, queries_ref, out_ref):
-    fields = query_rows(queries_ref[:, FEAT:])
-    best = best_over_keys(keys_ref.at[:, :FEAT], keys_ref.at[:, FEAT:], queries_ref[:, :FEAT], fields, 4)
-    out_ref[...] = jnp.full(out_ref.shape, -1.0, f32)
-    for k in range(8):
-        out_ref[k : k + 1, :CAP] = best[:, k * CAP : (k + 1) * CAP]
-
-
-def last_kernel(spread_ref, busy_ref, rank_ref, out_ref, flag_ref):
+def last_kernel(spread_ref, out_ref, flag_ref):
     best = jnp.max(spread_ref[...], axis=0)
+    out_ref[...] = best
     worst = jnp.max(jnp.max(best, axis=0, keepdims=True), axis=1, keepdims=True)
     flag_ref[...] = jnp.broadcast_to(worst, flag_ref.shape)
-    owned = jnp.concatenate([best[k : k + 1] for k in range(ROW_DEV // META)], axis=1)
-    busy = jnp.max(busy_ref[...], axis=0, keepdims=True)
-    high, middle, low = pieces(busy)
-    parts = jnp.concatenate([high.astype(f32), middle.astype(f32), low.astype(f32), jnp.zeros((5, META), f32)], axis=0)
-    rank = rank_ref[...]
-    pick = hot(iota((META, ROW_DEV), 0) == rank)
-    taken = mm(parts.astype(bf16), pick)
-    value = taken[0:1] + taken[1:2] + taken[2:3]
-    out_ref[...] = jnp.where(rank >= 0, value, owned)
 
 
 def call(kernel, shapes, args, specs, scratch=(), flops=0, bytes_accessed=0, vmem=28):
@@ -334,35 +410,42 @@
 VMEM, SMEM = pltpu.VMEM, pltpu.SMEM
 
 
+def places():
+    table = np.full((SLOTS, META), -1, np.float32)
+    for chip, block in enumerate(BLOCKS):
+        for k, row in enumerate(block):
+            if k < 8:
+                table[chip * 8 + k, 0] = row
+            else:
+                table[chip * 8 + k - 8, 1] = row
+                table[chip * 8 + k - 4, 2] = row
+    return jnp.asarray(table, bf16)
+
+
 def fast(embeddings, clusters, order):
     shape = jax.ShapeDtypeStruct
     y = lax.axis_index("y")
     chip = (lax.axis_index("x") * 4 + lax.axis_index("z")) * 4 + y
-    outbox, box, rank, flag = call(
+    swap = [(0, 1), (1, 0)]
+
+    def to_chips(value):
+        return lax.all_to_all(value, CHIP_AXES, split_axis=0, concat_axis=0, tiled=True)
+
+    outbox, flag = call(
         pack_kernel,
-        (
-            shape((CHIPS, 8, WIDE), bf16),
-            shape((CAP, NARROW), bf16),
-            shape((1, ROW_DEV), i32),
-            shape((8, 128), f32),
-        ),
-        (chip[None].astype(i32), embeddings, clusters[None, :], order[None, :]),
-        (SMEM, pl.ANY, pl.ANY, pl.ANY),
+        (shape((CHIPS, 8, WIDE), bf16), shape((8, 128), f32)),
+        (chip[None].astype(i32), embeddings, clusters[None, :], order[None, :], places()),
+        (SMEM, pl.ANY, pl.ANY, pl.ANY, pl.ANY),
         scratch=(
             pltpu.VMEM((ROW_DEV, FEAT), bf16),
             pltpu.VMEM((1, ROW_DEV), i32),
             pltpu.VMEM((1, ROW_DEV), i32),
-            pltpu.SemaphoreType.DMA((3,)),
+            pltpu.VMEM((SLOTS, META), bf16),
+            pltpu.SemaphoreType.DMA((4,)),
         ),
         vmem=58,
-        flops=2 * 700_000_000,
-        bytes_accessed=3_000_000,
     )
-    busy_keys = lax.all_gather(box, CLUSTER_AXES, axis=0, tiled=True)
-    inbox = lax.all_to_all(outbox, CHIP_AXES, split_axis=0, concat_axis=0, tiled=True)
-    swap = [(0, 1), (1, 0)]
-    along = [box] + [lax.ppermute(box, "y", [(i, (i - d) % 4) for i in range(4)]) for d in (1, 2, 3)]
-    inbox, *along = lax.optimization_barrier((inbox, *along))
+    inbox = to_chips(outbox)
     other = lax.ppermute(inbox, "core", swap)
     fix, flag_block = call(
         fix_kernel,
@@ -372,51 +455,36 @@
         flops=2 * 100_000_000,
         bytes_accessed=2_000_000,
     )
-    keys, metas, best = call(
-        main_kernel,
-        (shape((2 * MAIN, FEAT), bf16), shape((2 * MAIN, META), bf16), shape((8, MAIN), f32)),
-        (inbox, other),
-        (VMEM, VMEM),
-        flops=2 * 1_400_000_000,
-        bytes_accessed=7_000_000,
-    )
     got = [
         lax.ppermute(fix[(d - 1) * FIX : d * FIX], "y", [(i, (i + d) % 4) for i in range(4)]) for d in (1, 2, 3)
     ]
+    keys, metas, best = call(
+        own_kernel,
+        (shape((2, MAIN, FEAT), bf16), shape((2, MAIN, META), bf16), shape((2, 8, MAIN), f32)),
+        (inbox,),
+        (VMEM,),
+        flops=2 * 1_500_000_000,
+        bytes_accessed=7_000_000,
+    )
     best, *got = lax.optimization_barrier((best, *got))
     tail = jnp.concatenate(got + [flag_block], axis=0)
     other_tail = lax.ppermute(tail, "core", swap)
     spread = call(
-        tail_kernel,
+        rest_kernel,
         shape((CHIPS, ROW_DEV // META, META), f32),
-        (keys, metas, best, tail, other_tail),
-        (VMEM, VMEM, VMEM, VMEM, VMEM),
-        flops=2 * 500_000_000,
-        bytes_accessed=4_000_000,
+        (other, keys, metas, best, tail, other_tail),
+        (VMEM,) * 6,
+        scratch=(pltpu.VMEM((2, MAIN, FEAT), bf16), pltpu.VMEM((2, MAIN, META), bf16)),
+        flops=2 * 2_000_000_000,
+        bytes_accessed=7_000_000,
     )
-    spread, *along = lax.optimization_barrier((spread, *along))
-    same = jnp.concatenate(along, axis=0)
-    busy_queries = jnp.concatenate([same, lax.ppermute(same, "core", swap)], axis=0)
-    returned = lax.all_to_all(spread, CHIP_AXES, split_axis=0, concat_axis=0, tiled=True)
-    partial = call(
-        busy_kernel,
-        shape((8, META), f32),
-        (busy_keys, busy_queries),
-        (VMEM, VMEM),
-        flops=2 * 900_000_000,
-        bytes_accessed=4_500_000,
-    )
-    partial, returned = lax.optimization_barrier((partial, returned))
-    both = jnp.maximum(partial[:4], lax.ppermute(partial[4:], "core", swap))
-    back = [lax.ppermute(both[d : d + 1], "y", [(i, (i + d) % 4) for i in range(4)]) for d in (1, 2, 3)]
-    busy = jnp.concatenate([both[:1], *back], axis=0)
     out, worst = call(
         last_kernel,
-        (shape((1, ROW_DEV), f32), shape((8, 128), f32)),
-        (returned, busy, rank),
-        (VMEM, VMEM, VMEM),
+        (shape((ROW_DEV // META, META), f32), shape((8, 128), f32)),
+        (to_chips(spread),),
+        (VMEM,),
     )
-    return out[0], worst[0, 0] > 2.0
+    return out.reshape(ROW_DEV), worst[0, 0] > 2.0
 
 
 def inverse_norms(row_values):

time: 104 us -> 109 us (1.048)
  blocking collectives: 0 us -> 52.4 us
  starting transfers between devices: 34.7 us -> 11.9 us
  waiting for transfers between devices: 33 us -> 10.9 us
  local copies, waits for them, and re-layouts: 5.03 us -> 1.16 us
  Pallas kernels: 15.9 us -> 18.2 us
    all_to_all x0 -> x1, blocking collectives: none -> 52.4 us  [to_chips(): lax.all_to_all(value, CHIP_AXES, split_axis=0, concat_axis=0, tiled=True)]
    ppermute x8 -> x0, waiting for transfers between devices: 27.4 us -> none  [the longest x3 23 us: fast(): lax.ppermute(box, 'y', [(i, (i - d) % 4) for i in range(4)])]
    all_to_all x2 -> x1, starting transfers between devices: 21.3 us -> 5.03 us  [to_chips(): lax.all_to_all(value, CHIP_AXES, split_axis=0, concat_axis=0, tiled=True)]
    ppermute x8 -> x0, starting transfers between devices: 8.73 us -> none  [the longest x3 4.66 us: fast(): lax.ppermute(box, 'y', [(i, (i - d) % 4) for i in range(4)])]
    all_to_all x2 -> x1, waiting for transfers between devices: 2.12 us -> 8.63 us  [to_chips(): lax.all_to_all(value, CHIP_AXES, split_axis=0, concat_axis=0, tiled=True)]
    unnamed x23 -> x9, local copies, waits for them, and re-layouts: 4.38 us -> 0.61 us
    pallas_call x6 -> x5, Pallas kernels: 15.9 us -> 18.2 us  [call(): pl.pallas_call(kernel, out_shape=shapes, in_specs=[pl.BlockSpec(memory_sp...]
    ppermute x1, starting transfers between devices: 1.82 us -> 3.1 us  [fast(): other = lax.ppermute(inbox, 'core', swap)]
  transfers between devices with their start and end apart: 16 -> 6, of which waited for: 10 -> 3; matrix products, arithmetic and copies ran while one was open for 2% -> 0% of each run, Pallas kernels for 11% -> 4%
where the time goes in v4:
time: 109 us
  blocking collectives  52.4 us (48%)
  Pallas kernels  18.2 us (17%)
  between operations  14.1 us (13%)
  starting transfers between devices  11.9 us (11%)
  waiting for transfers between devices  10.9 us (10%)
  local copies, waits for them, and re-layouts  1.16 us (1%)
    all_to_all x1, blocking collectives, to_chips(): lax.all_to_all(value, CHIP_AXES, split_axis=0, concat_axis=0, tiled=True)  52.4 us
    pallas_call x5, Pallas kernels, call(): pl.pallas_call(kernel, out_shape=shapes, in_specs=[pl.BlockSpec(memory_sp...  18.2 us
    all_to_all x1, waiting for transfers between devices, to_chips(): lax.all_to_all(value, CHIP_AXES, split_axis=0, concat_axis=0, tiled=True)  8.63 us
    all_to_all x1, starting transfers between devices, to_chips(): lax.all_to_all(value, CHIP_AXES, split_axis=0, concat_axis=0, tiled=True)  5.03 us
    ppermute x1, starting transfers between devices, fast(): other = lax.ppermute(inbox, 'core', swap)  3.1 us
    ppermute x3, starting transfers between devices, fast(): lax.ppermute(fix[(d - 1) * FIX:d * FIX], 'y', [(i, (i + d) % 4) for i in...  2.32 us
  transfers between devices with their start and end apart: 6, of which 3 were waited for; matrix products, arithmetic and copies ran while one was open for 0% of the time, Pallas kernels for 4%

profile of v4, /device:TPU:1, one launch (start us, length us, event | category | flops | bytes accessed | tf_op | source)
XLA Modules:
  0.0 108.6 jit_solution(17526911013630019889)
XLA Ops:
  6.5 6.0 %shard_map.48 = (bf16[64,8,3200]{2,1,0:T(8,128)(2,1)}, f32[8,128]{1,0:T(8,128)}) custom-call(s32[1]{0:T(128)} %bitcast.7.chip_ref, bf16[512,1024]{1,0:T(8,128)(2,1)} %emb_hbm.1, s32[1,512]{1,0:T(1,128)} %bitcast.71, s32[1,512]{1,0:T(1,128)} %bitcast.72, bf16[512,128]{1,0:T(8,128)(2,1)} %constant.98.clone.table_hbm), custom_call_target="tpu_custom_call" | custom-call | tf_op jit(solution)/shard_map/pallas_call | solution.py:399
  12.5 0.0 copy-start
  12.5 52.4 %all_to_all.47.in_ref = bf16[64,8,3200]{2,1,0:T(8,128)(2,1)S(1)} all-to-all(bf16[64,8,3200]{2,1,0:T(8,128)(2,1)} %get-tuple-element.80), channel_id=1, replica_groups=mesh['x'=4,'z'=4,'y'=4,'core'=2] {'x','z','y'}, dimensions={0} | all-to-all | bytes 6553600 | tf_op jit(solution)/shard_map/all_to_all | solution.py:432
  64.9 3.1 %collective-permute-start = (bf16[64,8,3200]{2,1,0:T(8,128)(2,1)S(1)}, bf16[64,8,3200]{2,1,0:T(8,128)(2,1)S(1)}, u32[]{:S(2)}, u32[]{:S(2)}) collective-permute-start(bf16[64,8,3200]{2,1,0:T(8,128)(2,1)S(1)} %all_to_all.47.in_ref), channel_id=1, source_target_pairs={{0,1},{1,0},{2,3},{3,2},{4,5},{5,4},{6,7},{7,6},{8,9},{9,8},{10,11... | collective-permute-start | bytes 9830408 | tf_op jit(solution)/shard_map/ppermute | solution.py:449
  68.0 0.0 copy-done
  68.0 1.0 shard_map.50
  69.0 0.7 collective-permute-start.3
  69.7 1.6 %collective-permute-start.2 = (bf16[32,1152]{1,0:T(8,128)(2,1)S(1)}, bf16[32,1152]{1,0:T(8,128)(2,1)S(1)}, u32[]{:S(2)}, u32[]{:S(2)}) collective-permute-start(bf16[32,1152]{1,0:T(8,128)(2,1)S(1)} %get-tuple-element.145), channel_id=1, source_target_pairs={{0,4},{2,6},{4,0},{6,2},{1,5},{3,7},{5,1},{7,3},{8,12},{10,14},{12... | collective-permute-start | bytes 221192 | tf_op jit(solution)/shard_map/ppermute | solution.py:459
  71.3 0.0 collective-permute-start.1
  71.4 3.8 %shard_map.49 = (bf16[2,768,1024]{2,1,0:T(8,128)(2,1)S(1)}, bf16[2,768,128]{2,1,0:T(8,128)(2,1)S(1)}, f32[2,8,768]{2,1,0:T(8,128)S(1)}) custom-call(bf16[64,8,3200]{2,1,0:T(8,128)(2,1)S(1)} %all_to_all.47.in_ref), custom_call_target="tpu_custom_call" | custom-call | flops 3000000000 | bytes 7000000 | tf_op jit(solution)/shard_map/pallas_call | solution.py:399
  75.2 0.0 collective-permute-done.3
  75.2 0.0 collective-permute-done.2
  75.2 1.1 %collective-permute-done.1 = bf16[32,1152]{1,0:T(8,128)(2,1)S(1)} collective-permute-done((bf16[32,1152]{1,0:T(8,128)(2,1)S(1)}, bf16[32,1152]{1,0:T(8,128)(2,1)S(1)}, u32[]{:S(2)}, u32[]{:S(2)}) %collective-permute-start.1) | collective-permute-done | bytes 73760 | tf_op jit(solution)/shard_map/ppermute | solution.py:459
  76.4 1.4 %collective-permute-start.4 = (bf16[112,1152]{1,0:T(8,128)(2,1)S(1)}, bf16[112,1152]{1,0:T(8,128)(2,1)S(1)}, u32[]{:S(2)}, u32[]{:S(2)}) collective-permute-start(bf16[112,1152]{1,0:T(8,128)(2,1)S(1)} %constant_dynamic-update-slice_fusion.own_tail_ref), channel_id=1, source_target_pairs={{0,1},{1,0},{2,3},{3,2},{4,5},{5,4},{6,7},{7,6},{8,9},{9,8},{10,11... | collective-permute-start | bytes 774152 | tf_op jit(solution)/shard_map/ppermute | solution.py:471
  77.8 1.2 %collective-permute-done.4.other_tail_ref = bf16[112,1152]{1,0:T(8,128)(2,1)S(1)} collective-permute-done((bf16[112,1152]{1,0:T(8,128)(2,1)S(1)}, bf16[112,1152]{1,0:T(8,128)(2,1)S(1)}, u32[]{:S(2)}, u32[]{:S(2)}) %collective-permute-start.4) | collective-permute-done | bytes 258080 | tf_op jit(solution)/shard_map/ppermute | solution.py:471
  79.0 0.0 collective-permute-done.in_ref
  79.0 0.0 copy-start.2
  79.0 7.3 %shard_map.51 = f32[64,4,128]{2,1,0:T(4,128)} custom-call(bf16[64,8,3200]{2,1,0:T(8,128)(2,1)S(1)} %collective-permute-done.in_ref, bf16[2,768,1024]{2,1,0:T(8,128)(2,1)S(1)} %get-tuple-element.81.keys_ref, bf16[2,768,128]{2,1,0:T(8,128)(2,1)S(1)} %get-tuple-element.82.metas_ref, f32[2,8,768]{2,1,0:T(8,128)S(1)} %get-tuple-element.86.best_ref, ...), custom_call_target="tpu_custom_call" | custom-call | flops 4000000000 | bytes 7000000 | tf_op jit(solution)/shard_map/pallas_call | solution.py:399
  86.2 5.0 %all-to-all-start.5 = ((f32[64,4,128]{2,1,0:T(4,128)}), f32[64,4,128]{2,1,0:T(4,128)S(1)}, u32[]{:S(2)}, u32[]{:S(2)}) async-start(f32[64,4,128]{2,1,0:T(4,128)} %shard_map.51), calls=%async_computation.5 | async-start | bytes 262144 | tf_op jit(solution)/shard_map/all_to_all | solution.py:432
  91.3 8.6 %all-to-all-done.5.spread_ref = f32[64,4,128]{2,1,0:T(4,128)S(1)} async-done(((f32[64,4,128]{2,1,0:T(4,128)}), f32[64,4,128]{2,1,0:T(4,128)S(1)}, u32[]{:S(2)}, u32[]{:S(2)}) %all-to-all-start.5) | async-done | bytes 131104 | tf_op jit(solution)/shard_map/all_to_all | solution.py:432
  99.9 0.1 shard_map.52
  100.0 0.5 slice.21
  101.2 0.0 copy-done.2
  101.2 0.0 copy-start.3
  101.2 0.6 copy-done.3
  (6 shorter events, 0.1 us)
Async XLA Ops:
  12.5 55.5 %copy-start = (f32[8,128]{1,0:T(8,128)S(1)}, f32[8,128]{1,0:T(8,128)}, u32[]{:S(2)}) copy-start(f32[8,128]{1,0:T(8,128)} %get-tuple-element.84.flag_in_ref) | copy-start | bytes 12292
  64.9 14.1 %collective-permute-start = (bf16[64,8,3200]{2,1,0:T(8,128)(2,1)S(1)}, bf16[64,8,3200]{2,1,0:T(8,128)(2,1)S(1)}, u32[]{:S(2)}, u32[]{:S(2)}) collective-permute-start(bf16[64,8,3200]{2,1,0:T(8,128)(2,1)S(1)} %all_to_all.47.in_ref), channel_id=1, source_target_pairs={{0,1},{1,0},{2,3},{3,2},{4,5},{5,4},{6,7},{7,6},{8,9},{9,8},{10,11... | collective-permute-start | bytes 9830408 | tf_op jit(solution)/shard_map/ppermute | solution.py:449
  69.0 6.2 %collective-permute-start.3 = (bf16[32,1152]{1,0:T(8,128)(2,1)S(1)}, bf16[32,1152]{1,0:T(8,128)(2,1)S(1)}, u32[]{:S(2)}, u32[]{:S(2)}) collective-permute-start(bf16[32,1152]{1,0:T(8,128)(2,1)S(1)} %get-tuple-element.144), channel_id=1, source_target_pairs={{0,6},{2,0},{4,2},{6,4},{1,7},{3,1},{5,3},{7,5},{8,14},{10,8},{12,... | collective-permute-start | bytes 221192 | tf_op jit(solution)/shard_map/ppermute | solution.py:459
  69.7 5.5 %collective-permute-start.2 = (bf16[32,1152]{1,0:T(8,128)(2,1)S(1)}, bf16[32,1152]{1,0:T(8,128)(2,1)S(1)}, u32[]{:S(2)}, u32[]{:S(2)}) collective-permute-start(bf16[32,1152]{1,0:T(8,128)(2,1)S(1)} %get-tuple-element.145), channel_id=1, source_target_pairs={{0,4},{2,6},{4,0},{6,2},{1,5},{3,7},{5,1},{7,3},{8,12},{10,14},{12... | collective-permute-start | bytes 221192 | tf_op jit(solution)/shard_map/ppermute | solution.py:459
  71.3 5.0 %collective-permute-start.1 = (bf16[32,1152]{1,0:T(8,128)(2,1)S(1)}, bf16[32,1152]{1,0:T(8,128)(2,1)S(1)}, u32[]{:S(2)}, u32[]{:S(2)}) collective-permute-start(bf16[32,1152]{1,0:T(8,128)(2,1)S(1)} %get-tuple-element.146), channel_id=1, source_target_pairs={{0,2},{2,4},{4,6},{6,0},{1,3},{3,5},{5,7},{7,1},{8,10},{10,12},{12... | collective-permute-start | bytes 221192 | tf_op jit(solution)/shard_map/ppermute | solution.py:459
  76.4 2.6 %collective-permute-start.4 = (bf16[112,1152]{1,0:T(8,128)(2,1)S(1)}, bf16[112,1152]{1,0:T(8,128)(2,1)S(1)}, u32[]{:S(2)}, u32[]{:S(2)}) collective-permute-start(bf16[112,1152]{1,0:T(8,128)(2,1)S(1)} %constant_dynamic-update-slice_fusion.own_tail_ref), channel_id=1, source_target_pairs={{0,1},{1,0},{2,3},{3,2},{4,5},{5,4},{6,7},{7,6},{8,9},{9,8},{10,11... | collective-permute-start | bytes 774152 | tf_op jit(solution)/shard_map/ppermute | solution.py:471
  79.0 22.2 %copy-start.2 = (s32[512]{0:T(512)S(1)}, s32[512]{0:T(512)}, u32[]{:S(2)}) copy-start(s32[512]{0:T(512)} %param.9) | copy-start | bytes 6148
  86.2 13.7 %all-to-all-start.5 = ((f32[64,4,128]{2,1,0:T(4,128)}), f32[64,4,128]{2,1,0:T(4,128)S(1)}, u32[]{:S(2)}, u32[]{:S(2)}) async-start(f32[64,4,128]{2,1,0:T(4,128)} %shard_map.51), calls=%async_computation.5 | async-start | bytes 262144 | tf_op jit(solution)/shard_map/all_to_all | solution.py:432
  101.2 0.6 copy-start.3

commit v5 on v3

--- a/solution.py
+++ b/solution.py
@@ -301,7 +301,8 @@
     best = best_over_keys(keys_ref.at[:, :FEAT], keys_ref.at[:, FEAT:], queries_ref[:, :FEAT], fields, 4)
     out_ref[...] = jnp.full(out_ref.shape, -1.0, f32)
     for k in range(8):
-        out_ref[k : k + 1, :CAP] = best[:, k * CAP : (k + 1) * CAP]
+        at = 2 * (k & 3) + (k >> 2)
+        out_ref[at : at + 1, :CAP] = best[:, k * CAP : (k + 1) * CAP]
 
 
 def last_kernel(spread_ref, busy_ref, rank_ref, out_ref, flag_ref):
@@ -406,10 +407,12 @@
         flops=2 * 900_000_000,
         bytes_accessed=4_500_000,
     )
-    partial, returned = lax.optimization_barrier((partial, returned))
-    both = jnp.maximum(partial[:4], lax.ppermute(partial[4:], "core", swap))
-    back = [lax.ppermute(both[d : d + 1], "y", [(i, (i + d) % 4) for i in range(4)]) for d in (1, 2, 3)]
-    busy = jnp.concatenate([both[:1], *back], axis=0)
+    parts = [partial[:2]]
+    for d in (1, 2, 3):
+        parts.append(lax.ppermute(partial[2 * d : 2 * d + 2], "y", [(i, (i + d) % 4) for i in range(4)]))
+    to_other = jnp.concatenate([part[1:] for part in parts], axis=0)
+    to_other, returned = lax.optimization_barrier((to_other, returned))
+    busy = jnp.concatenate([part[:1] for part in parts] + [lax.ppermute(to_other, "core", swap)], axis=0)
     out, worst = call(
         last_kernel,
         (shape((1, ROW_DEV), f32), shape((8, 128), f32)),

time: 104 us -> 103 us (level)
  waiting for transfers between devices: 33 us -> 29.8 us
  starting transfers between devices: 34.7 us -> 37.3 us
    ppermute x4, starting transfers between devices: 3.65 us -> 6.27 us  [the longest x3 4.05 us: fast(): lax.ppermute(partial[2 * d:2 * d + 2], 'y', [(i, (i + d) % 4) for i in ra...]
    all_to_all x1, waiting for transfers between devices: 2.11 us -> 0.01 us  [fast(): lax.all_to_all(spread, CHIP_AXES, split_axis=0, concat_axis=0, tiled=True)]
  transfers between devices with their start and end apart: 16 -> 16, of which waited for: 10 -> 7; matrix products, arithmetic and copies ran while one was open for 2% -> 2% of each run, Pallas kernels for 11% -> 11%
where the time goes in v5:
time: 103 us; the launch traced here: 102 us
  starting transfers between devices  37.3 us (36%)
  waiting for transfers between devices  29.8 us (29%)
  Pallas kernels  15.9 us (15%)
  between operations  14.3 us (14%)
  local copies, waits for them, and re-layouts  5.07 us (5%)
    ppermute x3, waiting for transfers between devices, fast(): lax.ppermute(box, 'y', [(i, (i - d) % 4) for i in range(4)])  23 us
    pallas_call x6, Pallas kernels, call(): pl.pallas_call(kernel, out_shape=shapes, in_specs=[pl.BlockSpec(memory_sp...  15.9 us
    all_to_all x1, starting transfers between devices, fast(): lax.all_to_all(outbox, CHIP_AXES, split_axis=0, concat_axis=0, tiled=True)  12.1 us
    all_to_all x1, starting transfers between devices, fast(): lax.all_to_all(spread, CHIP_AXES, split_axis=0, concat_axis=0, tiled=True)  9.19 us
    ppermute x3, starting transfers between devices, fast(): lax.ppermute(box, 'y', [(i, (i - d) % 4) for i in range(4)])  4.66 us
    unnamed x23, local copies, waits for them, and re-layouts  4.38 us
    ppermute x3, starting transfers between devices, fast(): lax.ppermute(partial[2 * d:2 * d + 2], 'y', [(i, (i + d) % 4) for i in ra...  4.05 us
    ppermute x3, waiting for transfers between devices, fast(): lax.ppermute(partial[2 * d:2 * d + 2], 'y', [(i, (i + d) % 4) for i in ra...  2.6 us
  transfers between devices with their start and end apart: 16, of which 7 were waited for; matrix products, arithmetic and copies ran while one was open for 2% of the time, Pallas kernels for 11%

profile of v5, /device:TPU:1, one launch (start us, length us, event | category | flops | bytes accessed | tf_op | source)
XLA Modules:
  0.0 102.5 jit_solution(5400639289780838482)
XLA Ops:
  6.5 4.8 %shard_map.39 = (bf16[64,8,1664]{2,1,0:T(8,128)(2,1)}, bf16[80,1152]{1,0:T(8,128)(2,1)}, s32[1,512]{1,0:T(1,128)}, f32[8,128]{1,0:T(8,128)}) custom-call(s32[1]{0:T(128)} %bitcast.7.chip_ref, bf16[512,1024]{1,0:T(8,128)(2,1)} %emb_hbm.1, s32[1,512]{1,0:T(1,128)} %bitcast.71, s32[1,512]{1,0:T(1,128)} %bitcast.72), custom_call_target="tpu_custom_call" | custom-call | flops 1400000000 | bytes 3000000 | tf_op jit(solution)/shard_map/pallas_call | solution.py:324
  11.4 0.0 copy-start.4
  11.4 0.0 copy-start
  11.4 12.1 %all-to-all-start.4 = ((bf16[64,8,1664]{2,1,0:T(8,128)(2,1)}), bf16[64,8,1664]{2,1,0:T(8,128)(2,1)S(1)}, u32[]{:S(2)}, u32[]{:S(2)}) async-start(bf16[64,8,1664]{2,1,0:T(8,128)(2,1)} %get-tuple-element.95), calls=%async_computation.4 | async-start | bytes 3407872 | tf_op jit(solution)/shard_map/all_to_all | solution.py:363
  23.5 0.0 all-gather.7.cloned.1.call-start
  23.6 0.7 all-gather.7.cloned.1.call-update
  24.3 0.0 copy-done.4
  24.3 1.1 %collective-permute-start.2 = (bf16[80,1152]{1,0:T(8,128)(2,1)S(1)}, bf16[80,1152]{1,0:T(8,128)(2,1)S(1)}, u32[]{:S(2)}, u32[]{:S(2)}) collective-permute-start(bf16[80,1152]{1,0:T(8,128)(2,1)S(1)} %copy-done.4), channel_id=1, source_target_pairs={{0,2},{2,4},{4,6},{6,0},{1,3},{3,5},{5,7},{7,1},{8,10},{10,12},{12... | collective-permute-start | bytes 552968 | tf_op jit(solution)/shard_map/ppermute | solution.py:365
  25.3 2.4 %collective-permute-start.1 = (bf16[80,1152]{1,0:T(8,128)(2,1)S(1)}, bf16[80,1152]{1,0:T(8,128)(2,1)S(1)}, u32[]{:S(2)}, u32[]{:S(2)}) collective-permute-start(bf16[80,1152]{1,0:T(8,128)(2,1)S(1)} %copy-done.4), channel_id=1, source_target_pairs={{0,4},{2,6},{4,0},{6,2},{1,5},{3,7},{5,1},{7,3},{8,12},{10,14},{12... | collective-permute-start | bytes 552968 | tf_op jit(solution)/shard_map/ppermute | solution.py:365
  27.7 1.2 %collective-permute-start = (bf16[80,1152]{1,0:T(8,128)(2,1)S(1)}, bf16[80,1152]{1,0:T(8,128)(2,1)S(1)}, u32[]{:S(2)}, u32[]{:S(2)}) collective-permute-start(bf16[80,1152]{1,0:T(8,128)(2,1)S(1)} %copy-done.4), channel_id=1, source_target_pairs={{0,6},{2,0},{4,2},{6,4},{1,7},{3,1},{5,3},{7,5},{8,14},{10,8},{12,... | collective-permute-start | bytes 552968 | tf_op jit(solution)/shard_map/ppermute | solution.py:365
  28.9 19.8 %collective-permute-done.2 = bf16[80,1152]{1,0:T(8,128)(2,1)S(1)} collective-permute-done((bf16[80,1152]{1,0:T(8,128)(2,1)S(1)}, bf16[80,1152]{1,0:T(8,128)(2,1)S(1)}, u32[]{:S(2)}, u32[]{:S(2)}) %collective-permute-start.2) | collective-permute-done | bytes 184352 | tf_op jit(solution)/shard_map/ppermute | solution.py:365
  48.7 3.2 %collective-permute-done.1 = bf16[80,1152]{1,0:T(8,128)(2,1)S(1)} collective-permute-done((bf16[80,1152]{1,0:T(8,128)(2,1)S(1)}, bf16[80,1152]{1,0:T(8,128)(2,1)S(1)}, u32[]{:S(2)}, u32[]{:S(2)}) %collective-permute-start.1) | collective-permute-done | bytes 184352 | tf_op jit(solution)/shard_map/ppermute | solution.py:365
  51.9 0.0 copy-start.5
  51.9 0.0 collective-permute-done
  51.9 0.0 copy-start.6
  51.9 0.0 all-to-all-done.4.own_ref.in_ref
  52.0 1.8 %collective-permute-start.3 = (bf16[64,8,1664]{2,1,0:T(8,128)(2,1)S(1)}, bf16[64,8,1664]{2,1,0:T(8,128)(2,1)S(1)}, u32[]{:S(2)}, u32[]{:S(2)}) collective-permute-start(bf16[64,8,1664]{2,1,0:T(8,128)(2,1)S(1)} %all-to-all-done.4.own_ref.in_ref), channel_id=1, source_target_pairs={{0,1},{1,0},{2,3},{3,2},{4,5},{5,4},{6,7},{7,6},{8,9},{9,8},{10,11... | collective-permute-start | bytes 5111816 | tf_op jit(solution)/shard_map/ppermute | solution.py:367
  53.8 0.0 copy-done
  53.8 1.0 shard_map.41
  54.8 0.1 collective-permute-start.6
  54.9 1.3 %collective-permute-start.5 = (bf16[32,1152]{1,0:T(8,128)(2,1)S(1)}, bf16[32,1152]{1,0:T(8,128)(2,1)S(1)}, u32[]{:S(2)}, u32[]{:S(2)}) collective-permute-start(bf16[32,1152]{1,0:T(8,128)(2,1)S(1)} %get-tuple-element.173), channel_id=1, source_target_pairs={{0,4},{2,6},{4,0},{6,2},{1,5},{3,7},{5,1},{7,3},{8,12},{10,14},{12... | collective-permute-start | bytes 221192 | tf_op jit(solution)/shard_map/ppermute | solution.py:385
  56.3 0.3 collective-permute-start.4
  56.5 0.5 collective-permute-done.3.other_ref
  57.0 3.8 %shard_map.40 = (bf16[1536,1024]{1,0:T(8,128)(2,1)S(1)}, bf16[1536,128]{1,0:T(8,128)(2,1)S(1)}, f32[8,768]{1,0:T(8,128)S(1)}) custom-call(bf16[64,8,1664]{2,1,0:T(8,128)(2,1)S(1)} %all-to-all-done.4.own_ref.in_ref, bf16[64,8,1664]{2,1,0:T(8,128)(2,1)S(1)} %collective-permute-done.3.other_ref), custom_call_target="tpu_custom_call" | custom-call | flops 2800000000 | bytes 7000000 | tf_op jit(solution)/shard_map/pallas_call | solution.py:324
  60.8 0.0 collective-permute-done.6
  60.8 0.0 collective-permute-done.5
  60.8 1.1 %collective-permute-done.4 = bf16[32,1152]{1,0:T(8,128)(2,1)S(1)} collective-permute-done((bf16[32,1152]{1,0:T(8,128)(2,1)S(1)}, bf16[32,1152]{1,0:T(8,128)(2,1)S(1)}, u32[]{:S(2)}, u32[]{:S(2)}) %collective-permute-start.4) | collective-permute-done | bytes 73760 | tf_op jit(solution)/shard_map/ppermute | solution.py:385
  62.0 1.1 %collective-permute-start.7 = (bf16[112,1152]{1,0:T(8,128)(2,1)S(1)}, bf16[112,1152]{1,0:T(8,128)(2,1)S(1)}, u32[]{:S(2)}, u32[]{:S(2)}) collective-permute-start(bf16[112,1152]{1,0:T(8,128)(2,1)S(1)} %constant_dynamic-update-slice_fusion.own_tail_ref), channel_id=1, source_target_pairs={{0,1},{1,0},{2,3},{3,2},{4,5},{5,4},{6,7},{7,6},{8,9},{9,8},{10,11... | collective-permute-start | bytes 774152 | tf_op jit(solution)/shard_map/ppermute | solution.py:389
  63.1 1.2 %collective-permute-done.7.other_tail_ref = bf16[112,1152]{1,0:T(8,128)(2,1)S(1)} collective-permute-done((bf16[112,1152]{1,0:T(8,128)(2,1)S(1)}, bf16[112,1152]{1,0:T(8,128)(2,1)S(1)}, u32[]{:S(2)}, u32[]{:S(2)}) %collective-permute-start.7) | collective-permute-done | bytes 258080 | tf_op jit(solution)/shard_map/ppermute | solution.py:389
  64.2 3.4 %shard_map.42 = f32[64,4,128]{2,1,0:T(4,128)} custom-call(bf16[1536,1024]{1,0:T(8,128)(2,1)S(1)} %get-tuple-element.97.keys_ref, bf16[1536,128]{1,0:T(8,128)(2,1)S(1)} %get-tuple-element.98.metas_ref, f32[8,768]{1,0:T(8,128)S(1)} %get-tuple-element.102.best_ref, bf16[112,1152]{1,0:T(8,128)(2,1)S(1)} %constant_dynamic-update-slice_fusion.own_tail_ref, ...), custom_call_target="tpu_custom_call" | custom-call | flops 1000000000 | bytes 4000000 | tf_op jit(solution)/shard_map/pallas_call | solution.py:324
  67.6 0.0 copy-done.5
  67.6 0.0 copy-done.6
  67.6 0.1 pad_maximum_fusion
  67.7 0.5 collective-permute-start.8
  68.2 9.2 %all-to-all-start.5 = ((f32[64,4,128]{2,1,0:T(4,128)}), f32[64,4,128]{2,1,0:T(4,128)S(1)}, u32[]{:S(2)}, u32[]{:S(2)}) async-start(f32[64,4,128]{2,1,0:T(4,128)} %shard_map.42), calls=%async_computation.5 | async-start | bytes 262144 | tf_op jit(solution)/shard_map/all_to_all | solution.py:401
  77.4 0.9 constant_dynamic-update-slice_fusion.7
  78.3 0.9 constant_dynamic-update-slice_fusion.6
  79.3 0.0 collective-permute-done.8
  79.3 0.1 constant_dynamic-update-slice_fusion.4.queries_ref
  79.4 0.0 copy-start.1
  79.4 0.0 all-gather.7.cloned.1.call-done.keys_ref
  79.4 0.0 copy-start.2
  79.5 1.8 %copy-done.2 = bf16[1280,1152]{1,0:T(8,128)(2,1)S(1)} copy-done((bf16[1280,1152]{1,0:T(8,128)(2,1)S(1)}, bf16[1280,1152]{1,0:T(8,128)(2,1)}, u32[]{:S(2)}) %copy-start.2) | copy-done | bytes 2949144
  81.3 0.0 copy-start.7
  81.3 2.7 %shard_map.43 = f32[8,128]{1,0:T(8,128)S(1)} custom-call(bf16[1280,1152]{1,0:T(8,128)(2,1)S(1)} %copy-done.2, bf16[640,1152]{1,0:T(8,128)(2,1)S(1)} %constant_dynamic-update-slice_fusion.4.queries_ref), custom_call_target="tpu_custom_call" | custom-call | flops 1800000000 | bytes 4500000 | tf_op jit(solution)/shard_map/pallas_call | solution.py:324
  83.9 1.1 %collective-permute-start.9 = (f32[2,128]{1,0:T(2,128)S(1)}, f32[2,128]{1,0:T(2,128)S(1)}, u32[]{:S(2)}, u32[]{:S(2)}) collective-permute-start(f32[2,128]{1,0:T(2,128)S(1)} %get-tuple-element.177), channel_id=1, source_target_pairs={{0,2},{2,4},{4,6},{6,0},{1,3},{3,5},{5,7},{7,1},{8,10},{10,12},{12... | collective-permute-start | bytes 3080 | tf_op jit(solution)/shard_map/ppermute | solution.py:412
  85.0 1.7 %collective-permute-start.11 = (f32[2,128]{1,0:T(2,128)S(1)}, f32[2,128]{1,0:T(2,128)S(1)}, u32[]{:S(2)}, u32[]{:S(2)}) collective-permute-start(f32[2,128]{1,0:T(2,128)S(1)} %get-tuple-element.178), channel_id=1, source_target_pairs={{0,6},{2,0},{4,2},{6,4},{1,7},{3,1},{5,3},{7,5},{8,14},{10,8},{12,... | collective-permute-start | bytes 3080 | tf_op jit(solution)/shard_map/ppermute | solution.py:412
  86.7 1.3 %collective-permute-start.10 = (f32[2,128]{1,0:T(2,128)S(1)}, f32[2,128]{1,0:T(2,128)S(1)}, u32[]{:S(2)}, u32[]{:S(2)}) collective-permute-start(f32[2,128]{1,0:T(2,128)S(1)} %get-tuple-element.179), channel_id=1, source_target_pairs={{0,4},{2,6},{4,0},{6,2},{1,5},{3,7},{5,1},{7,3},{8,12},{10,14},{12... | collective-permute-start | bytes 3080 | tf_op jit(solution)/shard_map/ppermute | solution.py:412
  88.0 0.0 collective-permute-done.9
  88.0 0.0 collective-permute-done.11
  88.0 2.6 %collective-permute-done.10 = f32[2,128]{1,0:T(2,128)S(1)} collective-permute-done((f32[2,128]{1,0:T(2,128)S(1)}, f32[2,128]{1,0:T(2,128)S(1)}, u32[]{:S(2)}, u32[]{:S(2)}) %collective-permute-start.10) | collective-permute-done | bytes 1056 | tf_op jit(solution)/shard_map/ppermute | solution.py:412
  90.6 0.0 all-to-all-done.5.spread_ref
  90.6 2.2 %collective-permute-start.12 = (f32[4,128]{1,0:T(4,128)S(1)}, f32[4,128]{1,0:T(4,128)S(1)}, u32[]{:S(2)}, u32[]{:S(2)}) collective-permute-start(f32[4,128]{1,0:T(4,128)S(1)} %pad_maximum_fusion.1), channel_id=1, source_target_pairs={{0,1},{1,0},{2,3},{3,2},{4,5},{5,4},{6,7},{7,6},{8,9},{9,8},{10,11... | collective-permute-start | bytes 6152 | tf_op jit(solution)/shard_map/ppermute | solution.py:415
  92.9 0.8 collective-permute-done.12
  93.7 0.0 copy-done.1
  93.7 0.2 shard_map.44
  93.9 0.5 slice.68
  95.0 0.0 copy-done.7
  95.0 0.0 copy-start.8
  95.1 0.6 copy-done.8
  (15 shorter events, 0.2 us)
Async XLA Ops:
  11.4 12.9 %copy-start.4 = (bf16[80,1152]{1,0:T(8,128)(2,1)S(1)}, bf16[80,1152]{1,0:T(8,128)(2,1)}, u32[]{:S(2)}) copy-start(bf16[80,1152]{1,0:T(8,128)(2,1)} %get-tuple-element.111) | copy-start | bytes 552964
  11.4 42.4 %copy-start = (f32[8,128]{1,0:T(8,128)S(1)}, f32[8,128]{1,0:T(8,128)}, u32[]{:S(2)}) copy-start(f32[8,128]{1,0:T(8,128)} %get-tuple-element.100.flag_in_ref) | copy-start | bytes 12292
  11.4 40.5 %all-to-all-start.4 = ((bf16[64,8,1664]{2,1,0:T(8,128)(2,1)}), bf16[64,8,1664]{2,1,0:T(8,128)(2,1)S(1)}, u32[]{:S(2)}, u32[]{:S(2)}) async-start(bf16[64,8,1664]{2,1,0:T(8,128)(2,1)} %get-tuple-element.95), calls=%async_computation.4 | async-start | bytes 3407872 | tf_op jit(solution)/shard_map/all_to_all | solution.py:363
  23.5 55.9 %all-gather.7.cloned.1.call-start = ((), (), s32[]{:S(2)}) async-start(), calls=%async_computation.7 | async-start | bytes 3133440 | tf_op jit(solution)/shard_map/all_gather | solution.py:362
  24.3 24.4 %collective-permute-start.2 = (bf16[80,1152]{1,0:T(8,128)(2,1)S(1)}, bf16[80,1152]{1,0:T(8,128)(2,1)S(1)}, u32[]{:S(2)}, u32[]{:S(2)}) collective-permute-start(bf16[80,1152]{1,0:T(8,128)(2,1)S(1)} %copy-done.4), channel_id=1, source_target_pairs={{0,2},{2,4},{4,6},{6,0},{1,3},{3,5},{5,7},{7,1},{8,10},{10,12},{12... | collective-permute-start | bytes 552968 | tf_op jit(solution)/shard_map/ppermute | solution.py:365
  25.3 26.6 %collective-permute-start.1 = (bf16[80,1152]{1,0:T(8,128)(2,1)S(1)}, bf16[80,1152]{1,0:T(8,128)(2,1)S(1)}, u32[]{:S(2)}, u32[]{:S(2)}) collective-permute-start(bf16[80,1152]{1,0:T(8,128)(2,1)S(1)} %copy-done.4), channel_id=1, source_target_pairs={{0,4},{2,6},{4,0},{6,2},{1,5},{3,7},{5,1},{7,3},{8,12},{10,14},{12... | collective-permute-start | bytes 552968 | tf_op jit(solution)/shard_map/ppermute | solution.py:365
  27.7 24.2 %collective-permute-start = (bf16[80,1152]{1,0:T(8,128)(2,1)S(1)}, bf16[80,1152]{1,0:T(8,128)(2,1)S(1)}, u32[]{:S(2)}, u32[]{:S(2)}) collective-permute-start(bf16[80,1152]{1,0:T(8,128)(2,1)S(1)} %copy-done.4), channel_id=1, source_target_pairs={{0,6},{2,0},{4,2},{6,4},{1,7},{3,1},{5,3},{7,5},{8,14},{10,8},{12,... | collective-permute-start | bytes 552968 | tf_op jit(solution)/shard_map/ppermute | solution.py:365
  51.9 15.7 %copy-start.5 = (bf16[80,1152]{1,0:T(8,128)(2,1)}, bf16[80,1152]{1,0:T(8,128)(2,1)S(1)}, u32[]{:S(2)}) copy-start(bf16[80,1152]{1,0:T(8,128)(2,1)S(1)} %collective-permute-done.1) | copy-start | bytes 552964
  51.9 15.7 %copy-start.6 = (bf16[80,1152]{1,0:T(8,128)(2,1)}, bf16[80,1152]{1,0:T(8,128)(2,1)S(1)}, u32[]{:S(2)}) copy-start(bf16[80,1152]{1,0:T(8,128)(2,1)S(1)} %collective-permute-done) | copy-start | bytes 552964
  52.0 5.0 %collective-permute-start.3 = (bf16[64,8,1664]{2,1,0:T(8,128)(2,1)S(1)}, bf16[64,8,1664]{2,1,0:T(8,128)(2,1)S(1)}, u32[]{:S(2)}, u32[]{:S(2)}) collective-permute-start(bf16[64,8,1664]{2,1,0:T(8,128)(2,1)S(1)} %all-to-all-done.4.own_ref.in_ref), channel_id=1, source_target_pairs={{0,1},{1,0},{2,3},{3,2},{4,5},{5,4},{6,7},{7,6},{8,9},{9,8},{10,11... | collective-permute-start | bytes 5111816 | tf_op jit(solution)/shard_map/ppermute | solution.py:367
  54.8 6.0 %collective-permute-start.6 = (bf16[32,1152]{1,0:T(8,128)(2,1)S(1)}, bf16[32,1152]{1,0:T(8,128)(2,1)S(1)}, u32[]{:S(2)}, u32[]{:S(2)}) collective-permute-start(bf16[32,1152]{1,0:T(8,128)(2,1)S(1)} %get-tuple-element.172), channel_id=1, source_target_pairs={{0,6},{2,0},{4,2},{6,4},{1,7},{3,1},{5,3},{7,5},{8,14},{10,8},{12,... | collective-permute-start | bytes 221192 | tf_op jit(solution)/shard_map/ppermute | solution.py:385
  54.9 5.9 %collective-permute-start.5 = (bf16[32,1152]{1,0:T(8,128)(2,1)S(1)}, bf16[32,1152]{1,0:T(8,128)(2,1)S(1)}, u32[]{:S(2)}, u32[]{:S(2)}) collective-permute-start(bf16[32,1152]{1,0:T(8,128)(2,1)S(1)} %get-tuple-element.173), channel_id=1, source_target_pairs={{0,4},{2,6},{4,0},{6,2},{1,5},{3,7},{5,1},{7,3},{8,12},{10,14},{12... | collective-permute-start | bytes 221192 | tf_op jit(solution)/shard_map/ppermute | solution.py:385
  56.3 5.6 %collective-permute-start.4 = (bf16[32,1152]{1,0:T(8,128)(2,1)S(1)}, bf16[32,1152]{1,0:T(8,128)(2,1)S(1)}, u32[]{:S(2)}, u32[]{:S(2)}) collective-permute-start(bf16[32,1152]{1,0:T(8,128)(2,1)S(1)} %get-tuple-element.174), channel_id=1, source_target_pairs={{0,2},{2,4},{4,6},{6,0},{1,3},{3,5},{5,7},{7,1},{8,10},{10,12},{12... | collective-permute-start | bytes 221192 | tf_op jit(solution)/shard_map/ppermute | solution.py:385
  62.0 2.3 %collective-permute-start.7 = (bf16[112,1152]{1,0:T(8,128)(2,1)S(1)}, bf16[112,1152]{1,0:T(8,128)(2,1)S(1)}, u32[]{:S(2)}, u32[]{:S(2)}) collective-permute-start(bf16[112,1152]{1,0:T(8,128)(2,1)S(1)} %constant_dynamic-update-slice_fusion.own_tail_ref), channel_id=1, source_target_pairs={{0,1},{1,0},{2,3},{3,2},{4,5},{5,4},{6,7},{7,6},{8,9},{9,8},{10,11... | collective-permute-start | bytes 774152 | tf_op jit(solution)/shard_map/ppermute | solution.py:389
  67.7 11.6 %collective-permute-start.8 = (bf16[320,1152]{1,0:T(8,128)(2,1)S(1)}, bf16[320,1152]{1,0:T(8,128)(2,1)S(1)}, u32[]{:S(2)}, u32[]{:S(2)}) collective-permute-start(bf16[320,1152]{1,0:T(8,128)(2,1)S(1)} %pad_maximum_fusion), channel_id=1, source_target_pairs={{0,1},{1,0},{2,3},{3,2},{4,5},{5,4},{6,7},{7,6},{8,9},{9,8},{10,11... | collective-permute-start | bytes 2211848 | tf_op jit(solution)/shard_map/ppermute | solution.py:400
  68.2 22.5 %all-to-all-start.5 = ((f32[64,4,128]{2,1,0:T(4,128)}), f32[64,4,128]{2,1,0:T(4,128)S(1)}, u32[]{:S(2)}, u32[]{:S(2)}) async-start(f32[64,4,128]{2,1,0:T(4,128)} %shard_map.42), calls=%async_computation.5 | async-start | bytes 262144 | tf_op jit(solution)/shard_map/all_to_all | solution.py:401
  79.4 14.3 %copy-start.1 = (s32[1,512]{1,0:T(1,128)S(1)}, s32[1,512]{1,0:T(1,128)}, u32[]{:S(2)}) copy-start(s32[1,512]{1,0:T(1,128)} %get-tuple-element.118.rank_ref) | copy-start | bytes 6148
  79.4 1.8 %copy-start.2 = (bf16[1280,1152]{1,0:T(8,128)(2,1)S(1)}, bf16[1280,1152]{1,0:T(8,128)(2,1)}, u32[]{:S(2)}) copy-start(bf16[1280,1152]{1,0:T(8,128)(2,1)} %all-gather.7.cloned.1.call-done.keys_ref) | copy-start | bytes 8847364
  81.3 13.8 %copy-start.7 = (s32[512]{0:T(512)S(1)}, s32[512]{0:T(512)}, u32[]{:S(2)}) copy-start(s32[512]{0:T(512)} %param.8) | copy-start | bytes 6148
  83.9 4.1 %collective-permute-start.9 = (f32[2,128]{1,0:T(2,128)S(1)}, f32[2,128]{1,0:T(2,128)S(1)}, u32[]{:S(2)}, u32[]{:S(2)}) collective-permute-start(f32[2,128]{1,0:T(2,128)S(1)} %get-tuple-element.177), channel_id=1, source_target_pairs={{0,2},{2,4},{4,6},{6,0},{1,3},{3,5},{5,7},{7,1},{8,10},{10,12},{12... | collective-permute-start | bytes 3080 | tf_op jit(solution)/shard_map/ppermute | solution.py:412
  85.0 3.0 %collective-permute-start.11 = (f32[2,128]{1,0:T(2,128)S(1)}, f32[2,128]{1,0:T(2,128)S(1)}, u32[]{:S(2)}, u32[]{:S(2)}) collective-permute-start(f32[2,128]{1,0:T(2,128)S(1)} %get-tuple-element.178), channel_id=1, source_target_pairs={{0,6},{2,0},{4,2},{6,4},{1,7},{3,1},{5,3},{7,5},{8,14},{10,8},{12,... | collective-permute-start | bytes 3080 | tf_op jit(solution)/shard_map/ppermute | solution.py:412
  86.7 3.9 %collective-permute-start.10 = (f32[2,128]{1,0:T(2,128)S(1)}, f32[2,128]{1,0:T(2,128)S(1)}, u32[]{:S(2)}, u32[]{:S(2)}) collective-permute-start(f32[2,128]{1,0:T(2,128)S(1)} %get-tuple-element.179), channel_id=1, source_target_pairs={{0,4},{2,6},{4,0},{6,2},{1,5},{3,7},{5,1},{7,3},{8,12},{10,14},{12... | collective-permute-start | bytes 3080 | tf_op jit(solution)/shard_map/ppermute | solution.py:412
  90.6 3.0 %collective-permute-start.12 = (f32[4,128]{1,0:T(4,128)S(1)}, f32[4,128]{1,0:T(4,128)S(1)}, u32[]{:S(2)}, u32[]{:S(2)}) collective-permute-start(f32[4,128]{1,0:T(4,128)S(1)} %pad_maximum_fusion.1), channel_id=1, source_target_pairs={{0,1},{1,0},{2,3},{3,2},{4,5},{5,4},{6,7},{7,6},{8,9},{9,8},{10,11... | collective-permute-start | bytes 6152 | tf_op jit(solution)/shard_map/ppermute | solution.py:415
  95.0 0.6 copy-start.8
Sparse Core Ops, SparseCore 0:
  26.6 52.3 all-gather.6

commit v6 on v5

--- a/solution.py
+++ b/solution.py
@@ -12,10 +12,10 @@
 CAP = 80
 CHIPS = 64
 BINS = 4
-PLACES = 12
+PLACES = 11
 FIX = 32
 META = 128
-WIDE = FEAT + FEAT // 2 + META
+WIDE = FEAT + FEAT // 2
 NARROW = FEAT + META
 SLOTS = CHIPS * 8
 EXTRA = CHIPS * 4
@@ -25,6 +25,8 @@
 LOW = -1e30
 BAD = 4.0
 FIELDS = 16
+FIELD_LANES = 16 * FIELDS
+FIELD_ROW = 3
 
 CHIP_AXES = ("x", "z", "y")
 ALL_AXES = ("x", "z", "y", "core")
@@ -117,10 +119,11 @@
     emb = emb_ref[...]
     wide = emb.astype(f32)
     square = wide * wide
-    square_high = square.astype(bf16)
-    square_low = (square - square_high.astype(f32)).astype(bf16)
-    ones = jnp.ones((8, emb.shape[1]), bf16)
-    total = (mm_t(ones, square_high) + mm_t(ones, square_low))[0:1, :] + 1e-06
+    folded = square[:, :META]
+    for k in range(1, FEAT // META):
+        folded = folded + square[:, k * META : (k + 1) * META]
+    ones = jnp.ones((8, META), bf16)
+    total = sum(mm_t(ones, piece) for piece in pieces(folded))[0:1, :] + 1e-06
     inv = lax.rsqrt(total)
     inv = inv * (1.5 - 0.5 * total * inv * inv)
     high, middle, low = pieces(inv)
@@ -139,12 +142,11 @@
     ]
     field_at = iota((META, rows), 0)
     meta = jnp.zeros((META, rows), f32)
-    meta_extra = jnp.zeros((META, rows), f32)
     for k, value in enumerate(fields):
         meta = jnp.where(field_at == k, value, meta)
-        meta_extra = jnp.where(field_at == FIELDS + k, value, meta_extra)
+    sent = jnp.concatenate([meta[:FIELDS]] * (FIELD_LANES // FIELDS), axis=0)
+    sent = jnp.where((iota((FIELD_LANES, rows), 0) >> 4) == new_place, sent, 0.0).astype(bf16)
     meta = meta.astype(bf16)
-    meta_extra = meta_extra.astype(bf16)
     pick = hot(iota((CAP, rows), 0) == rank)
     box_ref[:, :FEAT] = mm(pick, emb).astype(bf16)
     box_ref[:, FEAT:] = mm_t(pick, meta).astype(bf16)
@@ -155,9 +157,21 @@
     half = FEAT // 2
     out_ref[:, :, :FEAT] = mm(pick, emb).astype(bf16).reshape(CHIPS, 8, FEAT)
     halves = mm(pick_first, emb[:, :half]) + mm(pick_second, emb[:, half:])
-    out_ref[:, :, FEAT : FEAT + half] = halves.astype(bf16).reshape(CHIPS, 8, half)
-    beside = mm_t(pick, meta) + mm_t(pick_first, meta_extra)
-    out_ref[:, :, FEAT + half :] = beside.astype(bf16).reshape(CHIPS, 8, META)
+    to_chip = hot(iota((CHIPS, rows), 0) == jnp.where(busy, -1, owner * BINS + new_bin))
+    beside = mm_t(to_chip, sent).astype(bf16)
+    beside = mm(hot(iota((SLOTS, CHIPS), 0) == iota((SLOTS, CHIPS), 1) * 8 + FIELD_ROW), beside)
+    halves = jnp.concatenate([halves[:, :FIELD_LANES] + beside, halves[:, FIELD_LANES:]], axis=1)
+    out_ref[:, :, FEAT:] = halves.astype(bf16).reshape(CHIPS, 8, half)
+
+
+def fields_of(ref):
+    block = ref[:, :, FEAT : FEAT + FIELD_LANES].reshape(SLOTS, FIELD_LANES)
+    spread = mm(hot(iota((SLOTS, SLOTS), 1) == (iota((SLOTS, SLOTS), 0) >> 3) * 8 + FIELD_ROW), block)
+    place, group = iota((SLOTS, FIELD_LANES), 0) & 7, iota((SLOTS, FIELD_LANES), 1) >> 4
+    whole = jnp.where(group == place, spread, 0.0).astype(bf16)
+    half = jnp.where(group == place + 8, spread, 0.0).astype(bf16)
+    source, lane = iota((FIELD_LANES, META), 0) & 15, iota((FIELD_LANES, META), 1)
+    return (mm(whole, hot(source == lane)) + mm(half, hot(source == lane - FIELDS))).astype(bf16)
 
 
 def shifted(step):
@@ -167,7 +181,7 @@
 
 def fix_kernel(y_ref, flag_in_ref, in_ref, fix_ref, flag_ref):
     half = FEAT // 2
-    meta = in_ref[:, :, FEAT + half :].reshape(SLOTS, META)
+    meta = fields_of(in_ref)
     turn = hot(iota((2 * FIELDS, META), 0) == iota((2 * FIELDS, META), 1))
     rows = mm_t(turn, meta)
     earlier = hot(iota((SLOTS, SLOTS), 0) < iota((SLOTS, SLOTS), 1))
@@ -263,7 +277,7 @@
     for k, ref in enumerate((own_ref, other_ref)):
         at = slice(k * MAIN, k * MAIN + SLOTS)
         keys_ref[at, :] = ref[:, :, :FEAT].reshape(SLOTS, FEAT)
-        meta = ref[:, :, FEAT + half :].reshape(SLOTS, META)
+        meta = fields_of(ref)
         metas_ref[at, :] = meta
         at = slice(k * MAIN + SLOTS, (k + 1) * MAIN)
         halves = ref[:, :, FEAT : FEAT + half].reshape(SLOTS, half)
@@ -308,7 +322,7 @@
 def last_kernel(spread_ref, busy_ref, rank_ref, out_ref, flag_ref):
     best = jnp.max(spread_ref[...], axis=0)
     worst = jnp.max(jnp.max(best, axis=0, keepdims=True), axis=1, keepdims=True)
-    flag_ref[...] = jnp.broadcast_to(worst, flag_ref.shape)
+    flag_ref[0] = jnp.where(jnp.max(worst) > 2.0, 1, 0)
     owned = jnp.concatenate([best[k : k + 1] for k in range(ROW_DEV // META)], axis=1)
     busy = jnp.max(busy_ref[...], axis=0, keepdims=True)
     high, middle, low = pieces(busy)
@@ -320,12 +334,12 @@
     out_ref[...] = jnp.where(rank >= 0, value, owned)
 
 
-def call(kernel, shapes, args, specs, scratch=(), flops=0, bytes_accessed=0, vmem=28):
+def call(kernel, shapes, args, specs, scratch=(), flops=0, bytes_accessed=0, vmem=28, outs=None):
     return pl.pallas_call(
         kernel,
         out_shape=shapes,
         in_specs=[pl.BlockSpec(memory_space=s) for s in specs],
-        out_specs=jax.tree.map(lambda _: pl.BlockSpec(memory_space=pltpu.VMEM), shapes),
+        out_specs=outs or jax.tree.map(lambda _: pl.BlockSpec(memory_space=VMEM), shapes),
         scratch_shapes=scratch,
         compiler_params=pltpu.CompilerParams(vmem_limit_bytes=vmem * 1024 * 1024),
         cost_estimate=pl.CostEstimate(flops=flops, bytes_accessed=bytes_accessed, transcendentals=0),
@@ -415,11 +429,12 @@
     busy = jnp.concatenate([part[:1] for part in parts] + [lax.ppermute(to_other, "core", swap)], axis=0)
     out, worst = call(
         last_kernel,
-        (shape((1, ROW_DEV), f32), shape((8, 128), f32)),
+        (shape((1, ROW_DEV), f32), shape((1,), i32)),
         (returned, busy, rank),
         (VMEM, VMEM, VMEM),
-    )
-    return out[0], worst[0, 0] > 2.0
+        outs=(pl.BlockSpec(memory_space=VMEM), pl.BlockSpec(memory_space=SMEM)),
+    )
+    return out[0], worst[0] > 0
 
 
 def inverse_norms(row_values):

time: 103 us -> 102 us (level)
  waiting for transfers between devices: 29.8 us -> 27.6 us
  Pallas kernels: 15.9 us -> 17.6 us
  local copies, waits for them, and re-layouts: 5.07 us -> 3.63 us
    pallas_call x6, Pallas kernels: 15.9 us -> 17.6 us  [call(): pl.pallas_call(kernel, out_shape=shapes, in_specs=[pl.BlockSpec(memory_sp...]
    ppermute x3, waiting for transfers between devices: 23 us -> 21.6 us  [fast(): lax.ppermute(box, 'y', [(i, (i - d) % 4) for i in range(4)])]
    unnamed x23 -> x21, local copies, waits for them, and re-layouts: 4.38 us -> 3.46 us
  transfers between devices with their start and end apart: 16 -> 16, of which waited for: 7 -> 6; matrix products, arithmetic and copies ran while one was open for 2% -> 1% of each run, Pallas kernels for 11% -> 12%
where the time goes in v6:
time: 102 us; the launch traced here: 101 us
  starting transfers between devices  38.2 us (37%)
  waiting for transfers between devices  27.6 us (27%)
  Pallas kernels  17.6 us (17%)
  between operations  14.3 us (14%)
  local copies, waits for them, and re-layouts  3.63 us (4%)
    ppermute x3, waiting for transfers between devices, fast(): lax.ppermute(box, 'y', [(i, (i - d) % 4) for i in range(4)])  21.6 us
    pallas_call x6, Pallas kernels, call(): pl.pallas_call(kernel, out_shape=shapes, in_specs=[pl.BlockSpec(memory_sp...  17.6 us
    all_to_all x1, starting transfers between devices, fast(): lax.all_to_all(outbox, CHIP_AXES, split_axis=0, concat_axis=0, tiled=True)  12.1 us
    all_to_all x1, starting transfers between devices, fast(): lax.all_to_all(spread, CHIP_AXES, split_axis=0, concat_axis=0, tiled=True)  10.1 us
    ppermute x3, starting transfers between devices, fast(): lax.ppermute(box, 'y', [(i, (i - d) % 4) for i in range(4)])  4.66 us
    ppermute x3, starting transfers between devices, fast(): lax.ppermute(partial[2 * d:2 * d + 2], 'y', [(i, (i + d) % 4) for i in ra...  4.04 us
    unnamed x21, local copies, waits for them, and re-layouts  3.46 us
    ppermute x3, waiting for transfers between devices, fast(): lax.ppermute(partial[2 * d:2 * d + 2], 'y', [(i, (i + d) % 4) for i in ra...  2.6 us
  transfers between devices with their start and end apart: 16, of which 6 were waited for; matrix products, arithmetic and copies ran while one was open for 1% of the time, Pallas kernels for 12%

profile of v6, /device:TPU:1, one launch (start us, length us, event | category | flops | bytes accessed | tf_op | source)
XLA Modules:
  0.0 101.4 jit_solution(5637464613654175776)
XLA Ops:
  6.5 4.4 %shard_map.39 = (bf16[64,8,1536]{2,1,0:T(8,128)(2,1)}, bf16[80,1152]{1,0:T(8,128)(2,1)}, s32[1,512]{1,0:T(1,128)}, f32[8,128]{1,0:T(8,128)}) custom-call(s32[1]{0:T(128)} %bitcast.7.chip_ref, bf16[512,1024]{1,0:T(8,128)(2,1)} %emb_hbm.1, s32[1,512]{1,0:T(1,128)} %bitcast.71, s32[1,512]{1,0:T(1,128)} %bitcast.72), custom_call_target="tpu_custom_call" | custom-call | flops 1400000000 | bytes 3000000 | tf_op jit(solution)/shard_map/pallas_call | solution.py:338
  10.9 0.0 copy-start.4
  11.0 0.0 copy-start
  11.0 12.1 %all-to-all-start.4 = ((bf16[64,8,1536]{2,1,0:T(8,128)(2,1)}), bf16[64,8,1536]{2,1,0:T(8,128)(2,1)S(1)}, u32[]{:S(2)}, u32[]{:S(2)}) async-start(bf16[64,8,1536]{2,1,0:T(8,128)(2,1)} %get-tuple-element.95), calls=%async_computation.4 | async-start | bytes 3145728 | tf_op jit(solution)/shard_map/all_to_all | solution.py:377
  23.1 0.0 all-gather.7.cloned.1.call-start
  23.1 0.7 all-gather.7.cloned.1.call-update
  23.8 0.0 copy-done.4
  23.8 1.1 %collective-permute-start.2 = (bf16[80,1152]{1,0:T(8,128)(2,1)S(1)}, bf16[80,1152]{1,0:T(8,128)(2,1)S(1)}, u32[]{:S(2)}, u32[]{:S(2)}) collective-permute-start(bf16[80,1152]{1,0:T(8,128)(2,1)S(1)} %copy-done.4), channel_id=1, source_target_pairs={{0,2},{2,4},{4,6},{6,0},{1,3},{3,5},{5,7},{7,1},{8,10},{10,12},{12... | collective-permute-start | bytes 552968 | tf_op jit(solution)/shard_map/ppermute | solution.py:379
  24.9 2.4 %collective-permute-start.1 = (bf16[80,1152]{1,0:T(8,128)(2,1)S(1)}, bf16[80,1152]{1,0:T(8,128)(2,1)S(1)}, u32[]{:S(2)}, u32[]{:S(2)}) collective-permute-start(bf16[80,1152]{1,0:T(8,128)(2,1)S(1)} %copy-done.4), channel_id=1, source_target_pairs={{0,4},{2,6},{4,0},{6,2},{1,5},{3,7},{5,1},{7,3},{8,12},{10,14},{12... | collective-permute-start | bytes 552968 | tf_op jit(solution)/shard_map/ppermute | solution.py:379
  27.3 1.2 %collective-permute-start = (bf16[80,1152]{1,0:T(8,128)(2,1)S(1)}, bf16[80,1152]{1,0:T(8,128)(2,1)S(1)}, u32[]{:S(2)}, u32[]{:S(2)}) collective-permute-start(bf16[80,1152]{1,0:T(8,128)(2,1)S(1)} %copy-done.4), channel_id=1, source_target_pairs={{0,6},{2,0},{4,2},{6,4},{1,7},{3,1},{5,3},{7,5},{8,14},{10,8},{12,... | collective-permute-start | bytes 552968 | tf_op jit(solution)/shard_map/ppermute | solution.py:379
  28.5 18.3 %collective-permute-done.2 = bf16[80,1152]{1,0:T(8,128)(2,1)S(1)} collective-permute-done((bf16[80,1152]{1,0:T(8,128)(2,1)S(1)}, bf16[80,1152]{1,0:T(8,128)(2,1)S(1)}, u32[]{:S(2)}, u32[]{:S(2)}) %collective-permute-start.2) | collective-permute-done | bytes 184352 | tf_op jit(solution)/shard_map/ppermute | solution.py:379
  46.8 3.3 %collective-permute-done.1 = bf16[80,1152]{1,0:T(8,128)(2,1)S(1)} collective-permute-done((bf16[80,1152]{1,0:T(8,128)(2,1)S(1)}, bf16[80,1152]{1,0:T(8,128)(2,1)S(1)}, u32[]{:S(2)}, u32[]{:S(2)}) %collective-permute-start.1) | collective-permute-done | bytes 184352 | tf_op jit(solution)/shard_map/ppermute | solution.py:379
  50.1 0.0 collective-permute-done
  50.1 0.0 copy-start.5
  50.1 0.0 all-to-all-done.4.own_ref.in_ref
  50.1 1.8 %collective-permute-start.3 = (bf16[64,8,1536]{2,1,0:T(8,128)(2,1)S(1)}, bf16[64,8,1536]{2,1,0:T(8,128)(2,1)S(1)}, u32[]{:S(2)}, u32[]{:S(2)}) collective-permute-start(bf16[64,8,1536]{2,1,0:T(8,128)(2,1)S(1)} %all-to-all-done.4.own_ref.in_ref), channel_id=1, source_target_pairs={{0,1},{1,0},{2,3},{3,2},{4,5},{5,4},{6,7},{7,6},{8,9},{9,8},{10,11... | collective-permute-start | bytes 4718600 | tf_op jit(solution)/shard_map/ppermute | solution.py:381
  51.9 0.0 copy-done
  51.9 1.6 %shard_map.41 = (bf16[96,1152]{1,0:T(8,128)(2,1)S(1)}, bf16[16,1152]{1,0:T(8,128)(2,1)S(1)}) custom-call(s32[1]{0:T(128)} %bitcast.10.y_ref, f32[8,128]{1,0:T(8,128)S(1)} %copy-done, bf16[64,8,1536]{2,1,0:T(8,128)(2,1)S(1)} %all-to-all-done.4.own_ref.in_ref), custom_call_target="tpu_custom_call" | custom-call | flops 200000000 | bytes 2000000 | tf_op jit(solution)/shard_map/pallas_call | solution.py:338
  53.6 0.3 collective-permute-start.6
  53.9 1.2 %collective-permute-start.5 = (bf16[32,1152]{1,0:T(8,128)(2,1)S(1)}, bf16[32,1152]{1,0:T(8,128)(2,1)S(1)}, u32[]{:S(2)}, u32[]{:S(2)}) collective-permute-start(bf16[32,1152]{1,0:T(8,128)(2,1)S(1)} %get-tuple-element.173), channel_id=1, source_target_pairs={{0,4},{2,6},{4,0},{6,2},{1,5},{3,7},{5,1},{7,3},{8,12},{10,14},{12... | collective-permute-start | bytes 221192 | tf_op jit(solution)/shard_map/ppermute | solution.py:399
  55.1 0.2 collective-permute-start.4
  55.3 0.0 collective-permute-done.3.other_ref
  55.3 4.9 %shard_map.40 = (bf16[1536,1024]{1,0:T(8,128)(2,1)S(1)}, bf16[1536,128]{1,0:T(8,128)(2,1)S(1)}, f32[8,768]{1,0:T(8,128)S(1)}) custom-call(bf16[64,8,1536]{2,1,0:T(8,128)(2,1)S(1)} %all-to-all-done.4.own_ref.in_ref, bf16[64,8,1536]{2,1,0:T(8,128)(2,1)S(1)} %collective-permute-done.3.other_ref), custom_call_target="tpu_custom_call" | custom-call | flops 2800000000 | bytes 7000000 | tf_op jit(solution)/shard_map/pallas_call | solution.py:338
  60.2 0.0 collective-permute-done.6
  60.2 0.0 collective-permute-done.5
  60.3 0.7 collective-permute-done.4
  61.0 1.0 %collective-permute-start.7 = (bf16[112,1152]{1,0:T(8,128)(2,1)S(1)}, bf16[112,1152]{1,0:T(8,128)(2,1)S(1)}, u32[]{:S(2)}, u32[]{:S(2)}) collective-permute-start(bf16[112,1152]{1,0:T(8,128)(2,1)S(1)} %constant_dynamic-update-slice_fusion.own_tail_ref), channel_id=1, source_target_pairs={{0,1},{1,0},{2,3},{3,2},{4,5},{5,4},{6,7},{7,6},{8,9},{9,8},{10,11... | collective-permute-start | bytes 774152 | tf_op jit(solution)/shard_map/ppermute | solution.py:403
  62.0 1.2 %collective-permute-done.7.other_tail_ref = bf16[112,1152]{1,0:T(8,128)(2,1)S(1)} collective-permute-done((bf16[112,1152]{1,0:T(8,128)(2,1)S(1)}, bf16[112,1152]{1,0:T(8,128)(2,1)S(1)}, u32[]{:S(2)}, u32[]{:S(2)}) %collective-permute-start.7) | collective-permute-done | bytes 258080 | tf_op jit(solution)/shard_map/ppermute | solution.py:403
  63.2 3.4 %shard_map.42 = f32[64,4,128]{2,1,0:T(4,128)} custom-call(bf16[1536,1024]{1,0:T(8,128)(2,1)S(1)} %get-tuple-element.97.keys_ref, bf16[1536,128]{1,0:T(8,128)(2,1)S(1)} %get-tuple-element.98.metas_ref, f32[8,768]{1,0:T(8,128)S(1)} %get-tuple-element.102.best_ref, bf16[112,1152]{1,0:T(8,128)(2,1)S(1)} %constant_dynamic-update-slice_fusion.own_tail_ref, ...), custom_call_target="tpu_custom_call" | custom-call | flops 1000000000 | bytes 4000000 | tf_op jit(solution)/shard_map/pallas_call | solution.py:338
  66.6 0.0 copy-done.5
  66.6 0.1 pad_maximum_fusion
  66.6 0.5 collective-permute-start.8
  67.1 10.1 %all-to-all-start.5 = ((f32[64,4,128]{2,1,0:T(4,128)}), f32[64,4,128]{2,1,0:T(4,128)S(1)}, u32[]{:S(2)}, u32[]{:S(2)}) async-start(f32[64,4,128]{2,1,0:T(4,128)} %shard_map.42), calls=%async_computation.5 | async-start | bytes 262144 | tf_op jit(solution)/shard_map/all_to_all | solution.py:415
  77.2 0.9 constant_dynamic-update-slice_fusion.7
  78.2 0.0 collective-permute-done.8
  78.2 0.1 constant_dynamic-update-slice_fusion.4.queries_ref
  78.3 0.0 copy-start.1
  78.3 0.0 all-gather.7.cloned.1.call-done.keys_ref
  78.4 0.0 copy-start.2
  78.4 1.8 %copy-done.2 = bf16[1280,1152]{1,0:T(8,128)(2,1)S(1)} copy-done((bf16[1280,1152]{1,0:T(8,128)(2,1)S(1)}, bf16[1280,1152]{1,0:T(8,128)(2,1)}, u32[]{:S(2)}) %copy-start.2) | copy-done | bytes 2949144
  80.2 0.0 copy-start.6
  80.2 2.6 %shard_map.43 = f32[8,128]{1,0:T(8,128)S(1)} custom-call(bf16[1280,1152]{1,0:T(8,128)(2,1)S(1)} %copy-done.2, bf16[640,1152]{1,0:T(8,128)(2,1)S(1)} %constant_dynamic-update-slice_fusion.4.queries_ref), custom_call_target="tpu_custom_call" | custom-call | flops 1800000000 | bytes 4500000 | tf_op jit(solution)/shard_map/pallas_call | solution.py:338
  82.8 1.1 %collective-permute-start.9 = (f32[2,128]{1,0:T(2,128)S(1)}, f32[2,128]{1,0:T(2,128)S(1)}, u32[]{:S(2)}, u32[]{:S(2)}) collective-permute-start(f32[2,128]{1,0:T(2,128)S(1)} %get-tuple-element.177), channel_id=1, source_target_pairs={{0,2},{2,4},{4,6},{6,0},{1,3},{3,5},{5,7},{7,1},{8,10},{10,12},{12... | collective-permute-start | bytes 3080 | tf_op jit(solution)/shard_map/ppermute | solution.py:426
  83.9 1.7 %collective-permute-start.11 = (f32[2,128]{1,0:T(2,128)S(1)}, f32[2,128]{1,0:T(2,128)S(1)}, u32[]{:S(2)}, u32[]{:S(2)}) collective-permute-start(f32[2,128]{1,0:T(2,128)S(1)} %get-tuple-element.178), channel_id=1, source_target_pairs={{0,6},{2,0},{4,2},{6,4},{1,7},{3,1},{5,3},{7,5},{8,14},{10,8},{12,... | collective-permute-start | bytes 3080 | tf_op jit(solution)/shard_map/ppermute | solution.py:426
  85.6 1.3 %collective-permute-start.10 = (f32[2,128]{1,0:T(2,128)S(1)}, f32[2,128]{1,0:T(2,128)S(1)}, u32[]{:S(2)}, u32[]{:S(2)}) collective-permute-start(f32[2,128]{1,0:T(2,128)S(1)} %get-tuple-element.179), channel_id=1, source_target_pairs={{0,4},{2,6},{4,0},{6,2},{1,5},{3,7},{5,1},{7,3},{8,12},{10,14},{12... | collective-permute-start | bytes 3080 | tf_op jit(solution)/shard_map/ppermute | solution.py:426
  86.9 0.0 collective-permute-done.9
  86.9 0.0 collective-permute-done.11
  86.9 2.6 %collective-permute-done.10 = f32[2,128]{1,0:T(2,128)S(1)} collective-permute-done((f32[2,128]{1,0:T(2,128)S(1)}, f32[2,128]{1,0:T(2,128)S(1)}, u32[]{:S(2)}, u32[]{:S(2)}) %collective-permute-start.10) | collective-permute-done | bytes 1056 | tf_op jit(solution)/shard_map/ppermute | solution.py:426
  89.5 0.0 all-to-all-done.5.spread_ref
  89.5 2.2 %collective-permute-start.12 = (f32[4,128]{1,0:T(4,128)S(1)}, f32[4,128]{1,0:T(4,128)S(1)}, u32[]{:S(2)}, u32[]{:S(2)}) collective-permute-start(f32[4,128]{1,0:T(4,128)S(1)} %pad_maximum_fusion.1), channel_id=1, source_target_pairs={{0,1},{1,0},{2,3},{3,2},{4,5},{5,4},{6,7},{7,6},{8,9},{9,8},{10,11... | collective-permute-start | bytes 6152 | tf_op jit(solution)/shard_map/ppermute | solution.py:429
  91.8 0.8 collective-permute-done.12
  92.6 0.0 copy-done.1
  92.6 0.7 shard_map.44
  93.9 0.0 copy-done.6
  94.0 0.0 copy-start.7
  94.0 0.6 copy-done.7
  (16 shorter events, 0.2 us)
Async XLA Ops:
  10.9 12.9 %copy-start.4 = (bf16[80,1152]{1,0:T(8,128)(2,1)S(1)}, bf16[80,1152]{1,0:T(8,128)(2,1)}, u32[]{:S(2)}) copy-start(bf16[80,1152]{1,0:T(8,128)(2,1)} %get-tuple-element.111) | copy-start | bytes 552964
  11.0 41.0 %copy-start = (f32[8,128]{1,0:T(8,128)S(1)}, f32[8,128]{1,0:T(8,128)}, u32[]{:S(2)}) copy-start(f32[8,128]{1,0:T(8,128)} %get-tuple-element.100.flag_in_ref) | copy-start | bytes 12292
  11.0 39.2 %all-to-all-start.4 = ((bf16[64,8,1536]{2,1,0:T(8,128)(2,1)}), bf16[64,8,1536]{2,1,0:T(8,128)(2,1)S(1)}, u32[]{:S(2)}, u32[]{:S(2)}) async-start(bf16[64,8,1536]{2,1,0:T(8,128)(2,1)} %get-tuple-element.95), calls=%async_computation.4 | async-start | bytes 3145728 | tf_op jit(solution)/shard_map/all_to_all | solution.py:377
  23.1 55.3 %all-gather.7.cloned.1.call-start = ((), (), s32[]{:S(2)}) async-start(), calls=%async_computation.7 | async-start | bytes 3133440 | tf_op jit(solution)/shard_map/all_gather | solution.py:376
  23.8 23.0 %collective-permute-start.2 = (bf16[80,1152]{1,0:T(8,128)(2,1)S(1)}, bf16[80,1152]{1,0:T(8,128)(2,1)S(1)}, u32[]{:S(2)}, u32[]{:S(2)}) collective-permute-start(bf16[80,1152]{1,0:T(8,128)(2,1)S(1)} %copy-done.4), channel_id=1, source_target_pairs={{0,2},{2,4},{4,6},{6,0},{1,3},{3,5},{5,7},{7,1},{8,10},{10,12},{12... | collective-permute-start | bytes 552968 | tf_op jit(solution)/shard_map/ppermute | solution.py:379
  24.9 25.2 %collective-permute-start.1 = (bf16[80,1152]{1,0:T(8,128)(2,1)S(1)}, bf16[80,1152]{1,0:T(8,128)(2,1)S(1)}, u32[]{:S(2)}, u32[]{:S(2)}) collective-permute-start(bf16[80,1152]{1,0:T(8,128)(2,1)S(1)} %copy-done.4), channel_id=1, source_target_pairs={{0,4},{2,6},{4,0},{6,2},{1,5},{3,7},{5,1},{7,3},{8,12},{10,14},{12... | collective-permute-start | bytes 552968 | tf_op jit(solution)/shard_map/ppermute | solution.py:379
  27.3 22.8 %collective-permute-start = (bf16[80,1152]{1,0:T(8,128)(2,1)S(1)}, bf16[80,1152]{1,0:T(8,128)(2,1)S(1)}, u32[]{:S(2)}, u32[]{:S(2)}) collective-permute-start(bf16[80,1152]{1,0:T(8,128)(2,1)S(1)} %copy-done.4), channel_id=1, source_target_pairs={{0,6},{2,0},{4,2},{6,4},{1,7},{3,1},{5,3},{7,5},{8,14},{10,8},{12,... | collective-permute-start | bytes 552968 | tf_op jit(solution)/shard_map/ppermute | solution.py:379
  50.1 16.4 %copy-start.5 = (bf16[80,1152]{1,0:T(8,128)(2,1)}, bf16[80,1152]{1,0:T(8,128)(2,1)S(1)}, u32[]{:S(2)}) copy-start(bf16[80,1152]{1,0:T(8,128)(2,1)S(1)} %collective-permute-done) | copy-start | bytes 552964
  50.1 5.2 %collective-permute-start.3 = (bf16[64,8,1536]{2,1,0:T(8,128)(2,1)S(1)}, bf16[64,8,1536]{2,1,0:T(8,128)(2,1)S(1)}, u32[]{:S(2)}, u32[]{:S(2)}) collective-permute-start(bf16[64,8,1536]{2,1,0:T(8,128)(2,1)S(1)} %all-to-all-done.4.own_ref.in_ref), channel_id=1, source_target_pairs={{0,1},{1,0},{2,3},{3,2},{4,5},{5,4},{6,7},{7,6},{8,9},{9,8},{10,11... | collective-permute-start | bytes 4718600 | tf_op jit(solution)/shard_map/ppermute | solution.py:381
  53.6 6.6 %collective-permute-start.6 = (bf16[32,1152]{1,0:T(8,128)(2,1)S(1)}, bf16[32,1152]{1,0:T(8,128)(2,1)S(1)}, u32[]{:S(2)}, u32[]{:S(2)}) collective-permute-start(bf16[32,1152]{1,0:T(8,128)(2,1)S(1)} %get-tuple-element.172), channel_id=1, source_target_pairs={{0,6},{2,0},{4,2},{6,4},{1,7},{3,1},{5,3},{7,5},{8,14},{10,8},{12,... | collective-permute-start | bytes 221192 | tf_op jit(solution)/shard_map/ppermute | solution.py:399
  53.9 6.3 %collective-permute-start.5 = (bf16[32,1152]{1,0:T(8,128)(2,1)S(1)}, bf16[32,1152]{1,0:T(8,128)(2,1)S(1)}, u32[]{:S(2)}, u32[]{:S(2)}) collective-permute-start(bf16[32,1152]{1,0:T(8,128)(2,1)S(1)} %get-tuple-element.173), channel_id=1, source_target_pairs={{0,4},{2,6},{4,0},{6,2},{1,5},{3,7},{5,1},{7,3},{8,12},{10,14},{12... | collective-permute-start | bytes 221192 | tf_op jit(solution)/shard_map/ppermute | solution.py:399
  55.1 5.8 %collective-permute-start.4 = (bf16[32,1152]{1,0:T(8,128)(2,1)S(1)}, bf16[32,1152]{1,0:T(8,128)(2,1)S(1)}, u32[]{:S(2)}, u32[]{:S(2)}) collective-permute-start(bf16[32,1152]{1,0:T(8,128)(2,1)S(1)} %get-tuple-element.174), channel_id=1, source_target_pairs={{0,2},{2,4},{4,6},{6,0},{1,3},{3,5},{5,7},{7,1},{8,10},{10,12},{12... | collective-permute-start | bytes 221192 | tf_op jit(solution)/shard_map/ppermute | solution.py:399
  61.0 2.2 %collective-permute-start.7 = (bf16[112,1152]{1,0:T(8,128)(2,1)S(1)}, bf16[112,1152]{1,0:T(8,128)(2,1)S(1)}, u32[]{:S(2)}, u32[]{:S(2)}) collective-permute-start(bf16[112,1152]{1,0:T(8,128)(2,1)S(1)} %constant_dynamic-update-slice_fusion.own_tail_ref), channel_id=1, source_target_pairs={{0,1},{1,0},{2,3},{3,2},{4,5},{5,4},{6,7},{7,6},{8,9},{9,8},{10,11... | collective-permute-start | bytes 774152 | tf_op jit(solution)/shard_map/ppermute | solution.py:403
  66.6 11.6 %collective-permute-start.8 = (bf16[320,1152]{1,0:T(8,128)(2,1)S(1)}, bf16[320,1152]{1,0:T(8,128)(2,1)S(1)}, u32[]{:S(2)}, u32[]{:S(2)}) collective-permute-start(bf16[320,1152]{1,0:T(8,128)(2,1)S(1)} %pad_maximum_fusion), channel_id=1, source_target_pairs={{0,1},{1,0},{2,3},{3,2},{4,5},{5,4},{6,7},{7,6},{8,9},{9,8},{10,11... | collective-permute-start | bytes 2211848 | tf_op jit(solution)/shard_map/ppermute | solution.py:414
  67.1 22.4 %all-to-all-start.5 = ((f32[64,4,128]{2,1,0:T(4,128)}), f32[64,4,128]{2,1,0:T(4,128)S(1)}, u32[]{:S(2)}, u32[]{:S(2)}) async-start(f32[64,4,128]{2,1,0:T(4,128)} %shard_map.42), calls=%async_computation.5 | async-start | bytes 262144 | tf_op jit(solution)/shard_map/all_to_all | solution.py:415
  78.3 14.3 %copy-start.1 = (s32[1,512]{1,0:T(1,128)S(1)}, s32[1,512]{1,0:T(1,128)}, u32[]{:S(2)}) copy-start(s32[1,512]{1,0:T(1,128)} %get-tuple-element.118.rank_ref) | copy-start | bytes 6148
  78.4 1.8 %copy-start.2 = (bf16[1280,1152]{1,0:T(8,128)(2,1)S(1)}, bf16[1280,1152]{1,0:T(8,128)(2,1)}, u32[]{:S(2)}) copy-start(bf16[1280,1152]{1,0:T(8,128)(2,1)} %all-gather.7.cloned.1.call-done.keys_ref) | copy-start | bytes 8847364
  80.2 13.7 %copy-start.6 = (s32[512]{0:T(512)S(1)}, s32[512]{0:T(512)}, u32[]{:S(2)}) copy-start(s32[512]{0:T(512)} %param.8) | copy-start | bytes 6148
  82.8 4.0 %collective-permute-start.9 = (f32[2,128]{1,0:T(2,128)S(1)}, f32[2,128]{1,0:T(2,128)S(1)}, u32[]{:S(2)}, u32[]{:S(2)}) collective-permute-start(f32[2,128]{1,0:T(2,128)S(1)} %get-tuple-element.177), channel_id=1, source_target_pairs={{0,2},{2,4},{4,6},{6,0},{1,3},{3,5},{5,7},{7,1},{8,10},{10,12},{12... | collective-permute-start | bytes 3080 | tf_op jit(solution)/shard_map/ppermute | solution.py:426
  83.9 3.0 %collective-permute-start.11 = (f32[2,128]{1,0:T(2,128)S(1)}, f32[2,128]{1,0:T(2,128)S(1)}, u32[]{:S(2)}, u32[]{:S(2)}) collective-permute-start(f32[2,128]{1,0:T(2,128)S(1)} %get-tuple-element.178), channel_id=1, source_target_pairs={{0,6},{2,0},{4,2},{6,4},{1,7},{3,1},{5,3},{7,5},{8,14},{10,8},{12,... | collective-permute-start | bytes 3080 | tf_op jit(solution)/shard_map/ppermute | solution.py:426
  85.6 3.9 %collective-permute-start.10 = (f32[2,128]{1,0:T(2,128)S(1)}, f32[2,128]{1,0:T(2,128)S(1)}, u32[]{:S(2)}, u32[]{:S(2)}) collective-permute-start(f32[2,128]{1,0:T(2,128)S(1)} %get-tuple-element.179), channel_id=1, source_target_pairs={{0,4},{2,6},{4,0},{6,2},{1,5},{3,7},{5,1},{7,3},{8,12},{10,14},{12... | collective-permute-start | bytes 3080 | tf_op jit(solution)/shard_map/ppermute | solution.py:426
  89.5 3.0 %collective-permute-start.12 = (f32[4,128]{1,0:T(4,128)S(1)}, f32[4,128]{1,0:T(4,128)S(1)}, u32[]{:S(2)}, u32[]{:S(2)}) collective-permute-start(f32[4,128]{1,0:T(4,128)S(1)} %pad_maximum_fusion.1), channel_id=1, source_target_pairs={{0,1},{1,0},{2,3},{3,2},{4,5},{5,4},{6,7},{7,6},{8,9},{9,8},{10,11... | collective-permute-start | bytes 6152 | tf_op jit(solution)/shard_map/ppermute | solution.py:429
  94.0 0.6 copy-start.7
Sparse Core Ops, SparseCore 0:
  26.1 50.7 all-gather.6

commit v7 on v6

--- a/solution.py
+++ b/solution.py
@@ -166,12 +166,12 @@
 
 def fields_of(ref):
     block = ref[:, :, FEAT : FEAT + FIELD_LANES].reshape(SLOTS, FIELD_LANES)
-    spread = mm(hot(iota((SLOTS, SLOTS), 1) == (iota((SLOTS, SLOTS), 0) >> 3) * 8 + FIELD_ROW), block)
+    block = mm(hot(iota((CHIPS, SLOTS), 1) == iota((CHIPS, SLOTS), 0) * 8 + FIELD_ROW), block).astype(bf16)
+    spread = mm(hot(iota((SLOTS, CHIPS), 1) == iota((SLOTS, CHIPS), 0) >> 3), block)
     place, group = iota((SLOTS, FIELD_LANES), 0) & 7, iota((SLOTS, FIELD_LANES), 1) >> 4
-    whole = jnp.where(group == place, spread, 0.0).astype(bf16)
-    half = jnp.where(group == place + 8, spread, 0.0).astype(bf16)
-    source, lane = iota((FIELD_LANES, META), 0) & 15, iota((FIELD_LANES, META), 1)
-    return (mm(whole, hot(source == lane)) + mm(half, hot(source == lane - FIELDS))).astype(bf16)
+    kept = jnp.where((group & 7) == place, spread, 0.0).astype(bf16)
+    source, lane = iota((FIELD_LANES, META), 0), iota((FIELD_LANES, META), 1)
+    return mm(kept, hot((source & 15) + FIELDS * (source >> 7) == lane)).astype(bf16)
 
 
 def shifted(step):
@@ -179,9 +179,10 @@
     return hot((iota((META, META), 0) == lanes + step) & (lanes < FIELDS))
 
 
-def fix_kernel(y_ref, flag_in_ref, in_ref, fix_ref, flag_ref):
+def fix_kernel(y_ref, flag_in_ref, in_ref, fix_ref, flag_ref, meta_ref):
     half = FEAT // 2
     meta = fields_of(in_ref)
+    meta_ref[...] = meta
     turn = hot(iota((2 * FIELDS, META), 0) == iota((2 * FIELDS, META), 1))
     rows = mm_t(turn, meta)
     earlier = hot(iota((SLOTS, SLOTS), 0) < iota((SLOTS, SLOTS), 1))
@@ -271,13 +272,13 @@
     return jnp.where(spread[:CHIPS] > 0.5, value, -1.0)
 
 
-def main_kernel(own_ref, other_ref, keys_ref, metas_ref, best_ref):
+def main_kernel(own_ref, own_meta_ref, other_ref, keys_ref, metas_ref, best_ref):
     half = FEAT // 2
     first, second = selections()
     for k, ref in enumerate((own_ref, other_ref)):
         at = slice(k * MAIN, k * MAIN + SLOTS)
         keys_ref[at, :] = ref[:, :, :FEAT].reshape(SLOTS, FEAT)
-        meta = fields_of(ref)
+        meta = own_meta_ref[...] if k == 0 else fields_of(ref)
         metas_ref[at, :] = meta
         at = slice(k * MAIN + SLOTS, (k + 1) * MAIN)
         halves = ref[:, :, FEAT : FEAT + half].reshape(SLOTS, half)
@@ -379,9 +380,9 @@
     along = [box] + [lax.ppermute(box, "y", [(i, (i - d) % 4) for i in range(4)]) for d in (1, 2, 3)]
     inbox, *along = lax.optimization_barrier((inbox, *along))
     other = lax.ppermute(inbox, "core", swap)
-    fix, flag_block = call(
+    fix, flag_block, own_meta = call(
         fix_kernel,
-        (shape((3 * FIX, NARROW), bf16), shape((FLAG_ROWS, NARROW), bf16)),
+        (shape((3 * FIX, NARROW), bf16), shape((FLAG_ROWS, NARROW), bf16), shape((SLOTS, META), bf16)),
         (y[None].astype(i32), flag, inbox),
         (SMEM, VMEM, VMEM),
         flops=2 * 100_000_000,
@@ -390,8 +391,8 @@
     keys, metas, best = call(
         main_kernel,
         (shape((2 * MAIN, FEAT), bf16), shape((2 * MAIN, META), bf16), shape((8, MAIN), f32)),
-        (inbox, other),
-        (VMEM, VMEM),
+        (inbox, own_meta, other),
+        (VMEM, VMEM, VMEM),
         flops=2 * 1_400_000_000,
         bytes_accessed=7_000_000,
     )
@@ -434,7 +435,7 @@
         (VMEM, VMEM, VMEM),
         outs=(pl.BlockSpec(memory_space=VMEM), pl.BlockSpec(memory_space=SMEM)),
     )
-    return out[0], worst[0] > 0
+    return out[0], worst[0]
 
 
 def inverse_norms(row_values):
@@ -482,7 +483,7 @@
 
 def local(embeddings, clusters, order):
     out, overflow = fast(embeddings, clusters, order)
-    return lax.cond(overflow, lambda: general(embeddings, clusters, order), lambda: out)
+    return lax.switch(overflow, [lambda: out, lambda: general(embeddings, clusters, order)])
 
 
 def solution(mesh):

time: 102 us -> 101 us (level)
  no operation moved by 1% of the time
where the time goes in v7:
time: 101 us
  starting transfers between devices  37.5 us (37%)
  waiting for transfers between devices  28.3 us (28%)
  Pallas kernels  16.8 us (17%)
  between operations  14.3 us (14%)
  local copies, waits for them, and re-layouts  3.63 us (4%)
    ppermute x3, waiting for transfers between devices, fast(): lax.ppermute(box, 'y', [(i, (i - d) % 4) for i in range(4)])  21.6 us
    pallas_call x6, Pallas kernels, call(): pl.pallas_call(kernel, out_shape=shapes, in_specs=[pl.BlockSpec(memory_sp...  16.8 us
    all_to_all x1, starting transfers between devices, fast(): lax.all_to_all(outbox, CHIP_AXES, split_axis=0, concat_axis=0, tiled=True)  12.1 us
    all_to_all x1, starting transfers between devices, fast(): lax.all_to_all(spread, CHIP_AXES, split_axis=0, concat_axis=0, tiled=True)  9.4 us
    ppermute x3, starting transfers between devices, fast(): lax.ppermute(box, 'y', [(i, (i - d) % 4) for i in range(4)])  4.66 us
    ppermute x3, starting transfers between devices, fast(): lax.ppermute(partial[2 * d:2 * d + 2], 'y', [(i, (i + d) % 4) for i in ra...  4.04 us
    unnamed x21, local copies, waits for them, and re-layouts  3.46 us
    ppermute x3, waiting for transfers between devices, fast(): lax.ppermute(partial[2 * d:2 * d + 2], 'y', [(i, (i + d) % 4) for i in ra...  2.6 us
  transfers between devices with their start and end apart: 16, of which 6 were waited for; matrix products, arithmetic and copies ran while one was open for 1% of the time, Pallas kernels for 12%

profile of v7, /device:TPU:1, one launch (start us, length us, event | category | flops | bytes accessed | tf_op | source)
XLA Modules:
  0.0 100.6 jit_solution(805141248032576081)
XLA Ops:
  6.5 4.4 %shard_map.39 = (bf16[64,8,1536]{2,1,0:T(8,128)(2,1)}, bf16[80,1152]{1,0:T(8,128)(2,1)}, s32[1,512]{1,0:T(1,128)}, f32[8,128]{1,0:T(8,128)}) custom-call(s32[1]{0:T(128)} %bitcast.7.chip_ref, bf16[512,1024]{1,0:T(8,128)(2,1)} %emb_hbm.1, s32[1,512]{1,0:T(1,128)} %bitcast.71, s32[1,512]{1,0:T(1,128)} %bitcast.72), custom_call_target="tpu_custom_call" | custom-call | flops 1400000000 | bytes 3000000 | tf_op jit(solution)/shard_map/pallas_call | solution.py:339
  10.9 0.0 copy-start.4
  11.0 0.0 copy-start
  11.0 12.1 %all-to-all-start.4 = ((bf16[64,8,1536]{2,1,0:T(8,128)(2,1)}), bf16[64,8,1536]{2,1,0:T(8,128)(2,1)S(1)}, u32[]{:S(2)}, u32[]{:S(2)}) async-start(bf16[64,8,1536]{2,1,0:T(8,128)(2,1)} %get-tuple-element.96), calls=%async_computation.4 | async-start | bytes 3145728 | tf_op jit(solution)/shard_map/all_to_all | solution.py:378
  23.1 0.0 all-gather.7.cloned.1.call-start
  23.1 0.7 all-gather.7.cloned.1.call-update
  23.8 0.0 copy-done.4
  23.8 1.1 %collective-permute-start.2 = (bf16[80,1152]{1,0:T(8,128)(2,1)S(1)}, bf16[80,1152]{1,0:T(8,128)(2,1)S(1)}, u32[]{:S(2)}, u32[]{:S(2)}) collective-permute-start(bf16[80,1152]{1,0:T(8,128)(2,1)S(1)} %copy-done.4), channel_id=1, source_target_pairs={{0,2},{2,4},{4,6},{6,0},{1,3},{3,5},{5,7},{7,1},{8,10},{10,12},{12... | collective-permute-start | bytes 552968 | tf_op jit(solution)/shard_map/ppermute | solution.py:380
  24.9 2.4 %collective-permute-start.1 = (bf16[80,1152]{1,0:T(8,128)(2,1)S(1)}, bf16[80,1152]{1,0:T(8,128)(2,1)S(1)}, u32[]{:S(2)}, u32[]{:S(2)}) collective-permute-start(bf16[80,1152]{1,0:T(8,128)(2,1)S(1)} %copy-done.4), channel_id=1, source_target_pairs={{0,4},{2,6},{4,0},{6,2},{1,5},{3,7},{5,1},{7,3},{8,12},{10,14},{12... | collective-permute-start | bytes 552968 | tf_op jit(solution)/shard_map/ppermute | solution.py:380
  27.3 1.2 %collective-permute-start = (bf16[80,1152]{1,0:T(8,128)(2,1)S(1)}, bf16[80,1152]{1,0:T(8,128)(2,1)S(1)}, u32[]{:S(2)}, u32[]{:S(2)}) collective-permute-start(bf16[80,1152]{1,0:T(8,128)(2,1)S(1)} %copy-done.4), channel_id=1, source_target_pairs={{0,6},{2,0},{4,2},{6,4},{1,7},{3,1},{5,3},{7,5},{8,14},{10,8},{12,... | collective-permute-start | bytes 552968 | tf_op jit(solution)/shard_map/ppermute | solution.py:380
  28.5 18.3 %collective-permute-done.2 = bf16[80,1152]{1,0:T(8,128)(2,1)S(1)} collective-permute-done((bf16[80,1152]{1,0:T(8,128)(2,1)S(1)}, bf16[80,1152]{1,0:T(8,128)(2,1)S(1)}, u32[]{:S(2)}, u32[]{:S(2)}) %collective-permute-start.2) | collective-permute-done | bytes 184352 | tf_op jit(solution)/shard_map/ppermute | solution.py:380
  46.8 3.3 %collective-permute-done.1 = bf16[80,1152]{1,0:T(8,128)(2,1)S(1)} collective-permute-done((bf16[80,1152]{1,0:T(8,128)(2,1)S(1)}, bf16[80,1152]{1,0:T(8,128)(2,1)S(1)}, u32[]{:S(2)}, u32[]{:S(2)}) %collective-permute-start.1) | collective-permute-done | bytes 184352 | tf_op jit(solution)/shard_map/ppermute | solution.py:380
  50.1 0.0 collective-permute-done
  50.1 0.0 copy-start.5
  50.1 0.0 all-to-all-done.4.in_ref.own_ref
  50.1 1.8 %collective-permute-start.3 = (bf16[64,8,1536]{2,1,0:T(8,128)(2,1)S(1)}, bf16[64,8,1536]{2,1,0:T(8,128)(2,1)S(1)}, u32[]{:S(2)}, u32[]{:S(2)}) collective-permute-start(bf16[64,8,1536]{2,1,0:T(8,128)(2,1)S(1)} %all-to-all-done.4.in_ref.own_ref), channel_id=1, source_target_pairs={{0,1},{1,0},{2,3},{3,2},{4,5},{5,4},{6,7},{7,6},{8,9},{9,8},{10,11... | collective-permute-start | bytes 4718600 | tf_op jit(solution)/shard_map/ppermute | solution.py:382
  51.9 0.0 copy-done
  51.9 1.6 %shard_map.40 = (bf16[96,1152]{1,0:T(8,128)(2,1)S(1)}, bf16[16,1152]{1,0:T(8,128)(2,1)S(1)}, bf16[512,128]{1,0:T(8,128)(2,1)S(1)}) custom-call(s32[1]{0:T(128)} %bitcast.10.y_ref, f32[8,128]{1,0:T(8,128)S(1)} %copy-done, bf16[64,8,1536]{2,1,0:T(8,128)(2,1)S(1)} %all-to-all-done.4.in_ref.own_ref), custom_call_target="tpu_custom_call" | custom-call | flops 200000000 | bytes 2000000 | tf_op jit(solution)/shard_map/pallas_call | solution.py:339
  53.5 0.3 collective-permute-start.6
  53.9 1.2 %collective-permute-start.5 = (bf16[32,1152]{1,0:T(8,128)(2,1)S(1)}, bf16[32,1152]{1,0:T(8,128)(2,1)S(1)}, u32[]{:S(2)}, u32[]{:S(2)}) collective-permute-start(bf16[32,1152]{1,0:T(8,128)(2,1)S(1)} %get-tuple-element.175), channel_id=1, source_target_pairs={{0,4},{2,6},{4,0},{6,2},{1,5},{3,7},{5,1},{7,3},{8,12},{10,14},{12... | collective-permute-start | bytes 221192 | tf_op jit(solution)/shard_map/ppermute | solution.py:400
  55.0 0.2 collective-permute-start.4
  55.3 0.0 collective-permute-done.3.other_ref
  55.3 4.2 %shard_map.41 = (bf16[1536,1024]{1,0:T(8,128)(2,1)S(1)}, bf16[1536,128]{1,0:T(8,128)(2,1)S(1)}, f32[8,768]{1,0:T(8,128)S(1)}) custom-call(bf16[64,8,1536]{2,1,0:T(8,128)(2,1)S(1)} %all-to-all-done.4.in_ref.own_ref, bf16[512,128]{1,0:T(8,128)(2,1)S(1)} %get-tuple-element.99.own_meta_ref, bf16[64,8,1536]{2,1,0:T(8,128)(2,1)S(1)} %collective-permute-done.3.other_ref), custom_call_target="tpu_custom_call" | custom-call | flops 2800000000 | bytes 7000000 | tf_op jit(solution)/shard_map/pallas_call | solution.py:339
  59.5 0.0 collective-permute-done.6
  59.5 0.0 collective-permute-done.5
  59.5 1.4 %collective-permute-done.4 = bf16[32,1152]{1,0:T(8,128)(2,1)S(1)} collective-permute-done((bf16[32,1152]{1,0:T(8,128)(2,1)S(1)}, bf16[32,1152]{1,0:T(8,128)(2,1)S(1)}, u32[]{:S(2)}, u32[]{:S(2)}) %collective-permute-start.4) | collective-permute-done | bytes 73760 | tf_op jit(solution)/shard_map/ppermute | solution.py:400
  60.9 1.0 %collective-permute-start.7 = (bf16[112,1152]{1,0:T(8,128)(2,1)S(1)}, bf16[112,1152]{1,0:T(8,128)(2,1)S(1)}, u32[]{:S(2)}, u32[]{:S(2)}) collective-permute-start(bf16[112,1152]{1,0:T(8,128)(2,1)S(1)} %constant_dynamic-update-slice_fusion.own_tail_ref), channel_id=1, source_target_pairs={{0,1},{1,0},{2,3},{3,2},{4,5},{5,4},{6,7},{7,6},{8,9},{9,8},{10,11... | collective-permute-start | bytes 774152 | tf_op jit(solution)/shard_map/ppermute | solution.py:404
  61.9 1.2 %collective-permute-done.7.other_tail_ref = bf16[112,1152]{1,0:T(8,128)(2,1)S(1)} collective-permute-done((bf16[112,1152]{1,0:T(8,128)(2,1)S(1)}, bf16[112,1152]{1,0:T(8,128)(2,1)S(1)}, u32[]{:S(2)}, u32[]{:S(2)}) %collective-permute-start.7) | collective-permute-done | bytes 258080 | tf_op jit(solution)/shard_map/ppermute | solution.py:404
  63.1 3.4 %shard_map.42 = f32[64,4,128]{2,1,0:T(4,128)} custom-call(bf16[1536,1024]{1,0:T(8,128)(2,1)S(1)} %get-tuple-element.100.keys_ref, bf16[1536,128]{1,0:T(8,128)(2,1)S(1)} %get-tuple-element.101.metas_ref, f32[8,768]{1,0:T(8,128)S(1)} %get-tuple-element.104.best_ref, bf16[112,1152]{1,0:T(8,128)(2,1)S(1)} %constant_dynamic-update-slice_fusion.own_tail_ref, ...), custom_call_target="tpu_custom_call" | custom-call | flops 1000000000 | bytes 4000000 | tf_op jit(solution)/shard_map/pallas_call | solution.py:339
  66.5 0.0 copy-done.5
  66.5 0.1 pad_maximum_fusion
  66.5 0.4 collective-permute-start.8
  67.0 9.4 %all-to-all-start.5 = ((f32[64,4,128]{2,1,0:T(4,128)}), f32[64,4,128]{2,1,0:T(4,128)S(1)}, u32[]{:S(2)}, u32[]{:S(2)}) async-start(f32[64,4,128]{2,1,0:T(4,128)} %shard_map.42), calls=%async_computation.5 | async-start | bytes 262144 | tf_op jit(solution)/shard_map/all_to_all | solution.py:416
  76.4 0.9 constant_dynamic-update-slice_fusion.7
  77.4 0.0 collective-permute-done.8
  77.4 0.1 constant_dynamic-update-slice_fusion.4.queries_ref
  77.5 0.0 copy-start.1
  77.5 0.0 all-gather.7.cloned.1.call-done.keys_ref
  77.6 0.0 copy-start.2
  77.6 1.8 %copy-done.2 = bf16[1280,1152]{1,0:T(8,128)(2,1)S(1)} copy-done((bf16[1280,1152]{1,0:T(8,128)(2,1)S(1)}, bf16[1280,1152]{1,0:T(8,128)(2,1)}, u32[]{:S(2)}) %copy-start.2) | copy-done | bytes 2949144
  79.4 0.0 copy-start.6
  79.4 2.6 %shard_map.43 = f32[8,128]{1,0:T(8,128)S(1)} custom-call(bf16[1280,1152]{1,0:T(8,128)(2,1)S(1)} %copy-done.2, bf16[640,1152]{1,0:T(8,128)(2,1)S(1)} %constant_dynamic-update-slice_fusion.4.queries_ref), custom_call_target="tpu_custom_call" | custom-call | flops 1800000000 | bytes 4500000 | tf_op jit(solution)/shard_map/pallas_call | solution.py:339
  82.0 1.1 %collective-permute-start.9 = (f32[2,128]{1,0:T(2,128)S(1)}, f32[2,128]{1,0:T(2,128)S(1)}, u32[]{:S(2)}, u32[]{:S(2)}) collective-permute-start(f32[2,128]{1,0:T(2,128)S(1)} %get-tuple-element.179), channel_id=1, source_target_pairs={{0,2},{2,4},{4,6},{6,0},{1,3},{3,5},{5,7},{7,1},{8,10},{10,12},{12... | collective-permute-start | bytes 3080 | tf_op jit(solution)/shard_map/ppermute | solution.py:427
  83.1 1.7 %collective-permute-start.11 = (f32[2,128]{1,0:T(2,128)S(1)}, f32[2,128]{1,0:T(2,128)S(1)}, u32[]{:S(2)}, u32[]{:S(2)}) collective-permute-start(f32[2,128]{1,0:T(2,128)S(1)} %get-tuple-element.180), channel_id=1, source_target_pairs={{0,6},{2,0},{4,2},{6,4},{1,7},{3,1},{5,3},{7,5},{8,14},{10,8},{12,... | collective-permute-start | bytes 3080 | tf_op jit(solution)/shard_map/ppermute | solution.py:427
  84.8 1.3 %collective-permute-start.10 = (f32[2,128]{1,0:T(2,128)S(1)}, f32[2,128]{1,0:T(2,128)S(1)}, u32[]{:S(2)}, u32[]{:S(2)}) collective-permute-start(f32[2,128]{1,0:T(2,128)S(1)} %get-tuple-element.181), channel_id=1, source_target_pairs={{0,4},{2,6},{4,0},{6,2},{1,5},{3,7},{5,1},{7,3},{8,12},{10,14},{12... | collective-permute-start | bytes 3080 | tf_op jit(solution)/shard_map/ppermute | solution.py:427
  86.1 0.0 collective-permute-done.9
  86.1 0.0 collective-permute-done.11
  86.1 2.6 %collective-permute-done.10 = f32[2,128]{1,0:T(2,128)S(1)} collective-permute-done((f32[2,128]{1,0:T(2,128)S(1)}, f32[2,128]{1,0:T(2,128)S(1)}, u32[]{:S(2)}, u32[]{:S(2)}) %collective-permute-start.10) | collective-permute-done | bytes 1056 | tf_op jit(solution)/shard_map/ppermute | solution.py:427
  88.7 0.0 all-to-all-done.5.spread_ref
  88.7 2.2 %collective-permute-start.12 = (f32[4,128]{1,0:T(4,128)S(1)}, f32[4,128]{1,0:T(4,128)S(1)}, u32[]{:S(2)}, u32[]{:S(2)}) collective-permute-start(f32[4,128]{1,0:T(4,128)S(1)} %pad_maximum_fusion.1), channel_id=1, source_target_pairs={{0,1},{1,0},{2,3},{3,2},{4,5},{5,4},{6,7},{7,6},{8,9},{9,8},{10,11... | collective-permute-start | bytes 6152 | tf_op jit(solution)/shard_map/ppermute | solution.py:430
  91.0 0.8 collective-permute-done.12
  91.8 0.0 copy-done.1
  91.8 0.7 shard_map.44
  93.1 0.0 copy-done.6
  93.2 0.0 copy-start.7
  93.2 0.6 copy-done.7
  (16 shorter events, 0.2 us)
Async XLA Ops:
  10.9 12.9 %copy-start.4 = (bf16[80,1152]{1,0:T(8,128)(2,1)S(1)}, bf16[80,1152]{1,0:T(8,128)(2,1)}, u32[]{:S(2)}) copy-start(bf16[80,1152]{1,0:T(8,128)(2,1)} %get-tuple-element.113) | copy-start | bytes 552964
  11.0 41.0 %copy-start = (f32[8,128]{1,0:T(8,128)S(1)}, f32[8,128]{1,0:T(8,128)}, u32[]{:S(2)}) copy-start(f32[8,128]{1,0:T(8,128)} %get-tuple-element.98.flag_in_ref) | copy-start | bytes 12292
  11.0 39.2 %all-to-all-start.4 = ((bf16[64,8,1536]{2,1,0:T(8,128)(2,1)}), bf16[64,8,1536]{2,1,0:T(8,128)(2,1)S(1)}, u32[]{:S(2)}, u32[]{:S(2)}) async-start(bf16[64,8,1536]{2,1,0:T(8,128)(2,1)} %get-tuple-element.96), calls=%async_computation.4 | async-start | bytes 3145728 | tf_op jit(solution)/shard_map/all_to_all | solution.py:378
  23.1 54.5 %all-gather.7.cloned.1.call-start = ((), (), s32[]{:S(2)}) async-start(), calls=%async_computation.7 | async-start | bytes 3133440 | tf_op jit(solution)/shard_map/all_gather | solution.py:377
  23.8 23.0 %collective-permute-start.2 = (bf16[80,1152]{1,0:T(8,128)(2,1)S(1)}, bf16[80,1152]{1,0:T(8,128)(2,1)S(1)}, u32[]{:S(2)}, u32[]{:S(2)}) collective-permute-start(bf16[80,1152]{1,0:T(8,128)(2,1)S(1)} %copy-done.4), channel_id=1, source_target_pairs={{0,2},{2,4},{4,6},{6,0},{1,3},{3,5},{5,7},{7,1},{8,10},{10,12},{12... | collective-permute-start | bytes 552968 | tf_op jit(solution)/shard_map/ppermute | solution.py:380
  24.9 25.2 %collective-permute-start.1 = (bf16[80,1152]{1,0:T(8,128)(2,1)S(1)}, bf16[80,1152]{1,0:T(8,128)(2,1)S(1)}, u32[]{:S(2)}, u32[]{:S(2)}) collective-permute-start(bf16[80,1152]{1,0:T(8,128)(2,1)S(1)} %copy-done.4), channel_id=1, source_target_pairs={{0,4},{2,6},{4,0},{6,2},{1,5},{3,7},{5,1},{7,3},{8,12},{10,14},{12... | collective-permute-start | bytes 552968 | tf_op jit(solution)/shard_map/ppermute | solution.py:380
  27.3 22.8 %collective-permute-start = (bf16[80,1152]{1,0:T(8,128)(2,1)S(1)}, bf16[80,1152]{1,0:T(8,128)(2,1)S(1)}, u32[]{:S(2)}, u32[]{:S(2)}) collective-permute-start(bf16[80,1152]{1,0:T(8,128)(2,1)S(1)} %copy-done.4), channel_id=1, source_target_pairs={{0,6},{2,0},{4,2},{6,4},{1,7},{3,1},{5,3},{7,5},{8,14},{10,8},{12,... | collective-permute-start | bytes 552968 | tf_op jit(solution)/shard_map/ppermute | solution.py:380
  50.1 16.4 %copy-start.5 = (bf16[80,1152]{1,0:T(8,128)(2,1)}, bf16[80,1152]{1,0:T(8,128)(2,1)S(1)}, u32[]{:S(2)}) copy-start(bf16[80,1152]{1,0:T(8,128)(2,1)S(1)} %collective-permute-done) | copy-start | bytes 552964
  50.1 5.1 %collective-permute-start.3 = (bf16[64,8,1536]{2,1,0:T(8,128)(2,1)S(1)}, bf16[64,8,1536]{2,1,0:T(8,128)(2,1)S(1)}, u32[]{:S(2)}, u32[]{:S(2)}) collective-permute-start(bf16[64,8,1536]{2,1,0:T(8,128)(2,1)S(1)} %all-to-all-done.4.in_ref.own_ref), channel_id=1, source_target_pairs={{0,1},{1,0},{2,3},{3,2},{4,5},{5,4},{6,7},{7,6},{8,9},{9,8},{10,11... | collective-permute-start | bytes 4718600 | tf_op jit(solution)/shard_map/ppermute | solution.py:382
  53.5 6.0 %collective-permute-start.6 = (bf16[32,1152]{1,0:T(8,128)(2,1)S(1)}, bf16[32,1152]{1,0:T(8,128)(2,1)S(1)}, u32[]{:S(2)}, u32[]{:S(2)}) collective-permute-start(bf16[32,1152]{1,0:T(8,128)(2,1)S(1)} %get-tuple-element.174), channel_id=1, source_target_pairs={{0,6},{2,0},{4,2},{6,4},{1,7},{3,1},{5,3},{7,5},{8,14},{10,8},{12,... | collective-permute-start | bytes 221192 | tf_op jit(solution)/shard_map/ppermute | solution.py:400
  53.9 5.6 %collective-permute-start.5 = (bf16[32,1152]{1,0:T(8,128)(2,1)S(1)}, bf16[32,1152]{1,0:T(8,128)(2,1)S(1)}, u32[]{:S(2)}, u32[]{:S(2)}) collective-permute-start(bf16[32,1152]{1,0:T(8,128)(2,1)S(1)} %get-tuple-element.175), channel_id=1, source_target_pairs={{0,4},{2,6},{4,0},{6,2},{1,5},{3,7},{5,1},{7,3},{8,12},{10,14},{12... | collective-permute-start | bytes 221192 | tf_op jit(solution)/shard_map/ppermute | solution.py:400
  55.0 5.8 %collective-permute-start.4 = (bf16[32,1152]{1,0:T(8,128)(2,1)S(1)}, bf16[32,1152]{1,0:T(8,128)(2,1)S(1)}, u32[]{:S(2)}, u32[]{:S(2)}) collective-permute-start(bf16[32,1152]{1,0:T(8,128)(2,1)S(1)} %get-tuple-element.176), channel_id=1, source_target_pairs={{0,2},{2,4},{4,6},{6,0},{1,3},{3,5},{5,7},{7,1},{8,10},{10,12},{12... | collective-permute-start | bytes 221192 | tf_op jit(solution)/shard_map/ppermute | solution.py:400
  60.9 2.2 %collective-permute-start.7 = (bf16[112,1152]{1,0:T(8,128)(2,1)S(1)}, bf16[112,1152]{1,0:T(8,128)(2,1)S(1)}, u32[]{:S(2)}, u32[]{:S(2)}) collective-permute-start(bf16[112,1152]{1,0:T(8,128)(2,1)S(1)} %constant_dynamic-update-slice_fusion.own_tail_ref), channel_id=1, source_target_pairs={{0,1},{1,0},{2,3},{3,2},{4,5},{5,4},{6,7},{7,6},{8,9},{9,8},{10,11... | collective-permute-start | bytes 774152 | tf_op jit(solution)/shard_map/ppermute | solution.py:404
  66.5 10.9 %collective-permute-start.8 = (bf16[320,1152]{1,0:T(8,128)(2,1)S(1)}, bf16[320,1152]{1,0:T(8,128)(2,1)S(1)}, u32[]{:S(2)}, u32[]{:S(2)}) collective-permute-start(bf16[320,1152]{1,0:T(8,128)(2,1)S(1)} %pad_maximum_fusion), channel_id=1, source_target_pairs={{0,1},{1,0},{2,3},{3,2},{4,5},{5,4},{6,7},{7,6},{8,9},{9,8},{10,11... | collective-permute-start | bytes 2211848 | tf_op jit(solution)/shard_map/ppermute | solution.py:415
  67.0 21.7 %all-to-all-start.5 = ((f32[64,4,128]{2,1,0:T(4,128)}), f32[64,4,128]{2,1,0:T(4,128)S(1)}, u32[]{:S(2)}, u32[]{:S(2)}) async-start(f32[64,4,128]{2,1,0:T(4,128)} %shard_map.42), calls=%async_computation.5 | async-start | bytes 262144 | tf_op jit(solution)/shard_map/all_to_all | solution.py:416
  77.5 14.3 %copy-start.1 = (s32[1,512]{1,0:T(1,128)S(1)}, s32[1,512]{1,0:T(1,128)}, u32[]{:S(2)}) copy-start(s32[1,512]{1,0:T(1,128)} %get-tuple-element.120.rank_ref) | copy-start | bytes 6148
  77.6 1.8 %copy-start.2 = (bf16[1280,1152]{1,0:T(8,128)(2,1)S(1)}, bf16[1280,1152]{1,0:T(8,128)(2,1)}, u32[]{:S(2)}) copy-start(bf16[1280,1152]{1,0:T(8,128)(2,1)} %all-gather.7.cloned.1.call-done.keys_ref) | copy-start | bytes 8847364
  79.4 13.7 %copy-start.6 = (s32[512]{0:T(512)S(1)}, s32[512]{0:T(512)}, u32[]{:S(2)}) copy-start(s32[512]{0:T(512)} %param.8) | copy-start | bytes 6148
  82.0 4.0 %collective-permute-start.9 = (f32[2,128]{1,0:T(2,128)S(1)}, f32[2,128]{1,0:T(2,128)S(1)}, u32[]{:S(2)}, u32[]{:S(2)}) collective-permute-start(f32[2,128]{1,0:T(2,128)S(1)} %get-tuple-element.179), channel_id=1, source_target_pairs={{0,2},{2,4},{4,6},{6,0},{1,3},{3,5},{5,7},{7,1},{8,10},{10,12},{12... | collective-permute-start | bytes 3080 | tf_op jit(solution)/shard_map/ppermute | solution.py:427
  83.1 3.0 %collective-permute-start.11 = (f32[2,128]{1,0:T(2,128)S(1)}, f32[2,128]{1,0:T(2,128)S(1)}, u32[]{:S(2)}, u32[]{:S(2)}) collective-permute-start(f32[2,128]{1,0:T(2,128)S(1)} %get-tuple-element.180), channel_id=1, source_target_pairs={{0,6},{2,0},{4,2},{6,4},{1,7},{3,1},{5,3},{7,5},{8,14},{10,8},{12,... | collective-permute-start | bytes 3080 | tf_op jit(solution)/shard_map/ppermute | solution.py:427
  84.8 3.9 %collective-permute-start.10 = (f32[2,128]{1,0:T(2,128)S(1)}, f32[2,128]{1,0:T(2,128)S(1)}, u32[]{:S(2)}, u32[]{:S(2)}) collective-permute-start(f32[2,128]{1,0:T(2,128)S(1)} %get-tuple-element.181), channel_id=1, source_target_pairs={{0,4},{2,6},{4,0},{6,2},{1,5},{3,7},{5,1},{7,3},{8,12},{10,14},{12... | collective-permute-start | bytes 3080 | tf_op jit(solution)/shard_map/ppermute | solution.py:427
  88.7 3.0 %collective-permute-start.12 = (f32[4,128]{1,0:T(4,128)S(1)}, f32[4,128]{1,0:T(4,128)S(1)}, u32[]{:S(2)}, u32[]{:S(2)}) collective-permute-start(f32[4,128]{1,0:T(4,128)S(1)} %pad_maximum_fusion.1), channel_id=1, source_target_pairs={{0,1},{1,0},{2,3},{3,2},{4,5},{5,4},{6,7},{7,6},{8,9},{9,8},{10,11... | collective-permute-start | bytes 6152 | tf_op jit(solution)/shard_map/ppermute | solution.py:430
  93.2 0.6 copy-start.7
Sparse Core Ops, SparseCore 0:
  26.1 50.7 all-gather.6

commit v8 on v7

--- a/solution.py
+++ b/solution.py
@@ -320,11 +320,14 @@
         out_ref[at : at + 1, :CAP] = best[:, k * CAP : (k + 1) * CAP]
 
 
-def last_kernel(spread_ref, busy_ref, rank_ref, out_ref, flag_ref):
+def owned_kernel(spread_ref, out_ref, flag_ref):
     best = jnp.max(spread_ref[...], axis=0)
     worst = jnp.max(jnp.max(best, axis=0, keepdims=True), axis=1, keepdims=True)
     flag_ref[0] = jnp.where(jnp.max(worst) > 2.0, 1, 0)
-    owned = jnp.concatenate([best[k : k + 1] for k in range(ROW_DEV // META)], axis=1)
+    out_ref[...] = jnp.concatenate([best[k : k + 1] for k in range(ROW_DEV // META)], axis=1)
+
+
+def last_kernel(owned_ref, busy_ref, rank_ref, out_ref):
     busy = jnp.max(busy_ref[...], axis=0, keepdims=True)
     high, middle, low = pieces(busy)
     parts = jnp.concatenate([high.astype(f32), middle.astype(f32), low.astype(f32), jnp.zeros((5, META), f32)], axis=0)
@@ -332,7 +335,7 @@
     pick = hot(iota((META, ROW_DEV), 0) == rank)
     taken = mm(parts.astype(bf16), pick)
     value = taken[0:1] + taken[1:2] + taken[2:3]
-    out_ref[...] = jnp.where(rank >= 0, value, owned)
+    out_ref[...] = jnp.where(rank >= 0, value, owned_ref[...])
 
 
 def call(kernel, shapes, args, specs, scratch=(), flops=0, bytes_accessed=0, vmem=28, outs=None):
@@ -428,13 +431,14 @@
     to_other = jnp.concatenate([part[1:] for part in parts], axis=0)
     to_other, returned = lax.optimization_barrier((to_other, returned))
     busy = jnp.concatenate([part[:1] for part in parts] + [lax.ppermute(to_other, "core", swap)], axis=0)
-    out, worst = call(
-        last_kernel,
+    owned, worst = call(
+        owned_kernel,
         (shape((1, ROW_DEV), f32), shape((1,), i32)),
-        (returned, busy, rank),
-        (VMEM, VMEM, VMEM),
+        (returned,),
+        (VMEM,),
         outs=(pl.BlockSpec(memory_space=VMEM), pl.BlockSpec(memory_space=SMEM)),
     )
+    out = call(last_kernel, shape((1, ROW_DEV), f32), (owned, busy, rank), (VMEM, VMEM, VMEM))
     return out[0], worst[0]
 
 

time: 101 us -> 100 us (0.990)
    pallas_call x6 -> x7, Pallas kernels: 16.8 us -> 17 us  [call(): pl.pallas_call(kernel, out_shape=shapes, in_specs=[pl.BlockSpec(memory_sp...]
  transfers between devices with their start and end apart: 16 -> 16, of which waited for: 6 -> 5; matrix products, arithmetic and copies ran while one was open for 1% -> 1% of each run, Pallas kernels for 12% -> 12%
where the time goes in v8:
time: 100 us; the launch traced here: 99.9 us
  starting transfers between devices  37.5 us (38%)
  waiting for transfers between devices  27.5 us (28%)
  Pallas kernels  17 us (17%)
  between operations  14.3 us (14%)
  local copies, waits for them, and re-layouts  3.63 us (4%)
    ppermute x3, waiting for transfers between devices, fast(): lax.ppermute(box, 'y', [(i, (i - d) % 4) for i in range(4)])  21.6 us
    pallas_call x7, Pallas kernels, call(): pl.pallas_call(kernel, out_shape=shapes, in_specs=[pl.BlockSpec(memory_sp...  17 us
    all_to_all x1, starting transfers between devices, fast(): lax.all_to_all(outbox, CHIP_AXES, split_axis=0, concat_axis=0, tiled=True)  12.1 us
    all_to_all x1, starting transfers between devices, fast(): lax.all_to_all(spread, CHIP_AXES, split_axis=0, concat_axis=0, tiled=True)  9.4 us
    ppermute x3, starting transfers between devices, fast(): lax.ppermute(box, 'y', [(i, (i - d) % 4) for i in range(4)])  4.66 us
    ppermute x3, starting transfers between devices, fast(): lax.ppermute(partial[2 * d:2 * d + 2], 'y', [(i, (i + d) % 4) for i in ra...  4.04 us
    unnamed x21, local copies, waits for them, and re-layouts  3.46 us
    ppermute x3, waiting for transfers between devices, fast(): lax.ppermute(partial[2 * d:2 * d + 2], 'y', [(i, (i + d) % 4) for i in ra...  2.6 us
  transfers between devices with their start and end apart: 16, of which 5 were waited for; matrix products, arithmetic and copies ran while one was open for 1% of the time, Pallas kernels for 12%

profile of v8, /device:TPU:1, one launch (start us, length us, event | category | flops | bytes accessed | tf_op | source)
XLA Modules:
  0.0 99.9 jit_solution(8973260793948887187)
XLA Ops:
  6.5 4.4 %shard_map.39 = (bf16[64,8,1536]{2,1,0:T(8,128)(2,1)}, bf16[80,1152]{1,0:T(8,128)(2,1)}, s32[1,512]{1,0:T(1,128)}, f32[8,128]{1,0:T(8,128)}) custom-call(s32[1]{0:T(128)} %bitcast.7.chip_ref, bf16[512,1024]{1,0:T(8,128)(2,1)} %emb_hbm.1, s32[1,512]{1,0:T(1,128)} %bitcast.71, s32[1,512]{1,0:T(1,128)} %bitcast.73), custom_call_target="tpu_custom_call" | custom-call | flops 1400000000 | bytes 3000000 | tf_op jit(solution)/shard_map/pallas_call | solution.py:342
  10.9 0.0 copy-start.4
  11.0 0.0 copy-start
  11.0 12.1 %all-to-all-start.4 = ((bf16[64,8,1536]{2,1,0:T(8,128)(2,1)}), bf16[64,8,1536]{2,1,0:T(8,128)(2,1)S(1)}, u32[]{:S(2)}, u32[]{:S(2)}) async-start(bf16[64,8,1536]{2,1,0:T(8,128)(2,1)} %get-tuple-element.96), calls=%async_computation.4 | async-start | bytes 3145728 | tf_op jit(solution)/shard_map/all_to_all | solution.py:381
  23.1 0.0 all-gather.7.cloned.1.call-start
  23.1 0.7 all-gather.7.cloned.1.call-update
  23.8 0.0 copy-done.4
  23.8 1.1 %collective-permute-start.2 = (bf16[80,1152]{1,0:T(8,128)(2,1)S(1)}, bf16[80,1152]{1,0:T(8,128)(2,1)S(1)}, u32[]{:S(2)}, u32[]{:S(2)}) collective-permute-start(bf16[80,1152]{1,0:T(8,128)(2,1)S(1)} %copy-done.4), channel_id=1, source_target_pairs={{0,2},{2,4},{4,6},{6,0},{1,3},{3,5},{5,7},{7,1},{8,10},{10,12},{12... | collective-permute-start | bytes 552968 | tf_op jit(solution)/shard_map/ppermute | solution.py:383
  24.9 2.4 %collective-permute-start.1 = (bf16[80,1152]{1,0:T(8,128)(2,1)S(1)}, bf16[80,1152]{1,0:T(8,128)(2,1)S(1)}, u32[]{:S(2)}, u32[]{:S(2)}) collective-permute-start(bf16[80,1152]{1,0:T(8,128)(2,1)S(1)} %copy-done.4), channel_id=1, source_target_pairs={{0,4},{2,6},{4,0},{6,2},{1,5},{3,7},{5,1},{7,3},{8,12},{10,14},{12... | collective-permute-start | bytes 552968 | tf_op jit(solution)/shard_map/ppermute | solution.py:383
  27.3 1.2 %collective-permute-start = (bf16[80,1152]{1,0:T(8,128)(2,1)S(1)}, bf16[80,1152]{1,0:T(8,128)(2,1)S(1)}, u32[]{:S(2)}, u32[]{:S(2)}) collective-permute-start(bf16[80,1152]{1,0:T(8,128)(2,1)S(1)} %copy-done.4), channel_id=1, source_target_pairs={{0,6},{2,0},{4,2},{6,4},{1,7},{3,1},{5,3},{7,5},{8,14},{10,8},{12,... | collective-permute-start | bytes 552968 | tf_op jit(solution)/shard_map/ppermute | solution.py:383
  28.5 18.3 %collective-permute-done.2 = bf16[80,1152]{1,0:T(8,128)(2,1)S(1)} collective-permute-done((bf16[80,1152]{1,0:T(8,128)(2,1)S(1)}, bf16[80,1152]{1,0:T(8,128)(2,1)S(1)}, u32[]{:S(2)}, u32[]{:S(2)}) %collective-permute-start.2) | collective-permute-done | bytes 184352 | tf_op jit(solution)/shard_map/ppermute | solution.py:383
  46.8 3.3 %collective-permute-done.1 = bf16[80,1152]{1,0:T(8,128)(2,1)S(1)} collective-permute-done((bf16[80,1152]{1,0:T(8,128)(2,1)S(1)}, bf16[80,1152]{1,0:T(8,128)(2,1)S(1)}, u32[]{:S(2)}, u32[]{:S(2)}) %collective-permute-start.1) | collective-permute-done | bytes 184352 | tf_op jit(solution)/shard_map/ppermute | solution.py:383
  50.1 0.0 collective-permute-done
  50.1 0.0 copy-start.5
  50.1 0.0 all-to-all-done.4.in_ref.own_ref
  50.1 1.8 %collective-permute-start.3 = (bf16[64,8,1536]{2,1,0:T(8,128)(2,1)S(1)}, bf16[64,8,1536]{2,1,0:T(8,128)(2,1)S(1)}, u32[]{:S(2)}, u32[]{:S(2)}) collective-permute-start(bf16[64,8,1536]{2,1,0:T(8,128)(2,1)S(1)} %all-to-all-done.4.in_ref.own_ref), channel_id=1, source_target_pairs={{0,1},{1,0},{2,3},{3,2},{4,5},{5,4},{6,7},{7,6},{8,9},{9,8},{10,11... | collective-permute-start | bytes 4718600 | tf_op jit(solution)/shard_map/ppermute | solution.py:385
  51.9 0.0 copy-done
  51.9 1.6 %shard_map.40 = (bf16[96,1152]{1,0:T(8,128)(2,1)S(1)}, bf16[16,1152]{1,0:T(8,128)(2,1)S(1)}, bf16[512,128]{1,0:T(8,128)(2,1)S(1)}) custom-call(s32[1]{0:T(128)} %bitcast.10.y_ref, f32[8,128]{1,0:T(8,128)S(1)} %copy-done, bf16[64,8,1536]{2,1,0:T(8,128)(2,1)S(1)} %all-to-all-done.4.in_ref.own_ref), custom_call_target="tpu_custom_call" | custom-call | flops 200000000 | bytes 2000000 | tf_op jit(solution)/shard_map/pallas_call | solution.py:342
  53.5 0.3 collective-permute-start.6
  53.9 1.2 %collective-permute-start.5 = (bf16[32,1152]{1,0:T(8,128)(2,1)S(1)}, bf16[32,1152]{1,0:T(8,128)(2,1)S(1)}, u32[]{:S(2)}, u32[]{:S(2)}) collective-permute-start(bf16[32,1152]{1,0:T(8,128)(2,1)S(1)} %get-tuple-element.175), channel_id=1, source_target_pairs={{0,4},{2,6},{4,0},{6,2},{1,5},{3,7},{5,1},{7,3},{8,12},{10,14},{12... | collective-permute-start | bytes 221192 | tf_op jit(solution)/shard_map/ppermute | solution.py:403
  55.0 0.2 collective-permute-start.4
  55.3 0.0 collective-permute-done.3.other_ref
  55.3 4.2 %shard_map.41 = (bf16[1536,1024]{1,0:T(8,128)(2,1)S(1)}, bf16[1536,128]{1,0:T(8,128)(2,1)S(1)}, f32[8,768]{1,0:T(8,128)S(1)}) custom-call(bf16[64,8,1536]{2,1,0:T(8,128)(2,1)S(1)} %all-to-all-done.4.in_ref.own_ref, bf16[512,128]{1,0:T(8,128)(2,1)S(1)} %get-tuple-element.99.own_meta_ref, bf16[64,8,1536]{2,1,0:T(8,128)(2,1)S(1)} %collective-permute-done.3.other_ref), custom_call_target="tpu_custom_call" | custom-call | flops 2800000000 | bytes 7000000 | tf_op jit(solution)/shard_map/pallas_call | solution.py:342
  59.5 0.0 collective-permute-done.6
  59.5 0.0 collective-permute-done.5
  59.5 1.4 %collective-permute-done.4 = bf16[32,1152]{1,0:T(8,128)(2,1)S(1)} collective-permute-done((bf16[32,1152]{1,0:T(8,128)(2,1)S(1)}, bf16[32,1152]{1,0:T(8,128)(2,1)S(1)}, u32[]{:S(2)}, u32[]{:S(2)}) %collective-permute-start.4) | collective-permute-done | bytes 73760 | tf_op jit(solution)/shard_map/ppermute | solution.py:403
  60.9 1.0 %collective-permute-start.7 = (bf16[112,1152]{1,0:T(8,128)(2,1)S(1)}, bf16[112,1152]{1,0:T(8,128)(2,1)S(1)}, u32[]{:S(2)}, u32[]{:S(2)}) collective-permute-start(bf16[112,1152]{1,0:T(8,128)(2,1)S(1)} %constant_dynamic-update-slice_fusion.own_tail_ref), channel_id=1, source_target_pairs={{0,1},{1,0},{2,3},{3,2},{4,5},{5,4},{6,7},{7,6},{8,9},{9,8},{10,11... | collective-permute-start | bytes 774152 | tf_op jit(solution)/shard_map/ppermute | solution.py:407
  61.9 1.2 %collective-permute-done.7.other_tail_ref = bf16[112,1152]{1,0:T(8,128)(2,1)S(1)} collective-permute-done((bf16[112,1152]{1,0:T(8,128)(2,1)S(1)}, bf16[112,1152]{1,0:T(8,128)(2,1)S(1)}, u32[]{:S(2)}, u32[]{:S(2)}) %collective-permute-start.7) | collective-permute-done | bytes 258080 | tf_op jit(solution)/shard_map/ppermute | solution.py:407
  63.1 3.4 %shard_map.42 = f32[64,4,128]{2,1,0:T(4,128)} custom-call(bf16[1536,1024]{1,0:T(8,128)(2,1)S(1)} %get-tuple-element.100.keys_ref, bf16[1536,128]{1,0:T(8,128)(2,1)S(1)} %get-tuple-element.101.metas_ref, f32[8,768]{1,0:T(8,128)S(1)} %get-tuple-element.104.best_ref, bf16[112,1152]{1,0:T(8,128)(2,1)S(1)} %constant_dynamic-update-slice_fusion.own_tail_ref, ...), custom_call_target="tpu_custom_call" | custom-call | flops 1000000000 | bytes 4000000 | tf_op jit(solution)/shard_map/pallas_call | solution.py:342
  66.5 0.0 copy-done.5
  66.5 0.1 pad_maximum_fusion
  66.5 0.4 collective-permute-start.8
  67.0 9.4 %all-to-all-start.5 = ((f32[64,4,128]{2,1,0:T(4,128)}), f32[64,4,128]{2,1,0:T(4,128)S(1)}, u32[]{:S(2)}, u32[]{:S(2)}) async-start(f32[64,4,128]{2,1,0:T(4,128)} %shard_map.42), calls=%async_computation.5 | async-start | bytes 262144 | tf_op jit(solution)/shard_map/all_to_all | solution.py:419
  76.4 0.9 constant_dynamic-update-slice_fusion.7
  77.4 0.0 collective-permute-done.8
  77.4 0.1 constant_dynamic-update-slice_fusion.4.queries_ref
  77.5 0.0 copy-start.1
  77.5 0.0 all-gather.7.cloned.1.call-done.keys_ref
  77.6 0.0 copy-start.2
  77.6 1.8 %copy-done.2 = bf16[1280,1152]{1,0:T(8,128)(2,1)S(1)} copy-done((bf16[1280,1152]{1,0:T(8,128)(2,1)S(1)}, bf16[1280,1152]{1,0:T(8,128)(2,1)}, u32[]{:S(2)}) %copy-start.2) | copy-done | bytes 2949144
  79.4 0.0 copy-start.6
  79.4 2.6 %shard_map.43 = f32[8,128]{1,0:T(8,128)S(1)} custom-call(bf16[1280,1152]{1,0:T(8,128)(2,1)S(1)} %copy-done.2, bf16[640,1152]{1,0:T(8,128)(2,1)S(1)} %constant_dynamic-update-slice_fusion.4.queries_ref), custom_call_target="tpu_custom_call" | custom-call | flops 1800000000 | bytes 4500000 | tf_op jit(solution)/shard_map/pallas_call | solution.py:342
  82.0 1.1 %collective-permute-start.9 = (f32[2,128]{1,0:T(2,128)S(1)}, f32[2,128]{1,0:T(2,128)S(1)}, u32[]{:S(2)}, u32[]{:S(2)}) collective-permute-start(f32[2,128]{1,0:T(2,128)S(1)} %get-tuple-element.179), channel_id=1, source_target_pairs={{0,2},{2,4},{4,6},{6,0},{1,3},{3,5},{5,7},{7,1},{8,10},{10,12},{12... | collective-permute-start | bytes 3080 | tf_op jit(solution)/shard_map/ppermute | solution.py:430
  83.1 1.7 %collective-permute-start.11 = (f32[2,128]{1,0:T(2,128)S(1)}, f32[2,128]{1,0:T(2,128)S(1)}, u32[]{:S(2)}, u32[]{:S(2)}) collective-permute-start(f32[2,128]{1,0:T(2,128)S(1)} %get-tuple-element.180), channel_id=1, source_target_pairs={{0,6},{2,0},{4,2},{6,4},{1,7},{3,1},{5,3},{7,5},{8,14},{10,8},{12,... | collective-permute-start | bytes 3080 | tf_op jit(solution)/shard_map/ppermute | solution.py:430
  84.8 1.3 %collective-permute-start.10 = (f32[2,128]{1,0:T(2,128)S(1)}, f32[2,128]{1,0:T(2,128)S(1)}, u32[]{:S(2)}, u32[]{:S(2)}) collective-permute-start(f32[2,128]{1,0:T(2,128)S(1)} %get-tuple-element.181), channel_id=1, source_target_pairs={{0,4},{2,6},{4,0},{6,2},{1,5},{3,7},{5,1},{7,3},{8,12},{10,14},{12... | collective-permute-start | bytes 3080 | tf_op jit(solution)/shard_map/ppermute | solution.py:430
  86.1 0.0 collective-permute-done.9
  86.1 0.0 collective-permute-done.11
  86.1 2.6 %collective-permute-done.10 = f32[2,128]{1,0:T(2,128)S(1)} collective-permute-done((f32[2,128]{1,0:T(2,128)S(1)}, f32[2,128]{1,0:T(2,128)S(1)}, u32[]{:S(2)}, u32[]{:S(2)}) %collective-permute-start.10) | collective-permute-done | bytes 1056 | tf_op jit(solution)/shard_map/ppermute | solution.py:430
  88.7 0.0 all-to-all-done.5.spread_ref
  88.7 2.2 %collective-permute-start.12 = (f32[4,128]{1,0:T(4,128)S(1)}, f32[4,128]{1,0:T(4,128)S(1)}, u32[]{:S(2)}, u32[]{:S(2)}) collective-permute-start(f32[4,128]{1,0:T(4,128)S(1)} %pad_maximum_fusion.1), channel_id=1, source_target_pairs={{0,1},{1,0},{2,3},{3,2},{4,5},{5,4},{6,7},{7,6},{8,9},{9,8},{10,11... | collective-permute-start | bytes 6152 | tf_op jit(solution)/shard_map/ppermute | solution.py:433
  91.0 0.7 shard_map.44
  92.3 0.0 collective-permute-done.12
  92.3 0.0 copy-done.1
  92.3 0.1 shard_map.45
  92.4 0.0 copy-done.6
  92.5 0.0 copy-start.7
  92.5 0.6 copy-done.7
  (16 shorter events, 0.2 us)
Async XLA Ops:
  10.9 12.9 %copy-start.4 = (bf16[80,1152]{1,0:T(8,128)(2,1)S(1)}, bf16[80,1152]{1,0:T(8,128)(2,1)}, u32[]{:S(2)}) copy-start(bf16[80,1152]{1,0:T(8,128)(2,1)} %get-tuple-element.113) | copy-start | bytes 552964
  11.0 41.0 %copy-start = (f32[8,128]{1,0:T(8,128)S(1)}, f32[8,128]{1,0:T(8,128)}, u32[]{:S(2)}) copy-start(f32[8,128]{1,0:T(8,128)} %get-tuple-element.98.flag_in_ref) | copy-start | bytes 12292
  11.0 39.2 %all-to-all-start.4 = ((bf16[64,8,1536]{2,1,0:T(8,128)(2,1)}), bf16[64,8,1536]{2,1,0:T(8,128)(2,1)S(1)}, u32[]{:S(2)}, u32[]{:S(2)}) async-start(bf16[64,8,1536]{2,1,0:T(8,128)(2,1)} %get-tuple-element.96), calls=%async_computation.4 | async-start | bytes 3145728 | tf_op jit(solution)/shard_map/all_to_all | solution.py:381
  23.1 54.5 %all-gather.7.cloned.1.call-start = ((), (), s32[]{:S(2)}) async-start(), calls=%async_computation.7 | async-start | bytes 3133440 | tf_op jit(solution)/shard_map/all_gather | solution.py:380
  23.8 23.0 %collective-permute-start.2 = (bf16[80,1152]{1,0:T(8,128)(2,1)S(1)}, bf16[80,1152]{1,0:T(8,128)(2,1)S(1)}, u32[]{:S(2)}, u32[]{:S(2)}) collective-permute-start(bf16[80,1152]{1,0:T(8,128)(2,1)S(1)} %copy-done.4), channel_id=1, source_target_pairs={{0,2},{2,4},{4,6},{6,0},{1,3},{3,5},{5,7},{7,1},{8,10},{10,12},{12... | collective-permute-start | bytes 552968 | tf_op jit(solution)/shard_map/ppermute | solution.py:383
  24.9 25.2 %collective-permute-start.1 = (bf16[80,1152]{1,0:T(8,128)(2,1)S(1)}, bf16[80,1152]{1,0:T(8,128)(2,1)S(1)}, u32[]{:S(2)}, u32[]{:S(2)}) collective-permute-start(bf16[80,1152]{1,0:T(8,128)(2,1)S(1)} %copy-done.4), channel_id=1, source_target_pairs={{0,4},{2,6},{4,0},{6,2},{1,5},{3,7},{5,1},{7,3},{8,12},{10,14},{12... | collective-permute-start | bytes 552968 | tf_op jit(solution)/shard_map/ppermute | solution.py:383
  27.3 22.8 %collective-permute-start = (bf16[80,1152]{1,0:T(8,128)(2,1)S(1)}, bf16[80,1152]{1,0:T(8,128)(2,1)S(1)}, u32[]{:S(2)}, u32[]{:S(2)}) collective-permute-start(bf16[80,1152]{1,0:T(8,128)(2,1)S(1)} %copy-done.4), channel_id=1, source_target_pairs={{0,6},{2,0},{4,2},{6,4},{1,7},{3,1},{5,3},{7,5},{8,14},{10,8},{12,... | collective-permute-start | bytes 552968 | tf_op jit(solution)/shard_map/ppermute | solution.py:383
  50.1 16.4 %copy-start.5 = (bf16[80,1152]{1,0:T(8,128)(2,1)}, bf16[80,1152]{1,0:T(8,128)(2,1)S(1)}, u32[]{:S(2)}) copy-start(bf16[80,1152]{1,0:T(8,128)(2,1)S(1)} %collective-permute-done) | copy-start | bytes 552964
  50.1 5.1 %collective-permute-start.3 = (bf16[64,8,1536]{2,1,0:T(8,128)(2,1)S(1)}, bf16[64,8,1536]{2,1,0:T(8,128)(2,1)S(1)}, u32[]{:S(2)}, u32[]{:S(2)}) collective-permute-start(bf16[64,8,1536]{2,1,0:T(8,128)(2,1)S(1)} %all-to-all-done.4.in_ref.own_ref), channel_id=1, source_target_pairs={{0,1},{1,0},{2,3},{3,2},{4,5},{5,4},{6,7},{7,6},{8,9},{9,8},{10,11... | collective-permute-start | bytes 4718600 | tf_op jit(solution)/shard_map/ppermute | solution.py:385
  53.5 6.0 %collective-permute-start.6 = (bf16[32,1152]{1,0:T(8,128)(2,1)S(1)}, bf16[32,1152]{1,0:T(8,128)(2,1)S(1)}, u32[]{:S(2)}, u32[]{:S(2)}) collective-permute-start(bf16[32,1152]{1,0:T(8,128)(2,1)S(1)} %get-tuple-element.174), channel_id=1, source_target_pairs={{0,6},{2,0},{4,2},{6,4},{1,7},{3,1},{5,3},{7,5},{8,14},{10,8},{12,... | collective-permute-start | bytes 221192 | tf_op jit(solution)/shard_map/ppermute | solution.py:403
  53.9 5.6 %collective-permute-start.5 = (bf16[32,1152]{1,0:T(8,128)(2,1)S(1)}, bf16[32,1152]{1,0:T(8,128)(2,1)S(1)}, u32[]{:S(2)}, u32[]{:S(2)}) collective-permute-start(bf16[32,1152]{1,0:T(8,128)(2,1)S(1)} %get-tuple-element.175), channel_id=1, source_target_pairs={{0,4},{2,6},{4,0},{6,2},{1,5},{3,7},{5,1},{7,3},{8,12},{10,14},{12... | collective-permute-start | bytes 221192 | tf_op jit(solution)/shard_map/ppermute | solution.py:403
  55.0 5.8 %collective-permute-start.4 = (bf16[32,1152]{1,0:T(8,128)(2,1)S(1)}, bf16[32,1152]{1,0:T(8,128)(2,1)S(1)}, u32[]{:S(2)}, u32[]{:S(2)}) collective-permute-start(bf16[32,1152]{1,0:T(8,128)(2,1)S(1)} %get-tuple-element.176), channel_id=1, source_target_pairs={{0,2},{2,4},{4,6},{6,0},{1,3},{3,5},{5,7},{7,1},{8,10},{10,12},{12... | collective-permute-start | bytes 221192 | tf_op jit(solution)/shard_map/ppermute | solution.py:403
  60.9 2.2 %collective-permute-start.7 = (bf16[112,1152]{1,0:T(8,128)(2,1)S(1)}, bf16[112,1152]{1,0:T(8,128)(2,1)S(1)}, u32[]{:S(2)}, u32[]{:S(2)}) collective-permute-start(bf16[112,1152]{1,0:T(8,128)(2,1)S(1)} %constant_dynamic-update-slice_fusion.own_tail_ref), channel_id=1, source_target_pairs={{0,1},{1,0},{2,3},{3,2},{4,5},{5,4},{6,7},{7,6},{8,9},{9,8},{10,11... | collective-permute-start | bytes 774152 | tf_op jit(solution)/shard_map/ppermute | solution.py:407
  66.5 10.9 %collective-permute-start.8 = (bf16[320,1152]{1,0:T(8,128)(2,1)S(1)}, bf16[320,1152]{1,0:T(8,128)(2,1)S(1)}, u32[]{:S(2)}, u32[]{:S(2)}) collective-permute-start(bf16[320,1152]{1,0:T(8,128)(2,1)S(1)} %pad_maximum_fusion), channel_id=1, source_target_pairs={{0,1},{1,0},{2,3},{3,2},{4,5},{5,4},{6,7},{7,6},{8,9},{9,8},{10,11... | collective-permute-start | bytes 2211848 | tf_op jit(solution)/shard_map/ppermute | solution.py:418
  67.0 21.7 %all-to-all-start.5 = ((f32[64,4,128]{2,1,0:T(4,128)}), f32[64,4,128]{2,1,0:T(4,128)S(1)}, u32[]{:S(2)}, u32[]{:S(2)}) async-start(f32[64,4,128]{2,1,0:T(4,128)} %shard_map.42), calls=%async_computation.5 | async-start | bytes 262144 | tf_op jit(solution)/shard_map/all_to_all | solution.py:419
  77.5 14.8 %copy-start.1 = (s32[1,512]{1,0:T(1,128)S(1)}, s32[1,512]{1,0:T(1,128)}, u32[]{:S(2)}) copy-start(s32[1,512]{1,0:T(1,128)} %get-tuple-element.122.rank_ref) | copy-start | bytes 6148
  77.6 1.8 %copy-start.2 = (bf16[1280,1152]{1,0:T(8,128)(2,1)S(1)}, bf16[1280,1152]{1,0:T(8,128)(2,1)}, u32[]{:S(2)}) copy-start(bf16[1280,1152]{1,0:T(8,128)(2,1)} %all-gather.7.cloned.1.call-done.keys_ref) | copy-start | bytes 8847364
  79.4 13.0 %copy-start.6 = (s32[512]{0:T(512)S(1)}, s32[512]{0:T(512)}, u32[]{:S(2)}) copy-start(s32[512]{0:T(512)} %param.8) | copy-start | bytes 6148
  82.0 4.0 %collective-permute-start.9 = (f32[2,128]{1,0:T(2,128)S(1)}, f32[2,128]{1,0:T(2,128)S(1)}, u32[]{:S(2)}, u32[]{:S(2)}) collective-permute-start(f32[2,128]{1,0:T(2,128)S(1)} %get-tuple-element.179), channel_id=1, source_target_pairs={{0,2},{2,4},{4,6},{6,0},{1,3},{3,5},{5,7},{7,1},{8,10},{10,12},{12... | collective-permute-start | bytes 3080 | tf_op jit(solution)/shard_map/ppermute | solution.py:430
  83.1 3.0 %collective-permute-start.11 = (f32[2,128]{1,0:T(2,128)S(1)}, f32[2,128]{1,0:T(2,128)S(1)}, u32[]{:S(2)}, u32[]{:S(2)}) collective-permute-start(f32[2,128]{1,0:T(2,128)S(1)} %get-tuple-element.180), channel_id=1, source_target_pairs={{0,6},{2,0},{4,2},{6,4},{1,7},{3,1},{5,3},{7,5},{8,14},{10,8},{12,... | collective-permute-start | bytes 3080 | tf_op jit(solution)/shard_map/ppermute | solution.py:430
  84.8 3.9 %collective-permute-start.10 = (f32[2,128]{1,0:T(2,128)S(1)}, f32[2,128]{1,0:T(2,128)S(1)}, u32[]{:S(2)}, u32[]{:S(2)}) collective-permute-start(f32[2,128]{1,0:T(2,128)S(1)} %get-tuple-element.181), channel_id=1, source_target_pairs={{0,4},{2,6},{4,0},{6,2},{1,5},{3,7},{5,1},{7,3},{8,12},{10,14},{12... | collective-permute-start | bytes 3080 | tf_op jit(solution)/shard_map/ppermute | solution.py:430
  88.7 3.5 %collective-permute-start.12 = (f32[4,128]{1,0:T(4,128)S(1)}, f32[4,128]{1,0:T(4,128)S(1)}, u32[]{:S(2)}, u32[]{:S(2)}) collective-permute-start(f32[4,128]{1,0:T(4,128)S(1)} %pad_maximum_fusion.1), channel_id=1, source_target_pairs={{0,1},{1,0},{2,3},{3,2},{4,5},{5,4},{6,7},{7,6},{8,9},{9,8},{10,11... | collective-permute-start | bytes 6152 | tf_op jit(solution)/shard_map/ppermute | solution.py:433
  92.5 0.6 copy-start.7
Sparse Core Ops, SparseCore 0:
  26.1 50.7 all-gather.6

commit v9 on v8

--- a/solution.py
+++ b/solution.py
@@ -426,7 +426,7 @@
         bytes_accessed=4_500_000,
     )
     parts = [partial[:2]]
-    for d in (1, 2, 3):
+    for d in (2, 1, 3):
         parts.append(lax.ppermute(partial[2 * d : 2 * d + 2], "y", [(i, (i + d) % 4) for i in range(4)]))
     to_other = jnp.concatenate([part[1:] for part in parts], axis=0)
     to_other, returned = lax.optimization_barrier((to_other, returned))

time: 100 us -> 101 us (1.010)
  transfers between devices with their start and end apart: 16 -> 16, of which waited for: 5 -> 7; matrix products, arithmetic and copies ran while one was open for 1% -> 1% of each run, Pallas kernels for 12% -> 12%
where the time goes in v9:
time: 101 us
  starting transfers between devices  37.8 us (37%)
  waiting for transfers between devices  27.9 us (28%)
  Pallas kernels  17 us (17%)
  between operations  14.2 us (14%)
  local copies, waits for them, and re-layouts  3.63 us (4%)
    ppermute x3, waiting for transfers between devices, fast(): lax.ppermute(box, 'y', [(i, (i - d) % 4) for i in range(4)])  21.6 us
    pallas_call x7, Pallas kernels, call(): pl.pallas_call(kernel, out_shape=shapes, in_specs=[pl.BlockSpec(memory_sp...  17 us
    all_to_all x1, starting transfers between devices, fast(): lax.all_to_all(outbox, CHIP_AXES, split_axis=0, concat_axis=0, tiled=True)  12.1 us
    all_to_all x1, starting transfers between devices, fast(): lax.all_to_all(spread, CHIP_AXES, split_axis=0, concat_axis=0, tiled=True)  9.4 us
    ppermute x3, starting transfers between devices, fast(): lax.ppermute(box, 'y', [(i, (i - d) % 4) for i in range(4)])  4.66 us
    ppermute x3, starting transfers between devices, fast(): lax.ppermute(partial[2 * d:2 * d + 2], 'y', [(i, (i + d) % 4) for i in ra...  4.05 us
    unnamed x21, local copies, waits for them, and re-layouts  3.46 us
    ppermute x3, waiting for transfers between devices, fast(): lax.ppermute(partial[2 * d:2 * d + 2], 'y', [(i, (i + d) % 4) for i in ra...  3.04 us
  transfers between devices with their start and end apart: 16, of which 7 were waited for; matrix products, arithmetic and copies ran while one was open for 1% of the time, Pallas kernels for 12%

profile of v9, /device:TPU:1, one launch (start us, length us, event | category | flops | bytes accessed | tf_op | source)
XLA Modules:
  0.0 100.6 jit_solution(2920340593222718870)
XLA Ops:
  6.5 4.4 %shard_map.39 = (bf16[64,8,1536]{2,1,0:T(8,128)(2,1)}, bf16[80,1152]{1,0:T(8,128)(2,1)}, s32[1,512]{1,0:T(1,128)}, f32[8,128]{1,0:T(8,128)}) custom-call(s32[1]{0:T(128)} %bitcast.7.chip_ref, bf16[512,1024]{1,0:T(8,128)(2,1)} %emb_hbm.1, s32[1,512]{1,0:T(1,128)} %bitcast.71, s32[1,512]{1,0:T(1,128)} %bitcast.73), custom_call_target="tpu_custom_call" | custom-call | flops 1400000000 | bytes 3000000 | tf_op jit(solution)/shard_map/pallas_call | solution.py:342
  10.9 0.0 copy-start.4
  11.0 0.0 copy-start
  11.0 12.1 %all-to-all-start.4 = ((bf16[64,8,1536]{2,1,0:T(8,128)(2,1)}), bf16[64,8,1536]{2,1,0:T(8,128)(2,1)S(1)}, u32[]{:S(2)}, u32[]{:S(2)}) async-start(bf16[64,8,1536]{2,1,0:T(8,128)(2,1)} %get-tuple-element.96), calls=%async_computation.4 | async-start | bytes 3145728 | tf_op jit(solution)/shard_map/all_to_all | solution.py:381
  23.1 0.0 all-gather.7.cloned.1.call-start
  23.1 0.7 all-gather.7.cloned.1.call-update
  23.8 0.0 copy-done.4
  23.8 1.1 %collective-permute-start.2 = (bf16[80,1152]{1,0:T(8,128)(2,1)S(1)}, bf16[80,1152]{1,0:T(8,128)(2,1)S(1)}, u32[]{:S(2)}, u32[]{:S(2)}) collective-permute-start(bf16[80,1152]{1,0:T(8,128)(2,1)S(1)} %copy-done.4), channel_id=1, source_target_pairs={{0,2},{2,4},{4,6},{6,0},{1,3},{3,5},{5,7},{7,1},{8,10},{10,12},{12... | collective-permute-start | bytes 552968 | tf_op jit(solution)/shard_map/ppermute | solution.py:383
  24.9 2.4 %collective-permute-start.1 = (bf16[80,1152]{1,0:T(8,128)(2,1)S(1)}, bf16[80,1152]{1,0:T(8,128)(2,1)S(1)}, u32[]{:S(2)}, u32[]{:S(2)}) collective-permute-start(bf16[80,1152]{1,0:T(8,128)(2,1)S(1)} %copy-done.4), channel_id=1, source_target_pairs={{0,4},{2,6},{4,0},{6,2},{1,5},{3,7},{5,1},{7,3},{8,12},{10,14},{12... | collective-permute-start | bytes 552968 | tf_op jit(solution)/shard_map/ppermute | solution.py:383
  27.3 1.2 %collective-permute-start = (bf16[80,1152]{1,0:T(8,128)(2,1)S(1)}, bf16[80,1152]{1,0:T(8,128)(2,1)S(1)}, u32[]{:S(2)}, u32[]{:S(2)}) collective-permute-start(bf16[80,1152]{1,0:T(8,128)(2,1)S(1)} %copy-done.4), channel_id=1, source_target_pairs={{0,6},{2,0},{4,2},{6,4},{1,7},{3,1},{5,3},{7,5},{8,14},{10,8},{12,... | collective-permute-start | bytes 552968 | tf_op jit(solution)/shard_map/ppermute | solution.py:383
  28.5 18.3 %collective-permute-done.2 = bf16[80,1152]{1,0:T(8,128)(2,1)S(1)} collective-permute-done((bf16[80,1152]{1,0:T(8,128)(2,1)S(1)}, bf16[80,1152]{1,0:T(8,128)(2,1)S(1)}, u32[]{:S(2)}, u32[]{:S(2)}) %collective-permute-start.2) | collective-permute-done | bytes 184352 | tf_op jit(solution)/shard_map/ppermute | solution.py:383
  46.8 3.3 %collective-permute-done.1 = bf16[80,1152]{1,0:T(8,128)(2,1)S(1)} collective-permute-done((bf16[80,1152]{1,0:T(8,128)(2,1)S(1)}, bf16[80,1152]{1,0:T(8,128)(2,1)S(1)}, u32[]{:S(2)}, u32[]{:S(2)}) %collective-permute-start.1) | collective-permute-done | bytes 184352 | tf_op jit(solution)/shard_map/ppermute | solution.py:383
  50.1 0.0 collective-permute-done
  50.1 0.0 copy-start.5
  50.1 0.0 all-to-all-done.4.in_ref.own_ref
  50.1 1.8 %collective-permute-start.3 = (bf16[64,8,1536]{2,1,0:T(8,128)(2,1)S(1)}, bf16[64,8,1536]{2,1,0:T(8,128)(2,1)S(1)}, u32[]{:S(2)}, u32[]{:S(2)}) collective-permute-start(bf16[64,8,1536]{2,1,0:T(8,128)(2,1)S(1)} %all-to-all-done.4.in_ref.own_ref), channel_id=1, source_target_pairs={{0,1},{1,0},{2,3},{3,2},{4,5},{5,4},{6,7},{7,6},{8,9},{9,8},{10,11... | collective-permute-start | bytes 4718600 | tf_op jit(solution)/shard_map/ppermute | solution.py:385
  51.9 0.0 copy-done
  51.9 1.6 %shard_map.40 = (bf16[96,1152]{1,0:T(8,128)(2,1)S(1)}, bf16[16,1152]{1,0:T(8,128)(2,1)S(1)}, bf16[512,128]{1,0:T(8,128)(2,1)S(1)}) custom-call(s32[1]{0:T(128)} %bitcast.10.y_ref, f32[8,128]{1,0:T(8,128)S(1)} %copy-done, bf16[64,8,1536]{2,1,0:T(8,128)(2,1)S(1)} %all-to-all-done.4.in_ref.own_ref), custom_call_target="tpu_custom_call" | custom-call | flops 200000000 | bytes 2000000 | tf_op jit(solution)/shard_map/pallas_call | solution.py:342
  53.5 0.3 collective-permute-start.6
  53.9 1.2 %collective-permute-start.5 = (bf16[32,1152]{1,0:T(8,128)(2,1)S(1)}, bf16[32,1152]{1,0:T(8,128)(2,1)S(1)}, u32[]{:S(2)}, u32[]{:S(2)}) collective-permute-start(bf16[32,1152]{1,0:T(8,128)(2,1)S(1)} %get-tuple-element.175), channel_id=1, source_target_pairs={{0,4},{2,6},{4,0},{6,2},{1,5},{3,7},{5,1},{7,3},{8,12},{10,14},{12... | collective-permute-start | bytes 221192 | tf_op jit(solution)/shard_map/ppermute | solution.py:403
  55.0 0.2 collective-permute-start.4
  55.3 0.0 collective-permute-done.3.other_ref
  55.3 4.2 %shard_map.41 = (bf16[1536,1024]{1,0:T(8,128)(2,1)S(1)}, bf16[1536,128]{1,0:T(8,128)(2,1)S(1)}, f32[8,768]{1,0:T(8,128)S(1)}) custom-call(bf16[64,8,1536]{2,1,0:T(8,128)(2,1)S(1)} %all-to-all-done.4.in_ref.own_ref, bf16[512,128]{1,0:T(8,128)(2,1)S(1)} %get-tuple-element.99.own_meta_ref, bf16[64,8,1536]{2,1,0:T(8,128)(2,1)S(1)} %collective-permute-done.3.other_ref), custom_call_target="tpu_custom_call" | custom-call | flops 2800000000 | bytes 7000000 | tf_op jit(solution)/shard_map/pallas_call | solution.py:342
  59.5 0.0 collective-permute-done.6
  59.5 0.0 collective-permute-done.5
  59.5 1.4 %collective-permute-done.4 = bf16[32,1152]{1,0:T(8,128)(2,1)S(1)} collective-permute-done((bf16[32,1152]{1,0:T(8,128)(2,1)S(1)}, bf16[32,1152]{1,0:T(8,128)(2,1)S(1)}, u32[]{:S(2)}, u32[]{:S(2)}) %collective-permute-start.4) | collective-permute-done | bytes 73760 | tf_op jit(solution)/shard_map/ppermute | solution.py:403
  60.9 1.0 %collective-permute-start.7 = (bf16[112,1152]{1,0:T(8,128)(2,1)S(1)}, bf16[112,1152]{1,0:T(8,128)(2,1)S(1)}, u32[]{:S(2)}, u32[]{:S(2)}) collective-permute-start(bf16[112,1152]{1,0:T(8,128)(2,1)S(1)} %constant_dynamic-update-slice_fusion.own_tail_ref), channel_id=1, source_target_pairs={{0,1},{1,0},{2,3},{3,2},{4,5},{5,4},{6,7},{7,6},{8,9},{9,8},{10,11... | collective-permute-start | bytes 774152 | tf_op jit(solution)/shard_map/ppermute | solution.py:407
  61.9 1.2 %collective-permute-done.7.other_tail_ref = bf16[112,1152]{1,0:T(8,128)(2,1)S(1)} collective-permute-done((bf16[112,1152]{1,0:T(8,128)(2,1)S(1)}, bf16[112,1152]{1,0:T(8,128)(2,1)S(1)}, u32[]{:S(2)}, u32[]{:S(2)}) %collective-permute-start.7) | collective-permute-done | bytes 258080 | tf_op jit(solution)/shard_map/ppermute | solution.py:407
  63.1 3.4 %shard_map.42 = f32[64,4,128]{2,1,0:T(4,128)} custom-call(bf16[1536,1024]{1,0:T(8,128)(2,1)S(1)} %get-tuple-element.100.keys_ref, bf16[1536,128]{1,0:T(8,128)(2,1)S(1)} %get-tuple-element.101.metas_ref, f32[8,768]{1,0:T(8,128)S(1)} %get-tuple-element.104.best_ref, bf16[112,1152]{1,0:T(8,128)(2,1)S(1)} %constant_dynamic-update-slice_fusion.own_tail_ref, ...), custom_call_target="tpu_custom_call" | custom-call | flops 1000000000 | bytes 4000000 | tf_op jit(solution)/shard_map/pallas_call | solution.py:342
  66.5 0.0 copy-done.5
  66.5 0.1 pad_maximum_fusion
  66.5 0.4 collective-permute-start.8
  67.0 9.4 %all-to-all-start.5 = ((f32[64,4,128]{2,1,0:T(4,128)}), f32[64,4,128]{2,1,0:T(4,128)S(1)}, u32[]{:S(2)}, u32[]{:S(2)}) async-start(f32[64,4,128]{2,1,0:T(4,128)} %shard_map.42), calls=%async_computation.5 | async-start | bytes 262144 | tf_op jit(solution)/shard_map/all_to_all | solution.py:419
  76.4 0.9 constant_dynamic-update-slice_fusion.7
  77.4 0.0 collective-permute-done.8
  77.4 0.1 constant_dynamic-update-slice_fusion.4.queries_ref
  77.5 0.0 copy-start.1
  77.5 0.0 all-gather.7.cloned.1.call-done.keys_ref
  77.6 0.0 copy-start.2
  77.6 1.8 %copy-done.2 = bf16[1280,1152]{1,0:T(8,128)(2,1)S(1)} copy-done((bf16[1280,1152]{1,0:T(8,128)(2,1)S(1)}, bf16[1280,1152]{1,0:T(8,128)(2,1)}, u32[]{:S(2)}) %copy-start.2) | copy-done | bytes 2949144
  79.4 0.0 copy-start.6
  79.4 2.6 %shard_map.43 = f32[8,128]{1,0:T(8,128)S(1)} custom-call(bf16[1280,1152]{1,0:T(8,128)(2,1)S(1)} %copy-done.2, bf16[640,1152]{1,0:T(8,128)(2,1)S(1)} %constant_dynamic-update-slice_fusion.4.queries_ref), custom_call_target="tpu_custom_call" | custom-call | flops 1800000000 | bytes 4500000 | tf_op jit(solution)/shard_map/pallas_call | solution.py:342
  82.0 2.6 %collective-permute-start.9 = (f32[2,128]{1,0:T(2,128)S(1)}, f32[2,128]{1,0:T(2,128)S(1)}, u32[]{:S(2)}, u32[]{:S(2)}) collective-permute-start(f32[2,128]{1,0:T(2,128)S(1)} %get-tuple-element.179), channel_id=1, source_target_pairs={{0,4},{2,6},{4,0},{6,2},{1,5},{3,7},{5,1},{7,3},{8,12},{10,14},{12... | collective-permute-start | bytes 3080 | tf_op jit(solution)/shard_map/ppermute | solution.py:430
  84.6 0.9 collective-permute-start.11
  85.5 0.6 collective-permute-start.10
  86.1 0.1 collective-permute-done.9
  86.2 1.0 collective-permute-done.11
  87.2 1.9 %collective-permute-done.10 = f32[2,128]{1,0:T(2,128)S(1)} collective-permute-done((f32[2,128]{1,0:T(2,128)S(1)}, f32[2,128]{1,0:T(2,128)S(1)}, u32[]{:S(2)}, u32[]{:S(2)}) %collective-permute-start.10) | collective-permute-done | bytes 1056 | tf_op jit(solution)/shard_map/ppermute | solution.py:430
  89.2 0.0 all-to-all-done.5.spread_ref
  89.2 2.5 %collective-permute-start.12 = (f32[4,128]{1,0:T(4,128)S(1)}, f32[4,128]{1,0:T(4,128)S(1)}, u32[]{:S(2)}, u32[]{:S(2)}) collective-permute-start(f32[4,128]{1,0:T(4,128)S(1)} %pad_maximum_fusion.1), channel_id=1, source_target_pairs={{0,1},{1,0},{2,3},{3,2},{4,5},{5,4},{6,7},{7,6},{8,9},{9,8},{10,11... | collective-permute-start | bytes 6152 | tf_op jit(solution)/shard_map/ppermute | solution.py:433
  91.7 0.7 shard_map.44
  93.0 0.0 collective-permute-done.12
  93.0 0.0 copy-done.1
  93.0 0.1 shard_map.45
  93.2 0.0 copy-done.6
  93.2 0.0 copy-start.7
  93.2 0.6 copy-done.7
  (16 shorter events, 0.2 us)
Async XLA Ops:
  10.9 12.9 %copy-start.4 = (bf16[80,1152]{1,0:T(8,128)(2,1)S(1)}, bf16[80,1152]{1,0:T(8,128)(2,1)}, u32[]{:S(2)}) copy-start(bf16[80,1152]{1,0:T(8,128)(2,1)} %get-tuple-element.113) | copy-start | bytes 552964
  11.0 41.0 %copy-start = (f32[8,128]{1,0:T(8,128)S(1)}, f32[8,128]{1,0:T(8,128)}, u32[]{:S(2)}) copy-start(f32[8,128]{1,0:T(8,128)} %get-tuple-element.98.flag_in_ref) | copy-start | bytes 12292
  11.0 39.2 %all-to-all-start.4 = ((bf16[64,8,1536]{2,1,0:T(8,128)(2,1)}), bf16[64,8,1536]{2,1,0:T(8,128)(2,1)S(1)}, u32[]{:S(2)}, u32[]{:S(2)}) async-start(bf16[64,8,1536]{2,1,0:T(8,128)(2,1)} %get-tuple-element.96), calls=%async_computation.4 | async-start | bytes 3145728 | tf_op jit(solution)/shard_map/all_to_all | solution.py:381
  23.1 54.5 %all-gather.7.cloned.1.call-start = ((), (), s32[]{:S(2)}) async-start(), calls=%async_computation.7 | async-start | bytes 3133440 | tf_op jit(solution)/shard_map/all_gather | solution.py:380
  23.8 23.0 %collective-permute-start.2 = (bf16[80,1152]{1,0:T(8,128)(2,1)S(1)}, bf16[80,1152]{1,0:T(8,128)(2,1)S(1)}, u32[]{:S(2)}, u32[]{:S(2)}) collective-permute-start(bf16[80,1152]{1,0:T(8,128)(2,1)S(1)} %copy-done.4), channel_id=1, source_target_pairs={{0,2},{2,4},{4,6},{6,0},{1,3},{3,5},{5,7},{7,1},{8,10},{10,12},{12... | collective-permute-start | bytes 552968 | tf_op jit(solution)/shard_map/ppermute | solution.py:383
  24.9 25.2 %collective-permute-start.1 = (bf16[80,1152]{1,0:T(8,128)(2,1)S(1)}, bf16[80,1152]{1,0:T(8,128)(2,1)S(1)}, u32[]{:S(2)}, u32[]{:S(2)}) collective-permute-start(bf16[80,1152]{1,0:T(8,128)(2,1)S(1)} %copy-done.4), channel_id=1, source_target_pairs={{0,4},{2,6},{4,0},{6,2},{1,5},{3,7},{5,1},{7,3},{8,12},{10,14},{12... | collective-permute-start | bytes 552968 | tf_op jit(solution)/shard_map/ppermute | solution.py:383
  27.3 22.8 %collective-permute-start = (bf16[80,1152]{1,0:T(8,128)(2,1)S(1)}, bf16[80,1152]{1,0:T(8,128)(2,1)S(1)}, u32[]{:S(2)}, u32[]{:S(2)}) collective-permute-start(bf16[80,1152]{1,0:T(8,128)(2,1)S(1)} %copy-done.4), channel_id=1, source_target_pairs={{0,6},{2,0},{4,2},{6,4},{1,7},{3,1},{5,3},{7,5},{8,14},{10,8},{12,... | collective-permute-start | bytes 552968 | tf_op jit(solution)/shard_map/ppermute | solution.py:383
  50.1 16.4 %copy-start.5 = (bf16[80,1152]{1,0:T(8,128)(2,1)}, bf16[80,1152]{1,0:T(8,128)(2,1)S(1)}, u32[]{:S(2)}) copy-start(bf16[80,1152]{1,0:T(8,128)(2,1)S(1)} %collective-permute-done) | copy-start | bytes 552964
  50.1 5.1 %collective-permute-start.3 = (bf16[64,8,1536]{2,1,0:T(8,128)(2,1)S(1)}, bf16[64,8,1536]{2,1,0:T(8,128)(2,1)S(1)}, u32[]{:S(2)}, u32[]{:S(2)}) collective-permute-start(bf16[64,8,1536]{2,1,0:T(8,128)(2,1)S(1)} %all-to-all-done.4.in_ref.own_ref), channel_id=1, source_target_pairs={{0,1},{1,0},{2,3},{3,2},{4,5},{5,4},{6,7},{7,6},{8,9},{9,8},{10,11... | collective-permute-start | bytes 4718600 | tf_op jit(solution)/shard_map/ppermute | solution.py:385
  53.5 6.0 %collective-permute-start.6 = (bf16[32,1152]{1,0:T(8,128)(2,1)S(1)}, bf16[32,1152]{1,0:T(8,128)(2,1)S(1)}, u32[]{:S(2)}, u32[]{:S(2)}) collective-permute-start(bf16[32,1152]{1,0:T(8,128)(2,1)S(1)} %get-tuple-element.174), channel_id=1, source_target_pairs={{0,6},{2,0},{4,2},{6,4},{1,7},{3,1},{5,3},{7,5},{8,14},{10,8},{12,... | collective-permute-start | bytes 221192 | tf_op jit(solution)/shard_map/ppermute | solution.py:403
  53.9 5.6 %collective-permute-start.5 = (bf16[32,1152]{1,0:T(8,128)(2,1)S(1)}, bf16[32,1152]{1,0:T(8,128)(2,1)S(1)}, u32[]{:S(2)}, u32[]{:S(2)}) collective-permute-start(bf16[32,1152]{1,0:T(8,128)(2,1)S(1)} %get-tuple-element.175), channel_id=1, source_target_pairs={{0,4},{2,6},{4,0},{6,2},{1,5},{3,7},{5,1},{7,3},{8,12},{10,14},{12... | collective-permute-start | bytes 221192 | tf_op jit(solution)/shard_map/ppermute | solution.py:403
  55.0 5.8 %collective-permute-start.4 = (bf16[32,1152]{1,0:T(8,128)(2,1)S(1)}, bf16[32,1152]{1,0:T(8,128)(2,1)S(1)}, u32[]{:S(2)}, u32[]{:S(2)}) collective-permute-start(bf16[32,1152]{1,0:T(8,128)(2,1)S(1)} %get-tuple-element.176), channel_id=1, source_target_pairs={{0,2},{2,4},{4,6},{6,0},{1,3},{3,5},{5,7},{7,1},{8,10},{10,12},{12... | collective-permute-start | bytes 221192 | tf_op jit(solution)/shard_map/ppermute | solution.py:403
  60.9 2.2 %collective-permute-start.7 = (bf16[112,1152]{1,0:T(8,128)(2,1)S(1)}, bf16[112,1152]{1,0:T(8,128)(2,1)S(1)}, u32[]{:S(2)}, u32[]{:S(2)}) collective-permute-start(bf16[112,1152]{1,0:T(8,128)(2,1)S(1)} %constant_dynamic-update-slice_fusion.own_tail_ref), channel_id=1, source_target_pairs={{0,1},{1,0},{2,3},{3,2},{4,5},{5,4},{6,7},{7,6},{8,9},{9,8},{10,11... | collective-permute-start | bytes 774152 | tf_op jit(solution)/shard_map/ppermute | solution.py:407
  66.5 10.9 %collective-permute-start.8 = (bf16[320,1152]{1,0:T(8,128)(2,1)S(1)}, bf16[320,1152]{1,0:T(8,128)(2,1)S(1)}, u32[]{:S(2)}, u32[]{:S(2)}) collective-permute-start(bf16[320,1152]{1,0:T(8,128)(2,1)S(1)} %pad_maximum_fusion), channel_id=1, source_target_pairs={{0,1},{1,0},{2,3},{3,2},{4,5},{5,4},{6,7},{7,6},{8,9},{9,8},{10,11... | collective-permute-start | bytes 2211848 | tf_op jit(solution)/shard_map/ppermute | solution.py:418
  67.0 22.2 %all-to-all-start.5 = ((f32[64,4,128]{2,1,0:T(4,128)}), f32[64,4,128]{2,1,0:T(4,128)S(1)}, u32[]{:S(2)}, u32[]{:S(2)}) async-start(f32[64,4,128]{2,1,0:T(4,128)} %shard_map.42), calls=%async_computation.5 | async-start | bytes 262144 | tf_op jit(solution)/shard_map/all_to_all | solution.py:419
  77.5 15.5 %copy-start.1 = (s32[1,512]{1,0:T(1,128)S(1)}, s32[1,512]{1,0:T(1,128)}, u32[]{:S(2)}) copy-start(s32[1,512]{1,0:T(1,128)} %get-tuple-element.122.rank_ref) | copy-start | bytes 6148
  77.6 1.8 %copy-start.2 = (bf16[1280,1152]{1,0:T(8,128)(2,1)S(1)}, bf16[1280,1152]{1,0:T(8,128)(2,1)}, u32[]{:S(2)}) copy-start(bf16[1280,1152]{1,0:T(8,128)(2,1)} %all-gather.7.cloned.1.call-done.keys_ref) | copy-start | bytes 8847364
  79.4 13.8 %copy-start.6 = (s32[512]{0:T(512)S(1)}, s32[512]{0:T(512)}, u32[]{:S(2)}) copy-start(s32[512]{0:T(512)} %param.8) | copy-start | bytes 6148
  82.0 4.2 %collective-permute-start.9 = (f32[2,128]{1,0:T(2,128)S(1)}, f32[2,128]{1,0:T(2,128)S(1)}, u32[]{:S(2)}, u32[]{:S(2)}) collective-permute-start(f32[2,128]{1,0:T(2,128)S(1)} %get-tuple-element.179), channel_id=1, source_target_pairs={{0,4},{2,6},{4,0},{6,2},{1,5},{3,7},{5,1},{7,3},{8,12},{10,14},{12... | collective-permute-start | bytes 3080 | tf_op jit(solution)/shard_map/ppermute | solution.py:430
  84.6 2.6 %collective-permute-start.11 = (f32[2,128]{1,0:T(2,128)S(1)}, f32[2,128]{1,0:T(2,128)S(1)}, u32[]{:S(2)}, u32[]{:S(2)}) collective-permute-start(f32[2,128]{1,0:T(2,128)S(1)} %get-tuple-element.180), channel_id=1, source_target_pairs={{0,6},{2,0},{4,2},{6,4},{1,7},{3,1},{5,3},{7,5},{8,14},{10,8},{12,... | collective-permute-start | bytes 3080 | tf_op jit(solution)/shard_map/ppermute | solution.py:430
  85.5 3.6 %collective-permute-start.10 = (f32[2,128]{1,0:T(2,128)S(1)}, f32[2,128]{1,0:T(2,128)S(1)}, u32[]{:S(2)}, u32[]{:S(2)}) collective-permute-start(f32[2,128]{1,0:T(2,128)S(1)} %get-tuple-element.181), channel_id=1, source_target_pairs={{0,2},{2,4},{4,6},{6,0},{1,3},{3,5},{5,7},{7,1},{8,10},{10,12},{12... | collective-permute-start | bytes 3080 | tf_op jit(solution)/shard_map/ppermute | solution.py:430
  89.2 3.8 %collective-permute-start.12 = (f32[4,128]{1,0:T(4,128)S(1)}, f32[4,128]{1,0:T(4,128)S(1)}, u32[]{:S(2)}, u32[]{:S(2)}) collective-permute-start(f32[4,128]{1,0:T(4,128)S(1)} %pad_maximum_fusion.1), channel_id=1, source_target_pairs={{0,1},{1,0},{2,3},{3,2},{4,5},{5,4},{6,7},{7,6},{8,9},{9,8},{10,11... | collective-permute-start | bytes 6152 | tf_op jit(solution)/shard_map/ppermute | solution.py:433
  93.2 0.6 copy-start.7
Sparse Core Ops, SparseCore 0:
  26.1 50.7 all-gather.6
